TPU v7x, 512 devices: a whole 4x8x8 slice. The times are simulated.
512 devices in a mesh: dp: 32 (over y, x), feat: 16 (over z, core).
Axes of the slice: x: 4, y: 8, z: 8, core: 2. Of those that a mesh axis runs over, the one named last changes fastest.
Arguments:
- data: bfloat16 [98304, 4096], P('dp', 'feat'), may hold values from -6 to 6
- block_counts: int32 [32], replicated, may hold values from 1 to 6, 64 in all
- basis: bfloat16 [4096, 256], P('feat'), may hold values from -0.09375 to 0.09375
Outputs:
- basis_scaled: float32 [4096, 256], P('feat')
- upper: float32 [256, 256], replicated
Inputs may be any that keep to these rules, and one draw needn't show every extreme that they name: `block_counts`: every index of dp has one or more valid blocks, the counts sum to 2 * 32, and the largest is exactly 6.
All inputs are finite; a program needn't handle non-finite values.
Results may differ from a plain program's by a relative error of at most 0.00065.
Values may be sent and summed in bfloat16 or wider, within the bound.
No kernel may reach another device: no remote copies, remote signals or barrier semaphores. Data moves between devices by JAX's collectives and lax.ppermute only.
A program may use at most 64 MiB of HBM per device.

v0:
```python
import math

import jax
import jax.numpy as jnp
from jax import lax
from jax.sharding import PartitionSpec as P

D = 4096
BLOCK = 512


def orthonormal(matrix):
    local_gram = jnp.dot(matrix.T, matrix, precision=lax.Precision.HIGHEST)
    gram_total = lax.psum(local_gram, "feat")
    lower = jnp.linalg.cholesky(gram_total)
    solved = jax.scipy.linalg.solve_triangular(lower, matrix.T, lower=True)
    return (solved.T, lower.T)


def on_device(data, block_counts, basis):
    rows_local, columns = data.shape
    stored = rows_local // BLOCK
    rank_width = basis.shape[1]
    my_index = lax.axis_index("dp")
    blocks = data.reshape(stored, BLOCK, columns)
    active = lax.dynamic_index_in_dim(block_counts, my_index, 0, False)

    def row_block(step, partial_value):
        piece = lax.dynamic_index_in_dim(blocks, step, 0, False)
        product = jnp.dot(piece, basis, preferred_element_type=jnp.float32)
        return lax.dynamic_update_index_in_dim(partial_value, product, step, 0)

    partial_value = lax.fori_loop(
        0, active, row_block, jnp.zeros((stored, BLOCK, rank_width), jnp.float32)
    )
    row_images = lax.psum(partial_value, "feat").astype(jnp.bfloat16)

    def feature_block(step, running):
        piece = lax.dynamic_index_in_dim(blocks, step, 0, False)
        image = lax.dynamic_index_in_dim(row_images, step, 0, False)
        return running + lax.dot_general(
            piece, image, (((0,), (0,)), ((), ())), preferred_element_type=jnp.float32
        )

    local_terms = lax.fori_loop(
        0, active, feature_block, jnp.zeros((columns, rank_width), jnp.float32)
    )
    summed_terms = lax.psum(local_terms, "dp")
    row_total = (jnp.sum(block_counts) * BLOCK).astype(jnp.float32)
    updated = basis.astype(jnp.float32) + summed_terms / row_total
    first_basis, upper_one = orthonormal(updated)
    second_basis, upper_two = orthonormal(first_basis)
    upper = jnp.dot(upper_two, upper_one, precision=lax.Precision.HIGHEST)
    return (second_basis * math.sqrt(D), upper)


def solution(mesh):
    in_specs = (P("dp", "feat"), P(), P("feat", None))
    out_specs = (P("feat", None), P())
    return jax.shard_map(
        on_device, mesh=mesh, in_specs=in_specs, out_specs=out_specs, check_vma=False
    )
```

profile of v0, /device:TPU:1, one launch (start us, length us, event | category | flops | bytes accessed | tf_op | source)
XLA Modules:
  0.0 618.8 jit_solution(8986923673449969841)
XLA Ops:
  7.2 0.0 all-reduce.6.cloned.1.call-start
  7.2 1.3 dynamic_slice.14
  8.5 0.0 copy-start.1
  8.5 0.3 broadcast_in_dim.12
  8.8 0.6 copy-done.1
  9.4 2.4 while.24
  10.0 1.2 fusion.70
  11.8 67.0 %all-reduce.11 = bf16[6,512,256]{2,1,0:T(8,128)(2,1)} all-reduce(f32[6,512,256]{2,1,0:T(8,128)S(1)} %get-tuple-element.60), channel_id=1, replica_groups=mesh['dp'=32,'feat'=16] {'feat'}, use_global_device_ids=true, to_apply=%region_2.3 | all-reduce | flops 786432 | bytes 4718592 | tf_op jit(solution)/shard_map/psum | solution.py:36
  78.9 0.0 copy-start.2
  78.9 2.6 while.25
  79.5 1.3 convolution_add_fusion.2
  81.4 0.0 copy-start
  81.5 0.7 copy-done
  82.1 0.0 all-reduce.6.cloned.1.call-update
  82.2 0.0 all-reduce.8.cloned.1.call-start
  82.2 0.0 copy-done.2
  82.2 0.7 reduce_sum.9
  83.6 165.1 %all-reduce.6.cloned.1.call-done = f32[256,256]{1,0:T(8,128)} async-done(((f32[256,256]{1,0:T(8,128)}), f32[256,256]{1,0:T(8,128)}) %all-reduce.6.cloned.1.call-update) | async-done | bytes 262160 | tf_op jit(solution)/shard_map/psum | solution.py:48
  248.6 2.3 fusion.45
  251.0 0.0 all-reduce.8.cloned.1.call-update
  251.0 0.0 all-reduce.10.cloned.1.call-start
  251.1 1.0 fusion.44
  252.0 115.9 %all-reduce.8.cloned.1.call-done = f32[256,256]{0,1:T(8,128)} async-done(((f32[256,256]{0,1:T(8,128)}), f32[256,256]{0,1:T(8,128)}) %all-reduce.8.cloned.1.call-update) | async-done | bytes 262160 | tf_op jit(solution)/shard_map/psum | solution.py:14
  368.0 1.1 copy.6
  369.1 1.0 fusion.15
  370.1 11.7 %cholesky.130 = f32[128,128]{1,0:T(8,128)S(1)} custom-call(f32[128,128]{1,0:T(8,128)S(1)} %cholesky.194), custom_call_target="Cholesky" | custom-call | tf_op jit(solution)/shard_map/jit(cholesky)/cholesky | solution.py:15
  381.8 9.8 %custom-call.13 = f32[1,128,128]{1,2,0:T(8,128)S(1)} custom-call(f32[1,128,128]{2,1,0:T(8,128)S(1)} %get-tuple-element.127), custom_call_target="InvertDiagBlocksLowerTriangular" | custom-call | tf_op jit(solution)/shard_map/jit(cholesky)/cholesky | solution.py:15
  391.7 0.2 constant_dynamic-update-slice_fusion.3
  391.9 0.3 convolution_subtract_fusion.3
  392.1 11.7 %cholesky.147 = f32[128,128]{1,0:T(8,128)S(1)} custom-call(f32[128,128]{1,0:T(8,128)S(1)} %convolution_subtract_fusion.3), custom_call_target="Cholesky" | custom-call | tf_op jit(solution)/shard_map/jit(cholesky)/cholesky | solution.py:15
  403.9 0.7 compare_reduce_fusion.2
  406.0 0.1 triangular_solve.75
  406.1 4.3 while.26
  406.3 0.6 fusion.73
  406.9 1.4 bitcast_dynamic-update-slice_fusion.4
  408.3 0.6 fusion.73
  408.9 1.4 bitcast_dynamic-update-slice_fusion.4
  410.4 19.7 %custom-call.14 = f32[2,128,128]{1,2,0:T(8,128)S(1)} custom-call(f32[2,128,128]{2,1,0:T(8,128)S(1)} %get-tuple-element.76), custom_call_target="InvertDiagBlocksLowerTriangular" | custom-call | tf_op jit(solution)/shard_map/jit(_solve_triangular)/triangular_solve | solution.py:16
  430.1 0.3 fusion.23
  430.4 0.4 convolution_subtract_fusion.1
  430.8 0.3 fusion.35
  431.1 1.1 fusion.9
  432.2 0.0 all-reduce.10.cloned.1.call-update
  432.2 114.5 %all-reduce.10.cloned.1.call-done = f32[256,256]{0,1:T(8,128)} async-done(((f32[256,256]{0,1:T(8,128)}), f32[256,256]{0,1:T(8,128)}) %all-reduce.10.cloned.1.call-update) | async-done | bytes 262160 | tf_op jit(solution)/shard_map/psum | solution.py:14
  546.7 1.1 copy.8
  547.8 1.0 fusion.14
  548.8 11.7 %cholesky.164 = f32[128,128]{1,0:T(8,128)S(1)} custom-call(f32[128,128]{1,0:T(8,128)S(1)} %cholesky.197), custom_call_target="Cholesky" | custom-call | tf_op jit(solution)/shard_map/jit(cholesky)/cholesky | solution.py:15
  560.6 9.8 %custom-call.15 = f32[1,128,128]{1,2,0:T(8,128)S(1)} custom-call(f32[1,128,128]{2,1,0:T(8,128)S(1)} %get-tuple-element.123), custom_call_target="InvertDiagBlocksLowerTriangular" | custom-call | tf_op jit(solution)/shard_map/jit(cholesky)/cholesky | solution.py:15
  570.4 0.2 constant_dynamic-update-slice_fusion.1
  570.6 0.3 convolution_subtract_fusion.2
  570.9 11.7 %cholesky.181 = f32[128,128]{1,0:T(8,128)S(1)} custom-call(f32[128,128]{1,0:T(8,128)S(1)} %convolution_subtract_fusion.2), custom_call_target="Cholesky" | custom-call | tf_op jit(solution)/shard_map/jit(cholesky)/cholesky | solution.py:15
  582.6 0.7 compare_reduce_fusion
  583.3 0.6 compare_reduce_fusion.1
  585.3 1.2 fusion.20
  586.6 4.1 while.27
  586.6 0.7 fusion.74
  587.2 1.3 bitcast_dynamic-update-slice_fusion.5
  588.6 0.7 fusion.74
  589.3 1.3 bitcast_dynamic-update-slice_fusion.5
  590.6 19.9 %custom-call.16 = f32[2,128,128]{1,2,0:T(8,128)S(1)} custom-call(f32[2,128,128]{2,1,0:T(8,128)S(1)} %get-tuple-element.77), custom_call_target="InvertDiagBlocksLowerTriangular" | custom-call | tf_op jit(solution)/shard_map/jit(_solve_triangular)/triangular_solve | solution.py:16
  610.5 0.3 fusion.31
  610.9 0.3 convolution_subtract_fusion
  611.1 0.3 fusion.30
  611.5 0.8 copy.9
  (19 shorter events, 0.3 us)
Async XLA Ops:
  7.2 241.5 %all-reduce.6.cloned.1.call-start = ((), (), s32[]{:S(2)}) async-start(), calls=%async_computation | async-start | bytes 524288 | tf_op jit(solution)/shard_map/psum | solution.py:48
  8.5 0.9 copy-start.1
  78.9 3.4 copy-start.2
  81.4 0.7 copy-start
  82.2 285.8 %all-reduce.8.cloned.1.call-start = ((), (), s32[]{:S(2)}) async-start(), calls=%async_computation.1 | async-start | bytes 524288 | tf_op jit(solution)/shard_map/psum | solution.py:14
  251.0 295.7 %all-reduce.10.cloned.1.call-start = ((), (), s32[]{:S(2)}) async-start(), calls=%async_computation.2 | async-start | bytes 524288 | tf_op jit(solution)/shard_map/psum | solution.py:14
Sparse Core Ops, SparseCore 0:
  82.3 166.3 all-reduce.5
  251.5 116.3 all-reduce.7
  432.4 114.2 all-reduce.9
where the time goes:
time: 617 us; the launch traced here: 619 us
  waiting for transfers between devices  396 us (64%)
  other arithmetic  112 us (18%)
  blocking collectives  67 us (11%)
  between operations  17.3 us (3%)
  local copies, waits for them, and re-layouts  14.1 us (2%)
  matrix products  9.97 us (2%)
    psum x2, waiting for transfers between devices, orthonormal(): gram_total = lax.psum(local_gram, 'feat')  230 us
    psum x1, waiting for transfers between devices, on_device(): summed_terms = lax.psum(local_terms, 'dp')  165 us
    another operation x13, other arithmetic, orthonormal(): lower = jnp.linalg.cholesky(gram_total)  68.7 us
    psum x1, blocking collectives, on_device(): row_images = lax.psum(partial_value, 'feat').astype(jnp.bfloat16)  67 us
    another operation x5, other arithmetic, orthonormal(): solved = jax.scipy.linalg.solve_triangular(lower, matrix.T, lower=True)  39.6 us
  transfers between devices with their start and end apart: 3, of which 3 were waited for; matrix products, arithmetic and copies ran while one was open for 0% of the time, Pallas kernels for 0%

commit v1 on v0

v1 whole, which is shorter than its diff:
```python
import math

import jax
import jax.numpy as jnp
from jax import lax
from jax.sharding import PartitionSpec as P

D = 4096
BLOCK = 512
CORES = 2
X = 4
F32 = jnp.float32
BF16 = jnp.bfloat16


def core_swap(value):
    count = lax.axis_size("feat")
    return lax.ppermute(value, "feat", [(i, i ^ 1) for i in range(count)])


def groups_z():
    count = lax.axis_size("feat")
    return [list(range(c, count, CORES)) for c in range(CORES)]


def groups_x():
    count = lax.axis_size("dp")
    return [list(range(y, y + X, 1)) for y in range(0, count, X)]


def spread(value, axis, groups, size):
    copies = jnp.broadcast_to(value[None], (size,) + value.shape)
    return lax.all_to_all(copies, axis, 0, 0, axis_index_groups=groups)


def sum_images(partial, feat):
    core = feat % CORES
    chips = lax.axis_size("feat") // CORES
    rows, rank = partial.shape
    split = partial.reshape(chips, CORES, rows // (chips * CORES), rank)
    mine = lax.dynamic_index_in_dim(split, core, 1, False)
    other = lax.dynamic_index_in_dim(split, 1 - core, 1, False)
    pair = mine + core_swap(other)
    pieces = lax.all_to_all(
        pair.astype(jnp.float16), "feat", 0, 0, axis_index_groups=groups_z()
    )
    return jnp.sum(pieces.astype(F32), axis=0)


def sum_gram(gram, dp, feat):
    core = feat % CORES
    chips = lax.axis_size("feat") // CORES
    rank = gram.shape[0]
    split = gram.reshape(X, CORES, rank // (X * CORES), rank)
    split = lax.dynamic_index_in_dim(split, dp % X, 0, False)
    mine = lax.dynamic_index_in_dim(split, core, 0, False)
    other = lax.dynamic_index_in_dim(split, 1 - core, 0, False)
    pair = mine + core_swap(other)
    total = jnp.sum(spread(pair, "feat", groups_z(), chips), axis=0)
    quarter = spread(total, "dp", groups_x(), X)
    theirs = core_swap(quarter)
    first = jnp.where(core == 0, quarter, theirs)
    second = jnp.where(core == 0, theirs, quarter)
    return jnp.stack([first, second], axis=1).reshape(rank, rank)


def orthonormal(matrix, dp, feat):
    local_gram = jnp.dot(matrix.T, matrix, precision=lax.Precision.HIGHEST)
    gram_total = sum_gram(local_gram, dp, feat)
    lower = jnp.linalg.cholesky(gram_total)
    solved = jax.scipy.linalg.solve_triangular(lower, matrix.T, lower=True)
    return (solved.T, lower.T)


def on_device(data, block_counts, basis):
    rows, columns = data.shape
    rank = basis.shape[1]
    dp = lax.axis_index("dp")
    feat = lax.axis_index("feat")
    dp_size = lax.axis_size("dp")
    active = lax.dynamic_index_in_dim(block_counts, dp, 0, False)

    partial = jnp.dot(data, basis, preferred_element_type=F32)
    images = sum_images(partial, feat)
    here = images.shape[0]
    row_ids = feat * here + lax.broadcasted_iota(jnp.int32, (here, 1), 0)
    images = jnp.where(row_ids < active * BLOCK, images, 0.0).astype(BF16)
    images = lax.all_gather(images, "feat", tiled=True)

    terms = lax.dot_general(
        data, images, (((0,), (0,)), ((), ())), preferred_element_type=F32
    )
    pieces = lax.all_to_all(terms.reshape(dp_size, columns // dp_size, rank), "dp", 0, 0)
    piece = jnp.sum(pieces, axis=0)
    summed_terms = spread(piece, "dp", None, dp_size).reshape(columns, rank)

    row_total = (jnp.sum(block_counts) * BLOCK).astype(F32)
    updated = basis.astype(F32) + summed_terms / row_total
    first_basis, upper_one = orthonormal(updated, dp, feat)
    second_basis, upper_two = orthonormal(first_basis, dp, feat)
    upper = jnp.dot(upper_two, upper_one, precision=lax.Precision.HIGHEST)
    return (second_basis * math.sqrt(D), upper)


def solution(mesh):
    in_specs = (P("dp", "feat"), P(), P("feat", None))
    out_specs = (P("feat", None), P())
    return jax.shard_map(
        on_device, mesh=mesh, in_specs=in_specs, out_specs=out_specs, check_vma=False
    )
```

time: 617 us -> 334 us (0.54)
  waiting for transfers between devices: 396 us -> 105 us
  starting transfers between devices: 0.12 us -> 50.5 us
  blocking collectives: 67 us -> 22 us
    psum x3 -> x0, waiting for transfers between devices: 395 us -> none  [the longest x2 230 us: orthonormal(): gram_total = lax.psum(local_gram, 'feat')]
    psum x1 -> x0, blocking collectives: 67 us -> none  [on_device(): row_images = lax.psum(partial_value, 'feat').astype(jnp.bfloat16)]
    all_to_all x0 -> x5, waiting for transfers between devices: none -> 59 us  [the longest x3 24.9 us: spread(): return lax.all_to_all(copies, axis, 0, 0, axis_index_groups=groups)]
    all_gather x0 -> x1, waiting for transfers between devices: none -> 39.1 us  [on_device(): images = lax.all_gather(images, 'feat', tiled=True)]
    all_to_all x0 -> x5, starting transfers between devices: none -> 25.7 us  [the longest x3 11.5 us: spread(): return lax.all_to_all(copies, axis, 0, 0, axis_index_groups=groups)]
    ppermute x0 -> x5, starting transfers between devices: none -> 24.8 us  [core_swap(): return lax.ppermute(value, 'feat', [(i, i ^ 1) for i in range(count)])]
    all_to_all x0 -> x2, blocking collectives: none -> 22 us  [spread(): return lax.all_to_all(copies, axis, 0, 0, axis_index_groups=groups)]
    ppermute x0 -> x5, waiting for transfers between devices: none -> 6.6 us  [core_swap(): return lax.ppermute(value, 'feat', [(i, i ^ 1) for i in range(count)])]
  transfers between devices with their start and end apart: 3 -> 11, of which waited for: 3 -> 11; matrix products, arithmetic and copies ran while one was open for 0% -> 0% of each run, Pallas kernels for 0% -> 0%
where the time goes in v1:
time: 334 us; the launch traced here: 333 us
  other arithmetic  112 us (34%)
  waiting for transfers between devices  105 us (31%)
  starting transfers between devices  50.5 us (15%)
  blocking collectives  22 us (7%)
  between operations  18.4 us (6%)
  local copies, waits for them, and re-layouts  15.6 us (5%)
  matrix products  9.04 us (3%)
    another operation x13, other arithmetic, orthonormal(): lower = jnp.linalg.cholesky(gram_total)  68.6 us
    another operation x5, other arithmetic, orthonormal(): solved = jax.scipy.linalg.solve_triangular(lower, matrix.T, lower=True)  39.4 us
    all_gather x1, waiting for transfers between devices, on_device(): images = lax.all_gather(images, 'feat', tiled=True)  39.1 us
    all_to_all x3, waiting for transfers between devices, spread(): return lax.all_to_all(copies, axis, 0, 0, axis_index_groups=groups)  24.9 us
    ppermute x5, starting transfers between devices, core_swap(): return lax.ppermute(value, 'feat', [(i, i ^ 1) for i in range(count)])  24.8 us
    all_to_all x1, waiting for transfers between devices, sum_images(): lax.all_to_all(pair.astype(jnp.float16), 'feat', 0, 0, axis_index_groups=...  22.3 us
    all_to_all x2, blocking collectives, spread(): return lax.all_to_all(copies, axis, 0, 0, axis_index_groups=groups)  22 us
    all_to_all x1, waiting for transfers between devices, on_device(): lax.all_to_all(terms.reshape(dp_size, columns // dp_size, rank), 'dp', 0, 0)  11.8 us
  transfers between devices with their start and end apart: 11, of which 11 were waited for; matrix products, arithmetic and copies ran while one was open for 0% of the time, Pallas kernels for 0%

profile of v1, /device:TPU:1, one launch (start us, length us, event | category | flops | bytes accessed | tf_op | source)
XLA Modules:
  0.0 333.2 jit_solution(15528174377840727508)
XLA Ops:
  7.2 1.4 copy-done
  8.6 1.5 fusion.43
  10.1 1.4 dynamic-slice_bitcast_fusion
  11.5 0.7 copy-done.1
  12.2 8.8 %collective-permute-start = (f32[8,192,256]{2,1,0:T(8,128)}, f32[8,192,256]{2,1,0:T(8,128)S(1)}, u32[]{:S(2)}, u32[]{:S(2)}) collective-permute-start(f32[8,192,256]{2,1,0:T(8,128)} %dynamic-slice_bitcast_fusion), channel_id=1, source_target_pairs={{0,1},{1,0},{2,3},{3,2},{4,5},{5,4},{6,7},{7,6},{8,9},{9,8},{10,11... | collective-permute-start | bytes 4718600 | tf_op jit(solution)/shard_map/ppermute | solution.py:18
  21.0 3.2 collective-permute-done
  24.2 2.5 fusion
  26.7 4.8 %all-to-all-start = ((f16[8,192,256]{2,1,0:T(8,128)(2,1)}), f16[8,192,256]{2,1,0:T(8,128)(2,1)S(1)}, u32[]{:S(2)}, u32[]{:S(2)}) async-start(f16[8,192,256]{2,1,0:T(8,128)(2,1)} %fusion), calls=%async_computation | async-start | bytes 1572864 | tf_op jit(solution)/shard_map/all_to_all | solution.py:44
  31.6 0.6 dynamic_slice.27
  32.8 22.3 %all-to-all-done = f16[8,192,256]{2,1,0:T(8,128)(2,1)S(1)} async-done(((f16[8,192,256]{2,1,0:T(8,128)(2,1)}), f16[8,192,256]{2,1,0:T(8,128)(2,1)S(1)}, u32[]{:S(2)}, u32[]{:S(2)}) %all-to-all-start) | async-done | bytes 786464 | tf_op jit(solution)/shard_map/all_to_all | solution.py:44
  55.2 0.7 select_convert_fusion
  56.0 39.1 %all-gather.2.cloned.1.call-done = bf16[3072,256]{1,0:T(8,128)(2,1)} async-done(((bf16[192,256]{1,0:T(8,128)(2,1)}), bf16[3072,256]{1,0:T(8,128)(2,1)}) %all-gather.2.cloned.1.call-update) | async-done | bytes 1572880 | tf_op jit(solution)/shard_map/all_gather | solution.py:88
  95.1 2.8 convolution_bitcast_fusion
  97.9 9.3 %all-to-all-start.1 = ((f32[32,8,256]{2,1,0:T(8,128)}), f32[32,8,256]{2,1,0:T(8,128)S(1)}, u32[]{:S(2)}, u32[]{:S(2)}) async-start(f32[32,8,256]{2,1,0:T(8,128)} %convolution_bitcast_fusion), calls=%async_computation.1 | async-start | bytes 524288 | tf_op jit(solution)/shard_map/all_to_all | solution.py:93
  107.3 11.8 %all-to-all-done.1 = f32[32,8,256]{2,1,0:T(8,128)S(1)} async-done(((f32[32,8,256]{2,1,0:T(8,128)}), f32[32,8,256]{2,1,0:T(8,128)S(1)}, u32[]{:S(2)}, u32[]{:S(2)}) %all-to-all-start.1) | async-done | bytes 262176 | tf_op jit(solution)/shard_map/all_to_all | solution.py:93
  119.2 0.7 broadcast_in_dim.25
  119.9 4.3 %all-to-all-start.2 = ((f32[32,8,256]{2,1,0:T(8,128)}), f32[32,8,256]{2,1,0:T(8,128)S(1)}, u32[]{:S(2)}, u32[]{:S(2)}) async-start(f32[32,8,256]{2,1,0:T(8,128)} %broadcast_in_dim.25), calls=%async_computation.2 | async-start | bytes 524288 | tf_op jit(solution)/shard_map/all_to_all | solution.py:33
  124.2 0.7 reduce_sum.47
  125.8 8.9 %all-to-all-done.2 = f32[32,8,256]{2,1,0:T(8,128)S(1)} async-done(((f32[32,8,256]{2,1,0:T(8,128)}), f32[32,8,256]{2,1,0:T(8,128)S(1)}, u32[]{:S(2)}, u32[]{:S(2)}) %all-to-all-start.2) | async-done | bytes 262176 | tf_op jit(solution)/shard_map/all_to_all | solution.py:33
  134.8 0.4 fusion.16
  135.3 5.4 %collective-permute-start.1 = (f32[32,256]{1,0:T(8,128)S(1)}, f32[32,256]{1,0:T(8,128)S(1)}, u32[]{:S(2)}, u32[]{:S(2)}) collective-permute-start(f32[32,256]{1,0:T(8,128)S(1)} %dynamic-slice_bitcast_fusion.2), channel_id=1, source_target_pairs={{0,1},{1,0},{2,3},{3,2},{4,5},{5,4},{6,7},{7,6},{8,9},{9,8},{10,11... | collective-permute-start | bytes 98312 | tf_op jit(solution)/shard_map/ppermute | solution.py:18
  140.7 0.8 collective-permute-done.1
  141.5 0.7 broadcast_in_dim.26
  142.2 3.9 %all-to-all-start.3 = ((f32[8,32,256]{2,1,0:T(8,128)}), f32[8,32,256]{2,1,0:T(8,128)S(1)}, u32[]{:S(2)}, u32[]{:S(2)}) async-start(f32[8,32,256]{2,1,0:T(8,128)} %broadcast_in_dim.26), calls=%async_computation.3 | async-start | bytes 524288 | tf_op jit(solution)/shard_map/all_to_all | solution.py:33
  146.1 11.2 %all-to-all-done.3 = f32[8,32,256]{2,1,0:T(8,128)S(1)} async-done(((f32[8,32,256]{2,1,0:T(8,128)}), f32[8,32,256]{2,1,0:T(8,128)S(1)}, u32[]{:S(2)}, u32[]{:S(2)}) %all-to-all-start.3) | async-done | bytes 262176 | tf_op jit(solution)/shard_map/all_to_all | solution.py:33
  157.3 0.7 broadcast_in_dim.27
  158.0 3.3 all-to-all-start.4
  161.3 4.8 %all-to-all-done.4 = f32[4,32,256]{2,1,0:T(8,128)S(1)} async-done(((f32[4,32,256]{2,1,0:T(8,128)}), f32[4,32,256]{2,1,0:T(8,128)S(1)}, u32[]{:S(2)}, u32[]{:S(2)}) %all-to-all-start.4) | async-done | bytes 131104 | tf_op jit(solution)/shard_map/all_to_all | solution.py:33
  166.1 4.9 %collective-permute-start.2 = (f32[4,32,256]{2,1,0:T(8,128)S(1)}, f32[4,32,256]{2,1,0:T(8,128)S(1)}, u32[]{:S(2)}, u32[]{:S(2)}) collective-permute-start(f32[4,32,256]{2,1,0:T(8,128)S(1)} %all-to-all-done.4), channel_id=1, source_target_pairs={{0,1},{1,0},{2,3},{3,2},{4,5},{5,4},{6,7},{7,6},{8,9},{9,8},{10,11... | collective-permute-start | bytes 393224 | tf_op jit(solution)/shard_map/ppermute | solution.py:18
  171.0 0.8 collective-permute-done.2
  172.0 11.7 %cholesky.130 = f32[128,128]{1,0:T(8,128)S(1)} custom-call(f32[128,128]{1,0:T(8,128)S(1)} %cholesky.194), custom_call_target="Cholesky" | custom-call | tf_op jit(solution)/shard_map/jit(cholesky)/cholesky | solution.py:70
  183.8 9.8 %custom-call.13 = f32[1,128,128]{1,2,0:T(8,128)S(1)} custom-call(f32[1,128,128]{2,1,0:T(8,128)S(1)} %get-tuple-element.59), custom_call_target="InvertDiagBlocksLowerTriangular" | custom-call | tf_op jit(solution)/shard_map/jit(cholesky)/cholesky | solution.py:70
  194.1 11.7 %cholesky.147 = f32[128,128]{1,0:T(8,128)S(1)} custom-call(f32[128,128]{1,0:T(8,128)S(1)} %convolution_subtract_fusion.3), custom_call_target="Cholesky" | custom-call | tf_op jit(solution)/shard_map/jit(cholesky)/cholesky | solution.py:70
  205.8 0.6 compare_reduce_fusion.2
  207.8 4.0 %while.4 = (s32[]{:T(128)}, f32[256,256]{1,0:T(8,128)S(1)}, s32[2,2]{1,0:T(2,128)S(1)}, f32[2,128,128]{2,1,0:T(8,128)S(1)}, s32[]{:T(128)}) while((s32[]{:T(128)}, f32[256,256]{1,0:T(8,128)S(1)}, s32[2,2]{1,0:T(2,128)S(1)}, f32[2,128,128]{2,1,0:T(8,128)S(1)}, s32[]{:T(128)}) %tuple.53), condition=%wide.while_cond, body=%wide.while_body.sunk | while | flops 2 | bytes 131181 | solution.py:71
  208.0 0.6 fusion.59
  208.6 1.3 bitcast_dynamic-update-slice_fusion.4
  210.0 0.6 fusion.59
  210.5 1.3 bitcast_dynamic-update-slice_fusion.4
  211.9 19.7 %custom-call.14 = f32[2,128,128]{1,2,0:T(8,128)S(1)} custom-call(f32[2,128,128]{2,1,0:T(8,128)S(1)} %get-tuple-element.18), custom_call_target="InvertDiagBlocksLowerTriangular" | custom-call | tf_op jit(solution)/shard_map/jit(_solve_triangular)/triangular_solve | solution.py:71
  231.5 0.3 fusion.17
  232.1 0.3 fusion.29
  232.4 0.4 fusion.1
  232.9 2.3 collective-permute-start.3
  235.2 0.8 collective-permute-done.3
  236.0 14.8 %all_to_all.36 = f32[8,32,256]{2,1,0:T(8,128)S(1)} all-to-all(f32[8,32,256]{2,1,0:T(8,128)S(1)} %broadcast_in_dim.28), channel_id=1, replica_groups={{0,2,4,6,8,10,12,14},{1,3,5,7,9,11,13,15},{16,18,20,22,24,26,28,30},{17..., dimensions={0} | all-to-all | bytes 524288 | tf_op jit(solution)/shard_map/all_to_all | solution.py:33
  250.8 7.2 %all_to_all.35 = f32[4,32,256]{2,1,0:T(8,128)S(1)} all-to-all(f32[4,32,256]{2,1,0:T(8,128)S(1)} %broadcast_in_dim.29), channel_id=1, replica_groups={{0,16,32,48},{64,80,96,112},{128,144,160,176},{192,208,224,240},{256,27..., dimensions={0} | all-to-all | bytes 262144 | tf_op jit(solution)/shard_map/all_to_all | solution.py:33
  258.1 3.5 %collective-permute-start.4 = (f32[4,32,256]{2,1,0:T(8,128)S(1)}, f32[4,32,256]{2,1,0:T(8,128)S(1)}, u32[]{:S(2)}, u32[]{:S(2)}) collective-permute-start(f32[4,32,256]{2,1,0:T(8,128)S(1)} %all_to_all.35), channel_id=1, source_target_pairs={{0,1},{1,0},{2,3},{3,2},{4,5},{5,4},{6,7},{7,6},{8,9},{9,8},{10,11... | collective-permute-start | bytes 393224 | tf_op jit(solution)/shard_map/ppermute | solution.py:18
  261.6 1.0 collective-permute-done.4
  262.8 11.7 %cholesky.164 = f32[128,128]{1,0:T(8,128)S(1)} custom-call(f32[128,128]{1,0:T(8,128)S(1)} %cholesky.197), custom_call_target="Cholesky" | custom-call | tf_op jit(solution)/shard_map/jit(cholesky)/cholesky | solution.py:70
  274.6 9.8 %custom-call.15 = f32[1,128,128]{1,2,0:T(8,128)S(1)} custom-call(f32[1,128,128]{2,1,0:T(8,128)S(1)} %get-tuple-element.55), custom_call_target="InvertDiagBlocksLowerTriangular" | custom-call | tf_op jit(solution)/shard_map/jit(cholesky)/cholesky | solution.py:70
  284.9 11.7 %cholesky.181 = f32[128,128]{1,0:T(8,128)S(1)} custom-call(f32[128,128]{1,0:T(8,128)S(1)} %convolution_subtract_fusion.2), custom_call_target="Cholesky" | custom-call | tf_op jit(solution)/shard_map/jit(cholesky)/cholesky | solution.py:70
  296.6 0.7 compare_reduce_fusion
  297.4 0.6 compare_reduce_fusion.1
  299.3 1.2 fusion.12
  300.6 4.3 %while.5 = (s32[]{:T(128)}, f32[256,256]{1,0:T(8,128)S(1)}, s32[2,2]{1,0:T(2,128)S(1)}, f32[2,128,128]{2,1,0:T(8,128)S(1)}, s32[]{:T(128)}) while((s32[]{:T(128)}, f32[256,256]{1,0:T(8,128)S(1)}, s32[2,2]{1,0:T(2,128)S(1)}, f32[2,128,128]{2,1,0:T(8,128)S(1)}, s32[]{:T(128)}) %tuple.61), condition=%wide.while_cond.clone, body=%wide.while_body.clone.sunk | while | flops 2 | bytes 131181 | solution.py:71
  300.9 0.7 fusion.60
  301.5 1.3 bitcast_dynamic-update-slice_fusion.5
  302.9 0.7 fusion.60
  303.6 1.3 bitcast_dynamic-update-slice_fusion.5
  304.9 19.7 %custom-call.16 = f32[2,128,128]{1,2,0:T(8,128)S(1)} custom-call(f32[2,128,128]{2,1,0:T(8,128)S(1)} %get-tuple-element.19), custom_call_target="InvertDiagBlocksLowerTriangular" | custom-call | tf_op jit(solution)/shard_map/jit(_solve_triangular)/triangular_solve | solution.py:71
  324.6 0.3 fusion.25
  325.2 0.3 fusion.24
  325.5 0.8 copy.27
  (57 shorter events, 2.9 us)
Async XLA Ops:
  7.2 1.4 copy-start
  10.1 2.1 copy-start.1
  12.2 12.0 %collective-permute-start = (f32[8,192,256]{2,1,0:T(8,128)}, f32[8,192,256]{2,1,0:T(8,128)S(1)}, u32[]{:S(2)}, u32[]{:S(2)}) collective-permute-start(f32[8,192,256]{2,1,0:T(8,128)} %dynamic-slice_bitcast_fusion), channel_id=1, source_target_pairs={{0,1},{1,0},{2,3},{3,2},{4,5},{5,4},{6,7},{7,6},{8,9},{9,8},{10,11... | collective-permute-start | bytes 4718600 | tf_op jit(solution)/shard_map/ppermute | solution.py:18
  26.7 4.8 %copy-start.3 = (s32[32]{0:T(128)S(1)}, s32[32]{0:T(128)}, u32[]{:S(2)}) copy-start(s32[32]{0:T(128)} %param.7) | copy-start | bytes 388
  26.7 28.4 %all-to-all-start = ((f16[8,192,256]{2,1,0:T(8,128)(2,1)}), f16[8,192,256]{2,1,0:T(8,128)(2,1)S(1)}, u32[]{:S(2)}, u32[]{:S(2)}) async-start(f16[8,192,256]{2,1,0:T(8,128)(2,1)} %fusion), calls=%async_computation | async-start | bytes 1572864 | tf_op jit(solution)/shard_map/all_to_all | solution.py:44
  31.5 63.6 %all-gather.2.cloned.1.call-start = ((), (), s32[]{:S(2)}) async-start(), calls=%async_computation.7 | async-start | bytes 1671168 | tf_op jit(solution)/shard_map/all_gather | solution.py:88
  97.9 27.0 %copy-start.2 = (bf16[256,256]{1,0:T(8,128)(2,1)S(1)}, bf16[256,256]{1,0:T(8,128)(2,1)}, u32[]{:S(2)}) copy-start(bf16[256,256]{1,0:T(8,128)(2,1)} %param.8) | copy-start | bytes 393220
  97.9 21.2 %all-to-all-start.1 = ((f32[32,8,256]{2,1,0:T(8,128)}), f32[32,8,256]{2,1,0:T(8,128)S(1)}, u32[]{:S(2)}, u32[]{:S(2)}) async-start(f32[32,8,256]{2,1,0:T(8,128)} %convolution_bitcast_fusion), calls=%async_computation.1 | async-start | bytes 524288 | tf_op jit(solution)/shard_map/all_to_all | solution.py:93
  119.9 14.8 %all-to-all-start.2 = ((f32[32,8,256]{2,1,0:T(8,128)}), f32[32,8,256]{2,1,0:T(8,128)S(1)}, u32[]{:S(2)}, u32[]{:S(2)}) async-start(f32[32,8,256]{2,1,0:T(8,128)} %broadcast_in_dim.25), calls=%async_computation.2 | async-start | bytes 524288 | tf_op jit(solution)/shard_map/all_to_all | solution.py:33
  135.3 6.2 %collective-permute-start.1 = (f32[32,256]{1,0:T(8,128)S(1)}, f32[32,256]{1,0:T(8,128)S(1)}, u32[]{:S(2)}, u32[]{:S(2)}) collective-permute-start(f32[32,256]{1,0:T(8,128)S(1)} %dynamic-slice_bitcast_fusion.2), channel_id=1, source_target_pairs={{0,1},{1,0},{2,3},{3,2},{4,5},{5,4},{6,7},{7,6},{8,9},{9,8},{10,11... | collective-permute-start | bytes 98312 | tf_op jit(solution)/shard_map/ppermute | solution.py:18
  142.2 15.0 %all-to-all-start.3 = ((f32[8,32,256]{2,1,0:T(8,128)}), f32[8,32,256]{2,1,0:T(8,128)S(1)}, u32[]{:S(2)}, u32[]{:S(2)}) async-start(f32[8,32,256]{2,1,0:T(8,128)} %broadcast_in_dim.26), calls=%async_computation.3 | async-start | bytes 524288 | tf_op jit(solution)/shard_map/all_to_all | solution.py:33
  158.0 8.1 %all-to-all-start.4 = ((f32[4,32,256]{2,1,0:T(8,128)}), f32[4,32,256]{2,1,0:T(8,128)S(1)}, u32[]{:S(2)}, u32[]{:S(2)}) async-start(f32[4,32,256]{2,1,0:T(8,128)} %broadcast_in_dim.27), calls=%async_computation.4 | async-start | bytes 262144 | tf_op jit(solution)/shard_map/all_to_all | solution.py:33
  166.1 5.7 %collective-permute-start.2 = (f32[4,32,256]{2,1,0:T(8,128)S(1)}, f32[4,32,256]{2,1,0:T(8,128)S(1)}, u32[]{:S(2)}, u32[]{:S(2)}) collective-permute-start(f32[4,32,256]{2,1,0:T(8,128)S(1)} %all-to-all-done.4), channel_id=1, source_target_pairs={{0,1},{1,0},{2,3},{3,2},{4,5},{5,4},{6,7},{7,6},{8,9},{9,8},{10,11... | collective-permute-start | bytes 393224 | tf_op jit(solution)/shard_map/ppermute | solution.py:18
  232.9 3.1 collective-permute-start.3
  258.1 4.5 %collective-permute-start.4 = (f32[4,32,256]{2,1,0:T(8,128)S(1)}, f32[4,32,256]{2,1,0:T(8,128)S(1)}, u32[]{:S(2)}, u32[]{:S(2)}) collective-permute-start(f32[4,32,256]{2,1,0:T(8,128)S(1)} %all_to_all.35), channel_id=1, source_target_pairs={{0,1},{1,0},{2,3},{3,2},{4,5},{5,4},{6,7},{7,6},{8,9},{9,8},{10,11... | collective-permute-start | bytes 393224 | tf_op jit(solution)/shard_map/ppermute | solution.py:18
Sparse Core Ops, SparseCore 0:
  56.1 38.9 all-gather.1

commit v2 on v1

--- a/solution.py
+++ b/solution.py
@@ -1,8 +1,11 @@
+import functools
 import math
 
 import jax
 import jax.numpy as jnp
 from jax import lax
+from jax.experimental import pallas as pl
+from jax.experimental.pallas import tpu as pltpu
 from jax.sharding import PartitionSpec as P
 
 D = 4096
@@ -11,6 +14,15 @@
 X = 4
 F32 = jnp.float32
 BF16 = jnp.bfloat16
+F16 = jnp.float16
+
+LIFT = 16.0
+FLOOR = 1e-4
+CLOSE = 4e-6
+STEPS = 14
+
+PLAIN = (((1,), (0,)), ((), ()))
+OUTER = (((1,), (1,)), ((), ()))
 
 
 def core_swap(value):
@@ -25,7 +37,7 @@
 
 def groups_x():
     count = lax.axis_size("dp")
-    return [list(range(y, y + X, 1)) for y in range(0, count, X)]
+    return [list(range(y, y + X)) for y in range(0, count, X)]
 
 
 def spread(value, axis, groups, size):
@@ -42,7 +54,7 @@
     other = lax.dynamic_index_in_dim(split, 1 - core, 1, False)
     pair = mine + core_swap(other)
     pieces = lax.all_to_all(
-        pair.astype(jnp.float16), "feat", 0, 0, axis_index_groups=groups_z()
+        (pair * LIFT).astype(F16), "feat", 0, 0, axis_index_groups=groups_z()
     )
     return jnp.sum(pieces.astype(F32), axis=0)
 
@@ -64,12 +76,92 @@
     return jnp.stack([first, second], axis=1).reshape(rank, rank)
 
 
-def orthonormal(matrix, dp, feat):
+def halves(value):
+    high = value.astype(BF16)
+    return high, (value - high.astype(F32)).astype(BF16)
+
+
+def product(left, right, dims):
+    dot = functools.partial(
+        lax.dot_general, dimension_numbers=dims, preferred_element_type=F32
+    )
+    return dot(left[0], right[0]) + (dot(left[0], right[1]) + dot(left[1], right[0]))
+
+
+def factor_kernel(gram_ref, matrix_ref, basis_ref, upper_ref, done_ref, inverse):
+    gram = gram_ref[...]
+    row = lax.broadcasted_iota(jnp.int32, gram.shape, 0)
+    col = lax.broadcasted_iota(jnp.int32, gram.shape, 1)
+    diagonal = jnp.where(row == col, gram, 0.0)
+    norms = jnp.sum(diagonal, axis=0, keepdims=True)
+    scale_down = lax.rsqrt(jnp.sum(diagonal, axis=1, keepdims=True))
+    scale_across = lax.rsqrt(norms)
+    unit = gram * scale_down * scale_across
+    eye = jnp.where(row == col, 1.0, 0.0)
+    keep = jnp.where(row > col, 1.0, jnp.where(row == col, 0.5, 0.0))
+    unit_parts = halves(unit)
+    inverse[...] = eye - (unit - eye) * keep
+
+    def improve():
+        now = inverse[...]
+        parts = halves(now)
+        moved = product(parts, unit_parts, PLAIN)
+        excess = product(halves(moved), parts, OUTER) - eye
+        inverse[...] = now - product(halves(excess * keep), parts, PLAIN)
+        return jnp.sum(excess * excess)
+
+    improve()
+    _, error = lax.while_loop(
+        lambda state: jnp.logical_and(state[0] < STEPS, jnp.logical_not(state[1] < CLOSE)),
+        lambda state: (state[0] + 1, improve()),
+        (2, improve()),
+    )
+    parts = halves(inverse[...])
+    upper = product(parts, unit_parts, PLAIN) / scale_across
+    upper_ref[...] = jnp.where(row <= col, upper, 0.0)
+    matrix = matrix_ref[...] * scale_across
+    basis_ref[...] = product(halves(matrix), parts, OUTER) * math.sqrt(D)
+    done = jnp.logical_and(error < CLOSE, jnp.min(norms) > FLOOR)
+    done_ref[0] = jnp.where(done, 1, 0)
+
+
+def factor(gram, matrix):
+    whole = jax.ShapeDtypeStruct(gram.shape, F32)
+    vmem = pl.BlockSpec(memory_space=pltpu.VMEM)
+    return pl.pallas_call(
+        factor_kernel,
+        out_shape=(whole, whole, jax.ShapeDtypeStruct((1,), jnp.int32)),
+        in_specs=[vmem, vmem],
+        out_specs=(vmem, vmem, pl.BlockSpec(memory_space=pltpu.SMEM)),
+        scratch_shapes=[pltpu.VMEM(gram.shape, F32)],
+        compiler_params=pltpu.CompilerParams(vmem_limit_bytes=32 * 1024 * 1024),
+        name="factor",
+    )(gram, matrix)
+
+
+def orthonormal(matrix):
     local_gram = jnp.dot(matrix.T, matrix, precision=lax.Precision.HIGHEST)
-    gram_total = sum_gram(local_gram, dp, feat)
+    gram_total = lax.psum(local_gram, "feat")
     lower = jnp.linalg.cholesky(gram_total)
     solved = jax.scipy.linalg.solve_triangular(lower, matrix.T, lower=True)
     return (solved.T, lower.T)
+
+
+def general(data, block_counts, basis):
+    rows, rank = data.shape[0], basis.shape[1]
+    active = lax.dynamic_index_in_dim(block_counts, lax.axis_index("dp"), 0, False)
+    valid = lax.broadcasted_iota(jnp.int32, (rows, 1), 0) < active * BLOCK
+    partial = jnp.dot(data, basis, preferred_element_type=F32)
+    images = lax.psum(jnp.where(valid, partial, 0.0), "feat").astype(BF16)
+    terms = lax.dot_general(
+        data, images, (((0,), (0,)), ((), ())), preferred_element_type=F32
+    )
+    row_total = (jnp.sum(block_counts) * BLOCK).astype(F32)
+    updated = basis.astype(F32) + lax.psum(terms, "dp") / row_total
+    first_basis, upper_one = orthonormal(updated)
+    second_basis, upper_two = orthonormal(first_basis)
+    upper = jnp.dot(upper_two, upper_one, precision=lax.Precision.HIGHEST)
+    return (second_basis * math.sqrt(D), upper)
 
 
 def on_device(data, block_counts, basis):
@@ -84,8 +176,8 @@
     images = sum_images(partial, feat)
     here = images.shape[0]
     row_ids = feat * here + lax.broadcasted_iota(jnp.int32, (here, 1), 0)
-    images = jnp.where(row_ids < active * BLOCK, images, 0.0).astype(BF16)
-    images = lax.all_gather(images, "feat", tiled=True)
+    images = jnp.where(row_ids < active * BLOCK, images, 0.0).astype(F16)
+    images = lax.all_gather(images, "feat", tiled=True).astype(BF16)
 
     terms = lax.dot_general(
         data, images, (((0,), (0,)), ((), ())), preferred_element_type=F32
@@ -94,12 +186,15 @@
     piece = jnp.sum(pieces, axis=0)
     summed_terms = spread(piece, "dp", None, dp_size).reshape(columns, rank)
 
-    row_total = (jnp.sum(block_counts) * BLOCK).astype(F32)
+    row_total = (jnp.sum(block_counts) * BLOCK).astype(F32) * LIFT
     updated = basis.astype(F32) + summed_terms / row_total
-    first_basis, upper_one = orthonormal(updated, dp, feat)
-    second_basis, upper_two = orthonormal(first_basis, dp, feat)
-    upper = jnp.dot(upper_two, upper_one, precision=lax.Precision.HIGHEST)
-    return (second_basis * math.sqrt(D), upper)
+    local_gram = jnp.dot(updated.T, updated, precision=lax.Precision.HIGHEST)
+    basis_scaled, upper, done = factor(sum_gram(local_gram, dp, feat), updated)
+    return lax.cond(
+        done[0] == 1,
+        lambda: (basis_scaled, upper),
+        lambda: general(data, block_counts, basis),
+    )
 
 
 def solution(mesh):

time: 334 us -> 745 us (2.23)
  waiting for transfers between devices: 105 us -> 411 us
  blocking collectives: 22 us -> 120 us
  starting transfers between devices: 50.5 us -> 28.9 us
  Pallas kernels: 0 us -> 12.4 us
    psum x0 -> x3, waiting for transfers between devices: none -> 374 us  [the longest x2 230 us: orthonormal(): gram_total = lax.psum(local_gram, 'feat')]
    psum x0 -> x1, blocking collectives: none -> 57.7 us  [general(): images = lax.psum(jnp.where(valid, partial, 0.0), 'feat').astype(BF16)]
    all_gather x1 -> x0, waiting for transfers between devices: 39.1 us -> none  [on_device(): images = lax.all_gather(images, 'feat', tiled=True)]
    all_to_all x0 -> x1, blocking collectives: none -> 21.4 us  [on_device(): lax.all_to_all(terms.reshape(dp_size, columns // dp_size, rank), 'dp', 0, 0)]
    all_gather x0 -> x1, blocking collectives: none -> 19.7 us  [on_device(): images = lax.all_gather(images, 'feat', tiled=True).astype(BF16)]
    all_to_all x3 -> x1, waiting for transfers between devices: 24.9 us -> 9.13 us  [spread(): return lax.all_to_all(copies, axis, 0, 0, axis_index_groups=groups)]
    pallas_call x0 -> x1, Pallas kernels: none -> 12.4 us  [factor(): pl.pallas_call(factor_kernel, out_shape=(whole, whole, jax.ShapeDtypeStru...]
    all_to_all x2 -> x1, waiting for transfers between devices: 34.1 us -> 22.3 us  [sum_images(): lax.all_to_all((pair * LIFT).astype(F16), 'feat', 0, 0, axis_index_groups...]
  transfers between devices with their start and end apart: 11 -> 8, of which waited for: 11 -> 8; matrix products, arithmetic and copies ran while one was open for 0% -> 0% of each run, Pallas kernels for 0% -> 0%
where the time goes in v2:
time: 745 us; the launch traced here: 738 us
  waiting for transfers between devices  411 us (55%)
  blocking collectives  120 us (16%)
  other arithmetic  116 us (16%)
  starting transfers between devices  28.9 us (4%)
  between operations  16.1 us (2%)
  matrix products  14.6 us (2%)
  local copies, waits for them, and re-layouts  14.6 us (2%)
  Pallas kernels  12.4 us (2%)
    psum x2, waiting for transfers between devices, orthonormal(): gram_total = lax.psum(local_gram, 'feat')  230 us
    psum x1, waiting for transfers between devices, general(): updated = basis.astype(F32) + lax.psum(terms, 'dp') / row_total  144 us
    another operation x13, other arithmetic, orthonormal(): lower = jnp.linalg.cholesky(gram_total)  68.7 us
    psum x1, blocking collectives, general(): images = lax.psum(jnp.where(valid, partial, 0.0), 'feat').astype(BF16)  57.7 us
    another operation x5, other arithmetic, orthonormal(): solved = jax.scipy.linalg.solve_triangular(lower, matrix.T, lower=True)  39.8 us
    all_to_all x1, waiting for transfers between devices, sum_images(): lax.all_to_all((pair * LIFT).astype(F16), 'feat', 0, 0, axis_index_groups...  22.3 us
    all_to_all x1, blocking collectives, on_device(): lax.all_to_all(terms.reshape(dp_size, columns // dp_size, rank), 'dp', 0, 0)  21.4 us
    all_to_all x2, blocking collectives, spread(): return lax.all_to_all(copies, axis, 0, 0, axis_index_groups=groups)  21.2 us
  transfers between devices with their start and end apart: 8, of which 8 were waited for; matrix products, arithmetic and copies ran while one was open for 0% of the time, Pallas kernels for 0%

profile of v2, /device:TPU:1, one launch (start us, length us, event | category | flops | bytes accessed | tf_op | source)
XLA Modules:
  0.0 737.7 jit_solution(4475864002306275385)
XLA Ops:
  7.2 2.0 fusion.54
  9.2 1.3 dynamic-slice_bitcast_fusion
  10.5 8.8 %collective-permute-start = (f32[8,192,256]{2,1,0:T(8,128)}, f32[8,192,256]{2,1,0:T(8,128)}, u32[]{:S(2)}, u32[]{:S(2)}) collective-permute-start(f32[8,192,256]{2,1,0:T(8,128)} %dynamic-slice_bitcast_fusion), channel_id=1, source_target_pairs={{0,1},{1,0},{2,3},{3,2},{4,5},{5,4},{6,7},{7,6},{8,9},{9,8},{10,11... | collective-permute-start | bytes 4718600 | tf_op jit(solution)/shard_map/ppermute | solution.py:30
  19.3 3.3 collective-permute-done
  22.6 2.6 fusion.46
  25.2 4.8 all-to-all-start
  30.0 0.6 dynamic_slice.23
  31.2 22.3 %all-to-all-done = f16[8,192,256]{2,1,0:T(8,128)(2,1)S(1)} async-done(((f16[8,192,256]{2,1,0:T(8,128)(2,1)}), f16[8,192,256]{2,1,0:T(8,128)(2,1)S(1)}, u32[]{:S(2)}, u32[]{:S(2)}) %all-to-all-start) | async-done | bytes 786464 | tf_op jit(solution)/shard_map/all_to_all | solution.py:56
  53.8 19.7 %all-gather.1 = f16[3072,256]{1,0:T(8,128)(2,1)S(1)} all-gather(f16[192,256]{1,0:T(8,128)(2,1)S(1)} %select_convert_fusion), channel_id=1, replica_groups=mesh['dp'=32,'feat'=16] {'feat'}, dimensions={0}, use_global_device_ids=true | all-gather | bytes 1671168 | tf_op jit(solution)/shard_map/all_gather | solution.py:180
  73.4 0.8 fusion.49
  74.2 21.4 %all_to_all.25 = f32[32,8,256]{2,1,0:T(8,128)S(1)} all-to-all(f32[32,8,256]{2,1,0:T(8,128)S(1)} %fusion.49), channel_id=1, replica_groups=mesh['dp'=32,'feat'=16] {'dp'}, dimensions={0} | all-to-all | bytes 524288 | tf_op jit(solution)/shard_map/all_to_all | solution.py:185
  95.7 0.7 broadcast_in_dim.45
  96.4 4.4 all-to-all-start.2
  100.8 0.6 reduce_sum.47
  102.1 9.1 %all-to-all-done.2 = f32[32,8,256]{2,1,0:T(8,128)S(1)} async-done(((f32[32,8,256]{2,1,0:T(8,128)}), f32[32,8,256]{2,1,0:T(8,128)S(1)}, u32[]{:S(2)}, u32[]{:S(2)}) %all-to-all-start.2) | async-done | bytes 262176 | tf_op jit(solution)/shard_map/all_to_all | solution.py:45
  111.2 0.6 fusion.55
  111.9 5.4 collective-permute-start.1
  117.3 0.8 collective-permute-done.1
  118.1 14.0 %all_to_all.26 = f32[8,32,256]{2,1,0:T(8,128)S(1)} all-to-all(f32[8,32,256]{2,1,0:T(8,128)S(1)} %broadcast_in_dim.46), channel_id=1, replica_groups={{0,2,4,6,8,10,12,14},{1,3,5,7,9,11,13,15},{16,18,20,22,24,26,28,30},{17..., dimensions={0} | all-to-all | bytes 524288 | tf_op jit(solution)/shard_map/all_to_all | solution.py:45
  132.2 7.2 all_to_all.27
  139.4 4.9 collective-permute-start.2
  144.4 1.0 collective-permute-done.2
  145.4 12.4 %factor.1 = (f32[256,256]{1,0:T(8,128)S(1)}, f32[256,256]{1,0:T(8,128)}, s32[1]{0:T(128)}) custom-call(f32[256,256]{1,0:T(8,128)S(1)} %bitcast.108, f32[256,256]{1,0:T(8,128)S(1)} %bitcast_add_fusion.3.matrix_ref), custom_call_target="tpu_custom_call" | custom-call | tf_op jit(solution)/shard_map/factor/pallas_call | solution.py:131
  158.4 571.7 %conditional.1 = (f32[256,256]{1,0:T(8,128)}, f32[256,256]{1,0:T(8,128)S(1)}) conditional(s32[]{:T(128)} %bitcast.28, (bf16[256,256]{1,0:T(8,128)(2,1)S(1)}, s32[32]{0:T(128)S(1)}, bf16[3072,256]{1,0:T(8,128)(2,1)S(1)}) %tuple.83, (f32[256,256]{1,0:T(8,128)S(1)}, f32[256,256]{1,0:T(8,128)}) %tuple.17), branch_computations={%region_4.16_spmd, %region_14.17_spmd} | conditional | flops 1815842304 | bytes 30550784 | solution.py:193
  158.5 0.6 dynamic_slice.17
  159.7 2.8 convolution_select_fusion
  162.5 57.7 %all-reduce.11 = bf16[3072,256]{1,0:T(8,128)(2,1)S(1)} all-reduce(f32[3072,256]{1,0:T(8,128)} %convolution_select_fusion), channel_id=1, replica_groups=mesh['dp'=32,'feat'=16] {'feat'}, use_global_device_ids=true, to_apply=%region_5.5 | all-reduce | flops 786432 | bytes 4718592 | tf_op jit(solution)/shard_map/cond/branch_0_fun/psum | solution.py:155
  220.3 1.3 fusion.2
  221.7 0.7 reduce_sum.40
  223.1 143.9 %all-reduce.6.cloned.1.call-done = f32[256,256]{0,1:T(8,128)} async-done(((f32[256,256]{0,1:T(8,128)}), f32[256,256]{0,1:T(8,128)}) %all-reduce.6.cloned.1.call-update) | async-done | bytes 262160 | tf_op jit(solution)/shard_map/cond/branch_0_fun/psum | solution.py:160
  367.1 2.2 fusion.41
  369.2 0.6 all-reduce.10.cloned.1.call-start
  369.8 1.0 fusion.40
  370.8 115.6 %all-reduce.8.cloned.1.call-done = f32[256,256]{0,1:T(8,128)} async-done(((f32[256,256]{0,1:T(8,128)}), f32[256,256]{0,1:T(8,128)}) %all-reduce.8.cloned.1.call-update) | async-done | bytes 262160 | tf_op jit(solution)/shard_map/cond/branch_0_fun/psum | solution.py:144
  486.4 1.1 copy.18
  487.5 1.0 fusion.11
  488.5 11.7 %cholesky.130 = f32[128,128]{1,0:T(8,128)S(1)} custom-call(f32[128,128]{1,0:T(8,128)S(1)} %cholesky.194), custom_call_target="Cholesky" | custom-call | tf_op jit(solution)/shard_map/cond/branch_0_fun/jit(cholesky)/cholesky | solution.py:145
  500.2 9.8 %custom-call.13 = f32[1,128,128]{1,2,0:T(8,128)S(1)} custom-call(f32[1,128,128]{2,1,0:T(8,128)S(1)} %get-tuple-element.85), custom_call_target="InvertDiagBlocksLowerTriangular" | custom-call | tf_op jit(solution)/shard_map/cond/branch_0_fun/jit(cholesky)/cholesky | solution.py:145
  510.5 11.7 %cholesky.147 = f32[128,128]{1,0:T(8,128)S(1)} custom-call(f32[128,128]{1,0:T(8,128)S(1)} %convolution_subtract_fusion.3), custom_call_target="Cholesky" | custom-call | tf_op jit(solution)/shard_map/cond/branch_0_fun/jit(cholesky)/cholesky | solution.py:145
  522.3 0.7 compare_reduce_fusion.2
  524.5 4.1 while.4
  524.5 0.6 fusion.76
  525.1 1.4 bitcast_dynamic-update-slice_fusion.4
  526.6 0.6 fusion.76
  527.2 1.4 bitcast_dynamic-update-slice_fusion.4
  528.6 19.8 %custom-call.14 = f32[2,128,128]{1,2,0:T(8,128)S(1)} custom-call(f32[2,128,128]{2,1,0:T(8,128)S(1)} %get-tuple-element.41), custom_call_target="InvertDiagBlocksLowerTriangular" | custom-call | tf_op jit(solution)/shard_map/cond/branch_0_fun/jit(_solve_triangular)/triangular_solve | solution.py:146
  549.0 0.3 fusion.31
  549.4 1.1 fusion.5
  550.5 114.5 %all-reduce.10.cloned.1.call-done = f32[256,256]{0,1:T(8,128)} async-done(((f32[256,256]{0,1:T(8,128)}), f32[256,256]{0,1:T(8,128)}) %all-reduce.10.cloned.1.call-update) | async-done | bytes 262160 | tf_op jit(solution)/shard_map/cond/branch_0_fun/psum | solution.py:144
  665.0 1.1 copy.20
  666.1 1.0 fusion.10
  667.1 11.7 %cholesky.164 = f32[128,128]{1,0:T(8,128)S(1)} custom-call(f32[128,128]{1,0:T(8,128)S(1)} %cholesky.197), custom_call_target="Cholesky" | custom-call | tf_op jit(solution)/shard_map/cond/branch_0_fun/jit(cholesky)/cholesky | solution.py:145
  678.8 9.8 %custom-call.15 = f32[1,128,128]{1,2,0:T(8,128)S(1)} custom-call(f32[1,128,128]{2,1,0:T(8,128)S(1)} %get-tuple-element.81), custom_call_target="InvertDiagBlocksLowerTriangular" | custom-call | tf_op jit(solution)/shard_map/cond/branch_0_fun/jit(cholesky)/cholesky | solution.py:145
  689.1 11.7 %cholesky.181 = f32[128,128]{1,0:T(8,128)S(1)} custom-call(f32[128,128]{1,0:T(8,128)S(1)} %convolution_subtract_fusion.2), custom_call_target="Cholesky" | custom-call | tf_op jit(solution)/shard_map/cond/branch_0_fun/jit(cholesky)/cholesky | solution.py:145
  700.9 0.7 compare_reduce_fusion
  701.6 0.6 compare_reduce_fusion.1
  703.6 1.2 fusion.16
  704.8 4.1 while.5
  704.9 0.6 fusion.77
  705.5 1.4 bitcast_dynamic-update-slice_fusion.5
  706.9 0.6 fusion.77
  707.5 1.4 bitcast_dynamic-update-slice_fusion.5
  708.9 19.9 %custom-call.16 = f32[2,128,128]{1,2,0:T(8,128)S(1)} custom-call(f32[2,128,128]{2,1,0:T(8,128)S(1)} %get-tuple-element.42), custom_call_target="InvertDiagBlocksLowerTriangular" | custom-call | tf_op jit(solution)/shard_map/cond/branch_0_fun/jit(_solve_triangular)/triangular_solve | solution.py:146
  730.2 0.7 copy-done.2
  (55 shorter events, 3.5 us)
Async XLA Ops:
  10.5 12.1 %collective-permute-start = (f32[8,192,256]{2,1,0:T(8,128)}, f32[8,192,256]{2,1,0:T(8,128)}, u32[]{:S(2)}, u32[]{:S(2)}) collective-permute-start(f32[8,192,256]{2,1,0:T(8,128)} %dynamic-slice_bitcast_fusion), channel_id=1, source_target_pairs={{0,1},{1,0},{2,3},{3,2},{4,5},{5,4},{6,7},{7,6},{8,9},{9,8},{10,11... | collective-permute-start | bytes 4718600 | tf_op jit(solution)/shard_map/ppermute | solution.py:30
  25.2 4.8 copy-start.3
  25.2 28.4 %all-to-all-start = ((f16[8,192,256]{2,1,0:T(8,128)(2,1)}), f16[8,192,256]{2,1,0:T(8,128)(2,1)S(1)}, u32[]{:S(2)}, u32[]{:S(2)}) async-start(f16[8,192,256]{2,1,0:T(8,128)(2,1)} %fusion.46), calls=%async_computation | async-start | bytes 1572864 | tf_op jit(solution)/shard_map/all_to_all | solution.py:56
  30.0 43.4 %copy-start = (bf16[3072,256]{1,0:T(8,128)(2,1)S(1)}, bf16[3072,256]{1,0:T(8,128)(2,1)}, u32[]{:S(2)}) copy-start(bf16[3072,256]{1,0:T(8,128)(2,1)} %param.8) | copy-start | bytes 4718596
  74.2 37.0 %copy-start.1 = (bf16[256,256]{1,0:T(8,128)(2,1)S(1)}, bf16[256,256]{1,0:T(8,128)(2,1)}, u32[]{:S(2)}) copy-start(bf16[256,256]{1,0:T(8,128)(2,1)} %param.10) | copy-start | bytes 393220
  96.4 14.8 %all-to-all-start.2 = ((f32[32,8,256]{2,1,0:T(8,128)}), f32[32,8,256]{2,1,0:T(8,128)S(1)}, u32[]{:S(2)}, u32[]{:S(2)}) async-start(f32[32,8,256]{2,1,0:T(8,128)} %broadcast_in_dim.45), calls=%async_computation.2 | async-start | bytes 524288 | tf_op jit(solution)/shard_map/all_to_all | solution.py:45
  111.9 6.2 collective-permute-start.1
  139.4 5.9 collective-permute-start.2
  158.4 208.6 %all-reduce.6.cloned.1.call-start = ((), (), s32[]{:S(2)}) async-start(), calls=%async_computation.5 | async-start | bytes 524288 | tf_op jit(solution)/shard_map/cond/branch_0_fun/psum | solution.py:160
  221.6 264.7 %all-reduce.8.cloned.1.call-start = ((), (), s32[]{:S(2)}) async-start(), calls=%async_computation.6 | async-start | bytes 524288 | tf_op jit(solution)/shard_map/cond/branch_0_fun/psum | solution.py:144
  369.2 295.7 %all-reduce.10.cloned.1.call-start = ((), (), s32[]{:S(2)}) async-start(), calls=%async_computation.7 | async-start | bytes 524288 | tf_op jit(solution)/shard_map/cond/branch_0_fun/psum | solution.py:144
  730.2 0.7 copy-start.2
Sparse Core Ops, SparseCore 0:
  221.8 145.2 all-reduce.5
  369.9 116.3 all-reduce.7
  550.6 114.3 all-reduce.9

commit v3 on v2

--- a/solution.py
+++ b/solution.py
@@ -45,34 +45,39 @@
     return lax.all_to_all(copies, axis, 0, 0, axis_index_groups=groups)
 
 
-def sum_images(partial, feat):
-    core = feat % CORES
+def sum_images(data, basis, core, other):
     chips = lax.axis_size("feat") // CORES
-    rows, rank = partial.shape
-    split = partial.reshape(chips, CORES, rows // (chips * CORES), rank)
-    mine = lax.dynamic_index_in_dim(split, core, 1, False)
-    other = lax.dynamic_index_in_dim(split, 1 - core, 1, False)
-    pair = mine + core_swap(other)
+    rows, columns = data.shape
+    split = data.reshape(chips, CORES, rows // (chips * CORES), columns)
+
+    def part(which):
+        picked = lax.dynamic_index_in_dim(split, which, 1, False)
+        return lax.dot_general(
+            picked, basis, (((2,), (0,)), ((), ())), preferred_element_type=F32
+        )
+
+    pair = part(core) + core_swap(part(other))
     pieces = lax.all_to_all(
         (pair * LIFT).astype(F16), "feat", 0, 0, axis_index_groups=groups_z()
     )
     return jnp.sum(pieces.astype(F32), axis=0)
 
 
-def sum_gram(gram, dp, feat):
-    core = feat % CORES
+def sum_gram(gram, first_core, low_pair, even):
     chips = lax.axis_size("feat") // CORES
     rank = gram.shape[0]
     split = gram.reshape(X, CORES, rank // (X * CORES), rank)
-    split = lax.dynamic_index_in_dim(split, dp % X, 0, False)
-    mine = lax.dynamic_index_in_dim(split, core, 0, False)
-    other = lax.dynamic_index_in_dim(split, 1 - core, 0, False)
-    pair = mine + core_swap(other)
+    low = jnp.where(even, split[0], split[1])
+    high = jnp.where(even, split[2], split[3])
+    split = jnp.where(low_pair, low, high)
+    mine = jnp.where(first_core, split[0], split[1])
+    theirs = jnp.where(first_core, split[1], split[0])
+    pair = mine + core_swap(theirs)
     total = jnp.sum(spread(pair, "feat", groups_z(), chips), axis=0)
-    quarter = spread(total, "dp", groups_x(), X)
-    theirs = core_swap(quarter)
-    first = jnp.where(core == 0, quarter, theirs)
-    second = jnp.where(core == 0, theirs, quarter)
+    half = spread(total, "dp", groups_x(), X)
+    theirs = core_swap(half)
+    first = jnp.where(first_core, half, theirs)
+    second = jnp.where(first_core, theirs, half)
     return jnp.stack([first, second], axis=1).reshape(rank, rank)
 
 
@@ -170,26 +175,32 @@
     dp = lax.axis_index("dp")
     feat = lax.axis_index("feat")
     dp_size = lax.axis_size("dp")
+    core = feat % CORES
+    here = rows // lax.axis_size("feat")
     active = lax.dynamic_index_in_dim(block_counts, dp, 0, False)
-
-    partial = jnp.dot(data, basis, preferred_element_type=F32)
-    images = sum_images(partial, feat)
-    here = images.shape[0]
     row_ids = feat * here + lax.broadcasted_iota(jnp.int32, (here, 1), 0)
-    images = jnp.where(row_ids < active * BLOCK, images, 0.0).astype(F16)
+    valid = jnp.where(row_ids < active * BLOCK, 1.0, 0.0)
+    row_total = (jnp.sum(block_counts) * BLOCK).astype(F32)
+    places = (core, 1 - core, core == 0, dp % X < 2, dp % 2 == 0)
+    data, basis, valid, row_total, places = lax.optimization_barrier(
+        (data, basis, valid, row_total, places)
+    )
+    core, other, first_core, low_pair, even = places
+
+    images = sum_images(data, basis, core, other)
+    images = (images * valid).astype(F16)
     images = lax.all_gather(images, "feat", tiled=True).astype(BF16)
 
     terms = lax.dot_general(
         data, images, (((0,), (0,)), ((), ())), preferred_element_type=F32
     )
+    terms = (terms / row_total).astype(F16)
     pieces = lax.all_to_all(terms.reshape(dp_size, columns // dp_size, rank), "dp", 0, 0)
-    piece = jnp.sum(pieces, axis=0)
-    summed_terms = spread(piece, "dp", None, dp_size).reshape(columns, rank)
-
-    row_total = (jnp.sum(block_counts) * BLOCK).astype(F32) * LIFT
-    updated = basis.astype(F32) + summed_terms / row_total
+    piece = jnp.sum(pieces.astype(F32), axis=0) / LIFT
+    step = spread(piece, "dp", None, dp_size).reshape(columns, rank)
+    updated = basis.astype(F32) + step
     local_gram = jnp.dot(updated.T, updated, precision=lax.Precision.HIGHEST)
-    basis_scaled, upper, done = factor(sum_gram(local_gram, dp, feat), updated)
+    basis_scaled, upper, done = factor(sum_gram(local_gram, first_core, low_pair, even), updated)
     return lax.cond(
         done[0] == 1,
         lambda: (basis_scaled, upper),

time: 745 us -> 744 us (level)
  blocking collectives: 120 us -> 160 us
  waiting for transfers between devices: 411 us -> 379 us
  starting transfers between devices: 28.9 us -> 19.5 us
    all_to_all x2 -> x0, waiting for transfers between devices: 31.4 us -> none  [the longest x1 22.3 us: sum_images(): lax.all_to_all((pair * LIFT).astype(F16), 'feat', 0, 0, axis_index_groups...]
    all_to_all x0 -> x1, blocking collectives: none -> 26.8 us  [sum_images(): lax.all_to_all((pair * LIFT).astype(F16), 'feat', 0, 0, axis_index_groups...]
    all_to_all x2 -> x3, blocking collectives: 21.2 us -> 35 us  [spread(): return lax.all_to_all(copies, axis, 0, 0, axis_index_groups=groups)]
    all_to_all x2 -> x0, starting transfers between devices: 9.14 us -> none  [the longest x1 4.79 us: sum_images(): lax.all_to_all((pair * LIFT).astype(F16), 'feat', 0, 0, axis_index_groups...]
  transfers between devices with their start and end apart: 8 -> 6, of which waited for: 8 -> 6; matrix products, arithmetic and copies ran while one was open for 0% -> 0% of each run, Pallas kernels for 0% -> 0%
where the time goes in v3:
time: 744 us; the launch traced here: 737 us
  waiting for transfers between devices  379 us (51%)
  blocking collectives  160 us (22%)
  other arithmetic  114 us (15%)
  starting transfers between devices  19.5 us (3%)
  matrix products  17.6 us (2%)
  between operations  16.1 us (2%)
  local copies, waits for them, and re-layouts  13.2 us (2%)
  Pallas kernels  12.4 us (2%)
    psum x2, waiting for transfers between devices, orthonormal(): gram_total = lax.psum(local_gram, 'feat')  230 us
    psum x1, waiting for transfers between devices, general(): updated = basis.astype(F32) + lax.psum(terms, 'dp') / row_total  144 us
    another operation x13, other arithmetic, orthonormal(): lower = jnp.linalg.cholesky(gram_total)  68.7 us
    psum x1, blocking collectives, general(): images = lax.psum(jnp.where(valid, partial, 0.0), 'feat').astype(BF16)  57.6 us
    another operation x5, other arithmetic, orthonormal(): solved = jax.scipy.linalg.solve_triangular(lower, matrix.T, lower=True)  40.2 us
    all_to_all x3, blocking collectives, spread(): return lax.all_to_all(copies, axis, 0, 0, axis_index_groups=groups)  35 us
    all_to_all x1, blocking collectives, sum_images(): lax.all_to_all((pair * LIFT).astype(F16), 'feat', 0, 0, axis_index_groups...  26.8 us
    all_gather x1, blocking collectives, on_device(): images = lax.all_gather(images, 'feat', tiled=True).astype(BF16)  21 us
  transfers between devices with their start and end apart: 6, of which 6 were waited for; matrix products, arithmetic and copies ran while one was open for 0% of the time, Pallas kernels for 0%

profile of v3, /device:TPU:1, one launch (start us, length us, event | category | flops | bytes accessed | tf_op | source)
XLA Modules:
  0.0 736.6 jit_solution(1189786040725366918)
XLA Ops:
  7.2 1.4 reduce_sum.45
  8.6 1.2 dynamic_slice.14
  11.2 1.5 fusion.56
  12.7 8.8 %collective-permute-start = (f32[8,192,256]{2,1,0:T(8,128)S(1)}, f32[8,192,256]{2,1,0:T(8,128)}, u32[]{:S(2)}, u32[]{:S(2)}) collective-permute-start(f32[8,192,256]{2,1,0:T(8,128)S(1)} %fusion.56), channel_id=1, source_target_pairs={{0,1},{1,0},{2,3},{3,2},{4,5},{5,4},{6,7},{7,6},{8,9},{9,8},{10,11... | collective-permute-start | bytes 4718600 | tf_op jit(solution)/shard_map/ppermute | solution.py:30
  21.5 3.1 collective-permute-done
  24.7 1.8 multiply_convert_fusion
  26.4 26.8 %all_to_all.25 = f16[8,192,256]{2,1,0:T(8,128)(2,1)S(1)} all-to-all(f16[8,192,256]{2,1,0:T(8,128)(2,1)S(1)} %multiply_convert_fusion), channel_id=1, replica_groups={{0,2,4,6,8,10,12,14},{1,3,5,7,9,11,13,15},{16,18,20,22,24,26,28,30},{17..., dimensions={0} | all-to-all | bytes 1572864 | tf_op jit(solution)/shard_map/all_to_all | solution.py:60
  53.4 21.0 %all-gather.1 = f16[3072,256]{1,0:T(8,128)(2,1)S(1)} all-gather(f16[192,256]{1,0:T(8,128)(2,1)S(1)} %multiply_convert_fusion.1), channel_id=1, replica_groups=mesh['dp'=32,'feat'=16] {'feat'}, dimensions={0}, use_global_device_ids=true | all-gather | bytes 1671168 | tf_op jit(solution)/shard_map/all_gather | solution.py:192
  74.4 0.6 fusion.53
  75.0 19.3 %all_to_all.26 = f16[32,8,256]{2,1,0:T(8,128)(2,1)S(1)} all-to-all(f16[32,8,256]{2,1,0:T(8,128)(2,1)S(1)} %fusion.53), channel_id=1, replica_groups=mesh['dp'=32,'feat'=16] {'dp'}, dimensions={0} | all-to-all | bytes 262144 | tf_op jit(solution)/shard_map/all_to_all | solution.py:198
  94.4 13.7 %all_to_all.27 = f32[32,8,256]{2,1,0:T(8,128)S(1)} all-to-all(f32[32,8,256]{2,1,0:T(8,128)S(1)} %broadcast_in_dim.41), channel_id=1, replica_groups=mesh['dp'=32,'feat'=16] {'dp'}, dimensions={0} | all-to-all | bytes 524288 | tf_op jit(solution)/shard_map/all_to_all | solution.py:45
  108.1 0.6 fusion.68
  108.8 5.4 collective-permute-start.1
  114.2 0.8 collective-permute-done.1
  115.1 14.1 %all_to_all.28 = f32[8,32,256]{2,1,0:T(8,128)S(1)} all-to-all(f32[8,32,256]{2,1,0:T(8,128)S(1)} %broadcast_in_dim.42), channel_id=1, replica_groups={{0,2,4,6,8,10,12,14},{1,3,5,7,9,11,13,15},{16,18,20,22,24,26,28,30},{17..., dimensions={0} | all-to-all | bytes 524288 | tf_op jit(solution)/shard_map/all_to_all | solution.py:45
  129.2 7.2 all_to_all.29
  136.4 4.9 collective-permute-start.2
  141.3 1.0 collective-permute-done.2
  142.4 12.4 %factor.1 = (f32[256,256]{1,0:T(8,128)S(1)}, f32[256,256]{1,0:T(8,128)}, s32[1]{0:T(128)}) custom-call(f32[256,256]{1,0:T(8,128)S(1)} %bitcast.107, f32[256,256]{1,0:T(8,128)S(1)} %bitcast_add_fusion.2.matrix_ref), custom_call_target="tpu_custom_call" | custom-call | tf_op jit(solution)/shard_map/factor/pallas_call | solution.py:136
  155.4 573.7 %conditional.1 = (f32[256,256]{1,0:T(8,128)}, f32[256,256]{1,0:T(8,128)S(1)}) conditional(s32[]{:T(128)} %bitcast.26, (bf16[256,256]{1,0:T(8,128)(2,1)S(1)}, s32[32]{0:T(128)S(1)}, bf16[3072,256]{1,0:T(8,128)(2,1)}) %tuple.87, (f32[256,256]{1,0:T(8,128)S(1)}, f32[256,256]{1,0:T(8,128)}) %tuple.19), branch_computations={%region_4.16_spmd, %region_14.17_spmd} | conditional | flops 1815842304 | bytes 30550784 | solution.py:204
  155.5 0.6 dynamic_slice.10
  156.7 2.8 convolution_select_fusion
  159.5 57.6 %all-reduce.11 = bf16[3072,256]{1,0:T(8,128)(2,1)} all-reduce(f32[3072,256]{1,0:T(8,128)S(1)} %convolution_select_fusion), channel_id=1, replica_groups=mesh['dp'=32,'feat'=16] {'feat'}, use_global_device_ids=true, to_apply=%region_5.5 | all-reduce | flops 786432 | bytes 4718592 | tf_op jit(solution)/shard_map/cond/branch_0_fun/psum | solution.py:160
  217.1 3.2 fusion.2
  220.3 0.7 reduce_sum.40
  221.8 143.9 %all-reduce.6.cloned.1.call-done = f32[256,256]{0,1:T(8,128)} async-done(((f32[256,256]{0,1:T(8,128)}), f32[256,256]{0,1:T(8,128)}) %all-reduce.6.cloned.1.call-update) | async-done | bytes 262160 | tf_op jit(solution)/shard_map/cond/branch_0_fun/psum | solution.py:165
  365.7 2.2 fusion.41
  367.9 0.3 all-reduce.10.cloned.1.call-start
  368.2 1.0 fusion.40
  369.2 115.9 %all-reduce.8.cloned.1.call-done = f32[256,256]{0,1:T(8,128)} async-done(((f32[256,256]{0,1:T(8,128)}), f32[256,256]{0,1:T(8,128)}) %all-reduce.8.cloned.1.call-update) | async-done | bytes 262160 | tf_op jit(solution)/shard_map/cond/branch_0_fun/psum | solution.py:149
  485.0 1.1 copy.26
  486.1 1.0 fusion.11
  487.1 11.7 %cholesky.130 = f32[128,128]{1,0:T(8,128)S(1)} custom-call(f32[128,128]{1,0:T(8,128)S(1)} %cholesky.194), custom_call_target="Cholesky" | custom-call | tf_op jit(solution)/shard_map/cond/branch_0_fun/jit(cholesky)/cholesky | solution.py:150
  498.8 9.8 %custom-call.13 = f32[1,128,128]{1,2,0:T(8,128)S(1)} custom-call(f32[1,128,128]{2,1,0:T(8,128)S(1)} %get-tuple-element.110), custom_call_target="InvertDiagBlocksLowerTriangular" | custom-call | tf_op jit(solution)/shard_map/cond/branch_0_fun/jit(cholesky)/cholesky | solution.py:150
  509.2 11.7 %cholesky.147 = f32[128,128]{1,0:T(8,128)S(1)} custom-call(f32[128,128]{1,0:T(8,128)S(1)} %convolution_subtract_fusion.3), custom_call_target="Cholesky" | custom-call | tf_op jit(solution)/shard_map/cond/branch_0_fun/jit(cholesky)/cholesky | solution.py:150
  520.9 0.7 compare_reduce_fusion.2
  523.1 4.1 while.4
  523.1 0.6 fusion.87
  523.7 1.4 bitcast_dynamic-update-slice_fusion.4
  525.2 0.6 fusion.87
  525.8 1.4 bitcast_dynamic-update-slice_fusion.4
  527.2 20.0 %custom-call.14 = f32[2,128,128]{1,2,0:T(8,128)S(1)} custom-call(f32[2,128,128]{2,1,0:T(8,128)S(1)} %get-tuple-element.59), custom_call_target="InvertDiagBlocksLowerTriangular" | custom-call | tf_op jit(solution)/shard_map/cond/branch_0_fun/jit(_solve_triangular)/triangular_solve | solution.py:151
  547.2 0.3 fusion.19
  547.8 0.3 fusion.31
  548.1 1.1 fusion.5
  549.2 114.5 %all-reduce.10.cloned.1.call-done = f32[256,256]{0,1:T(8,128)} async-done(((f32[256,256]{0,1:T(8,128)}), f32[256,256]{0,1:T(8,128)}) %all-reduce.10.cloned.1.call-update) | async-done | bytes 262160 | tf_op jit(solution)/shard_map/cond/branch_0_fun/psum | solution.py:149
  663.7 1.1 copy.28
  664.8 1.0 fusion.10
  665.8 11.7 %cholesky.164 = f32[128,128]{1,0:T(8,128)S(1)} custom-call(f32[128,128]{1,0:T(8,128)S(1)} %cholesky.197), custom_call_target="Cholesky" | custom-call | tf_op jit(solution)/shard_map/cond/branch_0_fun/jit(cholesky)/cholesky | solution.py:150
  677.6 9.8 %custom-call.15 = f32[1,128,128]{1,2,0:T(8,128)S(1)} custom-call(f32[1,128,128]{2,1,0:T(8,128)S(1)} %get-tuple-element.106), custom_call_target="InvertDiagBlocksLowerTriangular" | custom-call | tf_op jit(solution)/shard_map/cond/branch_0_fun/jit(cholesky)/cholesky | solution.py:150
  687.6 0.3 convolution_subtract_fusion.2
  687.9 11.7 %cholesky.181 = f32[128,128]{1,0:T(8,128)S(1)} custom-call(f32[128,128]{1,0:T(8,128)S(1)} %convolution_subtract_fusion.2), custom_call_target="Cholesky" | custom-call | tf_op jit(solution)/shard_map/cond/branch_0_fun/jit(cholesky)/cholesky | solution.py:150
  699.6 0.7 compare_reduce_fusion
  700.3 0.6 compare_reduce_fusion.1
  702.4 1.2 fusion.16
  703.6 4.1 while.5
  703.6 0.6 fusion.88
  704.2 1.4 bitcast_dynamic-update-slice_fusion.5
  705.7 0.6 fusion.88
  706.3 1.4 bitcast_dynamic-update-slice_fusion.5
  707.7 20.2 %custom-call.16 = f32[2,128,128]{1,2,0:T(8,128)S(1)} custom-call(f32[2,128,128]{2,1,0:T(8,128)S(1)} %get-tuple-element.60), custom_call_target="InvertDiagBlocksLowerTriangular" | custom-call | tf_op jit(solution)/shard_map/cond/branch_0_fun/jit(_solve_triangular)/triangular_solve | solution.py:151
  727.9 0.3 fusion.27
  728.5 0.3 fusion.26
  729.2 0.7 copy-done.2
  (54 shorter events, 2.4 us)
Async XLA Ops:
  7.2 17.5 %copy-start.1 = (bf16[256,256]{1,0:T(8,128)(2,1)S(1)}, bf16[256,256]{1,0:T(8,128)(2,1)}, u32[]{:S(2)}) copy-start(bf16[256,256]{1,0:T(8,128)(2,1)} %param.10) | copy-start | bytes 393220
  7.2 17.5 %copy-start = (bf16[3072,256]{1,0:T(8,128)(2,1)S(1)}, bf16[3072,256]{1,0:T(8,128)(2,1)}, u32[]{:S(2)}) copy-start(bf16[3072,256]{1,0:T(8,128)(2,1)} %param.8) | copy-start | bytes 4718596
  12.7 11.9 %collective-permute-start = (f32[8,192,256]{2,1,0:T(8,128)S(1)}, f32[8,192,256]{2,1,0:T(8,128)}, u32[]{:S(2)}, u32[]{:S(2)}) collective-permute-start(f32[8,192,256]{2,1,0:T(8,128)S(1)} %fusion.56), channel_id=1, source_target_pairs={{0,1},{1,0},{2,3},{3,2},{4,5},{5,4},{6,7},{7,6},{8,9},{9,8},{10,11... | collective-permute-start | bytes 4718600 | tf_op jit(solution)/shard_map/ppermute | solution.py:30
  108.8 6.3 collective-permute-start.1
  115.1 40.4 %copy-start.3 = (s32[32]{0:T(128)S(1)}, s32[32]{0:T(128)}, u32[]{:S(2)}) copy-start(s32[32]{0:T(128)} %param.9) | copy-start | bytes 388
  136.4 5.9 collective-permute-start.2
  155.4 210.3 %all-reduce.6.cloned.1.call-start = ((), (), s32[]{:S(2)}) async-start(), calls=%async_computation.5 | async-start | bytes 524288 | tf_op jit(solution)/shard_map/cond/branch_0_fun/psum | solution.py:165
  220.3 264.7 %all-reduce.8.cloned.1.call-start = ((), (), s32[]{:S(2)}) async-start(), calls=%async_computation.6 | async-start | bytes 524288 | tf_op jit(solution)/shard_map/cond/branch_0_fun/psum | solution.py:149
  367.9 295.9 %all-reduce.10.cloned.1.call-start = ((), (), s32[]{:S(2)}) async-start(), calls=%async_computation.7 | async-start | bytes 524288 | tf_op jit(solution)/shard_map/cond/branch_0_fun/psum | solution.py:149
  729.1 0.7 copy-start.2
Sparse Core Ops, SparseCore 0:
  220.4 145.2 all-reduce.5
  368.6 116.3 all-reduce.7
  549.4 114.3 all-reduce.9

commit v4 on v3

--- a/solution.py
+++ b/solution.py
@@ -22,6 +22,7 @@
 STEPS = 14
 
 PLAIN = (((1,), (0,)), ((), ()))
+ROWS = (((0,), (0,)), ((), ()))
 OUTER = (((1,), (1,)), ((), ()))
 
 
@@ -35,9 +36,13 @@
     return [list(range(c, count, CORES)) for c in range(CORES)]
 
 
-def groups_x():
-    count = lax.axis_size("dp")
-    return [list(range(y, y + X)) for y in range(0, count, X)]
+def groups_xc():
+    count, width = lax.axis_size("dp"), lax.axis_size("feat")
+    return [
+        [(y + x) * width + z + c for x in range(X) for c in range(CORES)]
+        for y in range(0, count, X)
+        for z in range(0, width, CORES)
+    ]
 
 
 def spread(value, axis, groups, size):
@@ -45,7 +50,15 @@
     return lax.all_to_all(copies, axis, 0, 0, axis_index_groups=groups)
 
 
-def sum_images(data, basis, core, other):
+def total(value, axis):
+    size = lax.axis_size(axis)
+    pieces = lax.all_to_all(
+        value.reshape((size, value.shape[0] // size) + value.shape[1:]), axis, 0, 0
+    )
+    return spread(jnp.sum(pieces, axis=0), axis, None, size).reshape(value.shape)
+
+
+def sum_images(data, basis, core, beside):
     chips = lax.axis_size("feat") // CORES
     rows, columns = data.shape
     split = data.reshape(chips, CORES, rows // (chips * CORES), columns)
@@ -56,29 +69,60 @@
             picked, basis, (((2,), (0,)), ((), ())), preferred_element_type=F32
         )
 
-    pair = part(core) + core_swap(part(other))
+    theirs = core_swap((part(1 - core) * LIFT).astype(F16))
+    mine, theirs, beside = lax.optimization_barrier((part(core), theirs, beside))
     pieces = lax.all_to_all(
-        (pair * LIFT).astype(F16), "feat", 0, 0, axis_index_groups=groups_z()
-    )
-    return jnp.sum(pieces.astype(F32), axis=0)
-
-
-def sum_gram(gram, first_core, low_pair, even):
+        (mine * LIFT + theirs.astype(F32)).astype(F16),
+        "feat",
+        0,
+        0,
+        axis_index_groups=groups_z(),
+    )
+    return jnp.sum(pieces.astype(F32), axis=0), beside
+
+
+def gram_kernel(place_ref, step_ref, basis_ref, updated_ref, mine_ref, theirs_ref, packed):
+    updated = basis_ref[...].astype(F32) + step_ref[...]
+    updated_ref[...] = updated
+    half = packed.shape[0]
+    share = mine_ref.shape[0]
+    dot = functools.partial(
+        lax.dot_general,
+        dimension_numbers=ROWS,
+        precision=lax.Precision.HIGHEST,
+        preferred_element_type=F32,
+    )
+    packed[:, : 2 * half] = dot(updated[:, :half], updated)
+    packed[:, 2 * half :] = dot(updated[:, half:], updated[:, half:])
+    first = place_ref[0] * CORES
+    mine = pl.multiple_of((first + place_ref[1]) * share, share)
+    theirs = pl.multiple_of((first + 1 - place_ref[1]) * share, share)
+    mine_ref[...] = packed[pl.ds(mine, share), :]
+    theirs_ref[...] = packed[pl.ds(theirs, share), :]
+
+
+def gram_share(place, step, basis):
+    rank = basis.shape[1]
+    half = rank // 2
+    share = jax.ShapeDtypeStruct((half // (X * CORES), rank + half), F32)
+    vmem = pl.BlockSpec(memory_space=pltpu.VMEM)
+    return pl.pallas_call(
+        gram_kernel,
+        out_shape=(jax.ShapeDtypeStruct(basis.shape, F32), share, share),
+        in_specs=[pl.BlockSpec(memory_space=pltpu.SMEM), vmem, vmem],
+        out_specs=(vmem, vmem, vmem),
+        scratch_shapes=[pltpu.VMEM((half, rank + half), F32)],
+        compiler_params=pltpu.CompilerParams(vmem_limit_bytes=32 * 1024 * 1024),
+        name="gram_share",
+    )(place, step, basis)
+
+
+def sum_gram(mine, theirs):
     chips = lax.axis_size("feat") // CORES
-    rank = gram.shape[0]
-    split = gram.reshape(X, CORES, rank // (X * CORES), rank)
-    low = jnp.where(even, split[0], split[1])
-    high = jnp.where(even, split[2], split[3])
-    split = jnp.where(low_pair, low, high)
-    mine = jnp.where(first_core, split[0], split[1])
-    theirs = jnp.where(first_core, split[1], split[0])
     pair = mine + core_swap(theirs)
-    total = jnp.sum(spread(pair, "feat", groups_z(), chips), axis=0)
-    half = spread(total, "dp", groups_x(), X)
-    theirs = core_swap(half)
-    first = jnp.where(first_core, half, theirs)
-    second = jnp.where(first_core, theirs, half)
-    return jnp.stack([first, second], axis=1).reshape(rank, rank)
+    summed = jnp.sum(spread(pair, "feat", groups_z(), chips), axis=0)
+    shares = spread(summed, ("dp", "feat"), groups_xc(), X * CORES)
+    return shares.reshape(-1, shares.shape[-1])
 
 
 def halves(value):
@@ -93,8 +137,12 @@
     return dot(left[0], right[0]) + (dot(left[0], right[1]) + dot(left[1], right[0]))
 
 
-def factor_kernel(gram_ref, matrix_ref, basis_ref, upper_ref, done_ref, inverse):
-    gram = gram_ref[...]
+def factor_kernel(packed_ref, matrix_ref, basis_ref, upper_ref, done_ref, inverse):
+    half = packed_ref.shape[0]
+    inverse[:half, :] = packed_ref[:, : 2 * half]
+    inverse[half:, :half] = packed_ref[:, half : 2 * half].T
+    inverse[half:, half:] = packed_ref[:, 2 * half :]
+    gram = inverse[...]
     row = lax.broadcasted_iota(jnp.int32, gram.shape, 0)
     col = lax.broadcasted_iota(jnp.int32, gram.shape, 1)
     diagonal = jnp.where(row == col, gram, 0.0)
@@ -130,23 +178,23 @@
     done_ref[0] = jnp.where(done, 1, 0)
 
 
-def factor(gram, matrix):
-    whole = jax.ShapeDtypeStruct(gram.shape, F32)
+def factor(packed, matrix):
+    whole = jax.ShapeDtypeStruct(matrix.shape, F32)
     vmem = pl.BlockSpec(memory_space=pltpu.VMEM)
     return pl.pallas_call(
         factor_kernel,
         out_shape=(whole, whole, jax.ShapeDtypeStruct((1,), jnp.int32)),
         in_specs=[vmem, vmem],
         out_specs=(vmem, vmem, pl.BlockSpec(memory_space=pltpu.SMEM)),
-        scratch_shapes=[pltpu.VMEM(gram.shape, F32)],
+        scratch_shapes=[pltpu.VMEM(matrix.shape, F32)],
         compiler_params=pltpu.CompilerParams(vmem_limit_bytes=32 * 1024 * 1024),
         name="factor",
-    )(gram, matrix)
+    )(packed, matrix)
 
 
 def orthonormal(matrix):
     local_gram = jnp.dot(matrix.T, matrix, precision=lax.Precision.HIGHEST)
-    gram_total = lax.psum(local_gram, "feat")
+    gram_total = total(local_gram, "feat")
     lower = jnp.linalg.cholesky(gram_total)
     solved = jax.scipy.linalg.solve_triangular(lower, matrix.T, lower=True)
     return (solved.T, lower.T)
@@ -157,12 +205,12 @@
     active = lax.dynamic_index_in_dim(block_counts, lax.axis_index("dp"), 0, False)
     valid = lax.broadcasted_iota(jnp.int32, (rows, 1), 0) < active * BLOCK
     partial = jnp.dot(data, basis, preferred_element_type=F32)
-    images = lax.psum(jnp.where(valid, partial, 0.0), "feat").astype(BF16)
+    images = total(jnp.where(valid, partial, 0.0), "feat").astype(BF16)
     terms = lax.dot_general(
         data, images, (((0,), (0,)), ((), ())), preferred_element_type=F32
     )
     row_total = (jnp.sum(block_counts) * BLOCK).astype(F32)
-    updated = basis.astype(F32) + lax.psum(terms, "dp") / row_total
+    updated = basis.astype(F32) + total(terms, "dp") / row_total
     first_basis, upper_one = orthonormal(updated)
     second_basis, upper_two = orthonormal(first_basis)
     upper = jnp.dot(upper_two, upper_one, precision=lax.Precision.HIGHEST)
@@ -181,13 +229,9 @@
     row_ids = feat * here + lax.broadcasted_iota(jnp.int32, (here, 1), 0)
     valid = jnp.where(row_ids < active * BLOCK, 1.0, 0.0)
     row_total = (jnp.sum(block_counts) * BLOCK).astype(F32)
-    places = (core, 1 - core, core == 0, dp % X < 2, dp % 2 == 0)
-    data, basis, valid, row_total, places = lax.optimization_barrier(
-        (data, basis, valid, row_total, places)
-    )
-    core, other, first_core, low_pair, even = places
-
-    images = sum_images(data, basis, core, other)
+    beside = (valid, row_total, jnp.stack([dp % X, core]))
+    images, beside = sum_images(data, basis, core, beside)
+    valid, row_total, place = beside
     images = (images * valid).astype(F16)
     images = lax.all_gather(images, "feat", tiled=True).astype(BF16)
 
@@ -198,9 +242,8 @@
     pieces = lax.all_to_all(terms.reshape(dp_size, columns // dp_size, rank), "dp", 0, 0)
     piece = jnp.sum(pieces.astype(F32), axis=0) / LIFT
     step = spread(piece, "dp", None, dp_size).reshape(columns, rank)
-    updated = basis.astype(F32) + step
-    local_gram = jnp.dot(updated.T, updated, precision=lax.Precision.HIGHEST)
-    basis_scaled, upper, done = factor(sum_gram(local_gram, first_core, low_pair, even), updated)
+    updated, mine, theirs = gram_share(place, step, basis)
+    basis_scaled, upper, done = factor(sum_gram(mine, theirs), updated)
     return lax.cond(
         done[0] == 1,
         lambda: (basis_scaled, upper),

time: 744 us -> 497 us (0.67)
  waiting for transfers between devices: 379 us -> 99.4 us
  blocking collectives: 160 us -> 199 us
  starting transfers between devices: 19.5 us -> 31.8 us
  between operations: 16.1 us -> 3.89 us
    psum x3 -> x0, waiting for transfers between devices: 374 us -> none  [the longest x2 230 us: orthonormal(): gram_total = lax.psum(local_gram, 'feat')]
    all_to_all x0 -> x4, waiting for transfers between devices: none -> 98.6 us  [the longest x1 71.1 us: total(): lax.all_to_all(value.reshape((size, value.shape[0] // size) + value.shape...]
    psum x1 -> x0, blocking collectives: 57.6 us -> none  [general(): images = lax.psum(jnp.where(valid, partial, 0.0), 'feat').astype(BF16)]
    all_to_all x3 -> x4, blocking collectives: 35 us -> 85.8 us  [spread(): return lax.all_to_all(copies, axis, 0, 0, axis_index_groups=groups)]
    all_to_all x1 -> x4, blocking collectives: 26.8 us -> 74.3 us  [the longest x3 46.2 us: total(): lax.all_to_all(value.reshape((size, value.shape[0] // size) + value.shape...]
    all_to_all x0 -> x4, starting transfers between devices: none -> 17.6 us  [the longest x3 13.1 us: spread(): return lax.all_to_all(copies, axis, 0, 0, axis_index_groups=groups)]
    ppermute x3 -> x2, starting transfers between devices: 19.1 us -> 14.2 us  [core_swap(): return lax.ppermute(value, 'feat', [(i, i ^ 1) for i in range(count)])]
  transfers between devices with their start and end apart: 6 -> 6, of which waited for: 6 -> 5; matrix products, arithmetic and copies ran while one was open for 0% -> 1% of each run, Pallas kernels for 0% -> 0%
where the time goes in v4:
time: 497 us; the launch traced here: 488 us
  blocking collectives  199 us (40%)
  other arithmetic  112 us (23%)
  waiting for transfers between devices  99.4 us (20%)
  starting transfers between devices  31.8 us (6%)
  Pallas kernels  13.5 us (3%)
  local copies, waits for them, and re-layouts  13.3 us (3%)
  matrix products  11.1 us (2%)
    all_to_all x4, blocking collectives, spread(): return lax.all_to_all(copies, axis, 0, 0, axis_index_groups=groups)  85.8 us
    all_to_all x1, waiting for transfers between devices, total(): lax.all_to_all(value.reshape((size, value.shape[0] // size) + value.shape...  71.1 us
    another operation x13, other arithmetic, orthonormal(): lower = jnp.linalg.cholesky(gram_total)  68.7 us
    all_to_all x3, blocking collectives, total(): lax.all_to_all(value.reshape((size, value.shape[0] // size) + value.shape...  46.2 us
    another operation x5, other arithmetic, orthonormal(): solved = jax.scipy.linalg.solve_triangular(lower, matrix.T, lower=True)  39.6 us
    all_to_all x1, blocking collectives, sum_images(): lax.all_to_all((mine * LIFT + theirs.astype(F32)).astype(F16), 'feat', 0,...  28.1 us
    all_to_all x3, waiting for transfers between devices, spread(): return lax.all_to_all(copies, axis, 0, 0, axis_index_groups=groups)  27.5 us
    all_gather x1, blocking collectives, on_device(): images = lax.all_gather(images, 'feat', tiled=True).astype(BF16)  19.6 us
  transfers between devices with their start and end apart: 6, of which 5 were waited for; matrix products, arithmetic and copies ran while one was open for 1% of the time, Pallas kernels for 0%

profile of v4, /device:TPU:1, one launch (start us, length us, event | category | flops | bytes accessed | tf_op | source)
XLA Modules:
  0.0 488.1 jit_solution(17189280378205279565)
XLA Ops:
  0.7 1.6 multiply_convert_fusion
  2.3 8.8 %collective-permute-start = (f16[8,192,256]{2,1,0:T(8,128)(2,1)S(1)}, f16[8,192,256]{2,1,0:T(8,128)(2,1)}, u32[]{:S(2)}, u32[]{:S(2)}) collective-permute-start(f16[8,192,256]{2,1,0:T(8,128)(2,1)S(1)} %multiply_convert_fusion), channel_id=1, source_target_pairs={{0,1},{1,0},{2,3},{3,2},{4,5},{5,4},{6,7},{7,6},{8,9},{9,8},{10,11... | collective-permute-start | bytes 2359304 | tf_op jit(solution)/shard_map/ppermute | solution.py:31
  11.1 0.6 reduce_sum.81
  11.8 0.6 dynamic_slice.16
  13.8 0.4 fusion.43
  14.2 1.4 add_convert_fusion
  15.6 28.1 %all_to_all.58 = f16[8,192,256]{2,1,0:T(8,128)(2,1)S(1)} all-to-all(f16[8,192,256]{2,1,0:T(8,128)(2,1)S(1)} %add_convert_fusion), channel_id=1, replica_groups={{0,2,4,6,8,10,12,14},{1,3,5,7,9,11,13,15},{16,18,20,22,24,26,28,30},{17..., dimensions={0} | all-to-all | bytes 1572864 | tf_op jit(solution)/shard_map/all_to_all | solution.py:74
  43.8 19.6 %all-gather.1 = f16[3072,256]{1,0:T(8,128)(2,1)S(1)} all-gather(f16[192,256]{1,0:T(8,128)(2,1)S(1)} %multiply_convert_fusion.1), channel_id=1, replica_groups=mesh['dp'=32,'feat'=16] {'feat'}, dimensions={0}, use_global_device_ids=true | all-gather | bytes 1671168 | tf_op jit(solution)/shard_map/all_gather | solution.py:236
  63.5 0.8 fusion.49
  64.3 19.3 %all_to_all.59 = f16[32,8,256]{2,1,0:T(8,128)(2,1)S(1)} all-to-all(f16[32,8,256]{2,1,0:T(8,128)(2,1)S(1)} %fusion.49), channel_id=1, replica_groups=mesh['dp'=32,'feat'=16] {'dp'}, dimensions={0} | all-to-all | bytes 262144 | tf_op jit(solution)/shard_map/all_to_all | solution.py:242
  83.6 13.7 %all_to_all.60 = f32[32,8,256]{2,1,0:T(8,128)S(1)} all-to-all(f32[32,8,256]{2,1,0:T(8,128)S(1)} %broadcast_in_dim.36), channel_id=1, replica_groups=mesh['dp'=32,'feat'=16] {'dp'}, dimensions={0} | all-to-all | bytes 524288 | tf_op jit(solution)/shard_map/all_to_all | solution.py:50
  97.4 1.0 gram_share.1
  98.4 5.4 %collective-permute-start.1 = (f32[16,384]{1,0:T(8,128)S(1)}, f32[16,384]{1,0:T(8,128)S(1)}, u32[]{:S(2)}, u32[]{:S(2)}) collective-permute-start(f32[16,384]{1,0:T(8,128)S(1)} %get-tuple-element.34), channel_id=1, source_target_pairs={{0,1},{1,0},{2,3},{3,2},{4,5},{5,4},{6,7},{7,6},{8,9},{9,8},{10,11... | collective-permute-start | bytes 73736 | tf_op jit(solution)/shard_map/ppermute | solution.py:31
  103.8 0.8 collective-permute-done.1
  104.6 12.3 %all_to_all.61 = f32[8,16,384]{2,1,0:T(8,128)S(1)} all-to-all(f32[8,16,384]{2,1,0:T(8,128)S(1)} %broadcast_in_dim.38), channel_id=1, replica_groups={{0,2,4,6,8,10,12,14},{1,3,5,7,9,11,13,15},{16,18,20,22,24,26,28,30},{17..., dimensions={0} | all-to-all | bytes 393216 | tf_op jit(solution)/shard_map/all_to_all | solution.py:50
  117.0 0.7 broadcast_in_dim.39
  117.7 5.3 %all-to-all-start.12 = ((f32[8,16,384]{2,1,0:T(8,128)}), f32[8,16,384]{2,1,0:T(8,128)S(1)}, u32[]{:S(2)}, u32[]{:S(2)}) async-start(f32[8,16,384]{2,1,0:T(8,128)} %broadcast_in_dim.39), calls=%async_computation.12 | async-start | bytes 393216 | tf_op jit(solution)/shard_map/all_to_all | solution.py:50
  122.9 5.9 %all-to-all-done.12 = f32[8,16,384]{2,1,0:T(8,128)S(1)} async-done(((f32[8,16,384]{2,1,0:T(8,128)}), f32[8,16,384]{2,1,0:T(8,128)S(1)}, u32[]{:S(2)}, u32[]{:S(2)}) %all-to-all-start.12) | async-done | bytes 196640 | tf_op jit(solution)/shard_map/all_to_all | solution.py:50
  128.8 12.6 %factor.1 = (f32[256,256]{1,0:T(8,128)}, f32[256,256]{1,0:T(8,128)}, s32[1]{0:T(128)}) custom-call(f32[128,384]{1,0:T(8,128)S(1)} %bitcast.115, f32[256,256]{1,0:T(8,128)S(1)} %get-tuple-element.35.matrix_ref), custom_call_target="tpu_custom_call" | custom-call | tf_op jit(solution)/shard_map/factor/pallas_call | solution.py:184
  142.1 345.0 %conditional.1 = (f32[256,256]{1,0:T(8,128)}, f32[256,256]{1,0:T(8,128)}) conditional(s32[]{:T(128)} %bitcast.34, (bf16[256,256]{1,0:T(8,128)(2,1)S(1)}, s32[32]{0:T(128)S(1)}, bf16[3072,256]{1,0:T(8,128)(2,1)S(1)}) %tuple.82, (f32[256,256]{1,0:T(8,128)}, f32[256,256]{1,0:T(8,128)}) %tuple.19), branch_computations={%region_4.16_spmd, %region_14.17_spmd} | conditional | flops 1815717376 | bytes 57568040 | solution.py:247
  142.1 0.8 dynamic_slice.10
  143.6 2.8 convolution_select_fusion
  146.4 4.5 all-to-all-start
  150.9 71.1 %all-to-all-done = f32[16,192,256]{2,1,0:T(8,128)S(1)} async-done(((f32[16,192,256]{2,1,0:T(8,128)}), f32[16,192,256]{2,1,0:T(8,128)S(1)}, u32[]{:S(2)}, u32[]{:S(2)}) %all-to-all-start) | async-done | bytes 3145760 | tf_op jit(solution)/shard_map/cond/branch_0_fun/all_to_all | solution.py:55
  222.3 45.2 %all_to_all.57 = bf16[16,192,256]{2,1,0:T(8,128)(2,1)S(1)} all-to-all(bf16[16,192,256]{2,1,0:T(8,128)(2,1)S(1)} %broadcast_in_dim.25), channel_id=1, replica_groups=mesh['dp'=32,'feat'=16] {'feat'}, dimensions={0} | all-to-all | bytes 3145728 | tf_op jit(solution)/shard_map/cond/branch_0_fun/all_to_all | solution.py:50
  267.4 0.7 convolution_bitcast_fusion
  268.2 15.7 %all_to_all.62 = f32[32,8,256]{2,1,0:T(8,128)S(1)} all-to-all(f32[32,8,256]{2,1,0:T(8,128)S(1)} %convolution_bitcast_fusion), channel_id=1, replica_groups=mesh['dp'=32,'feat'=16] {'dp'}, dimensions={0} | all-to-all | bytes 524288 | tf_op jit(solution)/shard_map/cond/branch_0_fun/all_to_all | solution.py:55
  284.0 0.7 broadcast_in_dim.26
  284.7 3.9 all-to-all-start.3
  288.5 0.7 reduce_sum.74
  290.0 10.7 %all-to-all-done.3 = f32[32,8,256]{2,1,0:T(8,128)S(1)} async-done(((f32[32,8,256]{2,1,0:T(8,128)}), f32[32,8,256]{2,1,0:T(8,128)S(1)}, u32[]{:S(2)}, u32[]{:S(2)}) %all-to-all-start.3) | async-done | bytes 262176 | tf_op jit(solution)/shard_map/cond/branch_0_fun/all_to_all | solution.py:50
  300.9 0.4 fusion.15
  301.3 16.0 %all_to_all.63 = f32[16,16,256]{2,1,0:T(8,128)S(1)} all-to-all(f32[16,16,256]{2,1,0:T(8,128)S(1)} %bitcast.122), channel_id=1, replica_groups=mesh['dp'=32,'feat'=16] {'feat'}, dimensions={0} | all-to-all | bytes 524288 | tf_op jit(solution)/shard_map/cond/branch_0_fun/all_to_all | solution.py:55
  317.3 0.7 broadcast_in_dim.27
  318.0 4.0 all-to-all-start.5
  322.0 10.9 %all-to-all-done.5 = f32[16,16,256]{2,1,0:T(8,128)S(1)} async-done(((f32[16,16,256]{2,1,0:T(8,128)}), f32[16,16,256]{2,1,0:T(8,128)S(1)}, u32[]{:S(2)}, u32[]{:S(2)}) %all-to-all-start.5) | async-done | bytes 262176 | tf_op jit(solution)/shard_map/cond/branch_0_fun/all_to_all | solution.py:50
  333.1 11.7 %cholesky.130 = f32[128,128]{1,0:T(8,128)S(1)} custom-call(f32[128,128]{1,0:T(8,128)S(1)} %cholesky.194), custom_call_target="Cholesky" | custom-call | tf_op jit(solution)/shard_map/cond/branch_0_fun/jit(cholesky)/cholesky | solution.py:198
  344.8 9.8 %custom-call.13 = f32[1,128,128]{1,2,0:T(8,128)S(1)} custom-call(f32[1,128,128]{2,1,0:T(8,128)S(1)} %get-tuple-element.109), custom_call_target="InvertDiagBlocksLowerTriangular" | custom-call | tf_op jit(solution)/shard_map/cond/branch_0_fun/jit(cholesky)/cholesky | solution.py:198
  355.1 11.7 %cholesky.147 = f32[128,128]{1,0:T(8,128)S(1)} custom-call(f32[128,128]{1,0:T(8,128)S(1)} %convolution_subtract_fusion.3), custom_call_target="Cholesky" | custom-call | tf_op jit(solution)/shard_map/cond/branch_0_fun/jit(cholesky)/cholesky | solution.py:198
  366.9 0.7 compare_reduce_fusion.2
  369.0 4.1 while.4
  369.0 0.7 fusion.72
  369.7 1.3 bitcast_dynamic-update-slice_fusion.4
  371.1 0.7 fusion.72
  371.7 1.3 bitcast_dynamic-update-slice_fusion.4
  373.1 19.7 %custom-call.14 = f32[2,128,128]{1,2,0:T(8,128)S(1)} custom-call(f32[2,128,128]{2,1,0:T(8,128)S(1)} %get-tuple-element.57), custom_call_target="InvertDiagBlocksLowerTriangular" | custom-call | tf_op jit(solution)/shard_map/cond/branch_0_fun/jit(_solve_triangular)/triangular_solve | solution.py:199
  392.8 0.3 fusion.16
  393.3 0.3 fusion.28
  393.7 0.4 fusion
  394.1 14.5 %all_to_all.64 = f32[16,16,256]{2,1,0:T(8,128)S(1)} all-to-all(f32[16,16,256]{2,1,0:T(8,128)S(1)} %bitcast.123), channel_id=1, replica_groups=mesh['dp'=32,'feat'=16] {'feat'}, dimensions={0} | all-to-all | bytes 524288 | tf_op jit(solution)/shard_map/cond/branch_0_fun/all_to_all | solution.py:55
  408.6 14.6 %all_to_all.65 = f32[16,16,256]{2,1,0:T(8,128)S(1)} all-to-all(f32[16,16,256]{2,1,0:T(8,128)S(1)} %broadcast_in_dim.28), channel_id=1, replica_groups=mesh['dp'=32,'feat'=16] {'feat'}, dimensions={0} | all-to-all | bytes 524288 | tf_op jit(solution)/shard_map/cond/branch_0_fun/all_to_all | solution.py:50
  423.4 11.7 %cholesky.164 = f32[128,128]{1,0:T(8,128)S(1)} custom-call(f32[128,128]{1,0:T(8,128)S(1)} %cholesky.197), custom_call_target="Cholesky" | custom-call | tf_op jit(solution)/shard_map/cond/branch_0_fun/jit(cholesky)/cholesky | solution.py:198
  435.2 9.8 %custom-call.15 = f32[1,128,128]{1,2,0:T(8,128)S(1)} custom-call(f32[1,128,128]{2,1,0:T(8,128)S(1)} %get-tuple-element.105), custom_call_target="InvertDiagBlocksLowerTriangular" | custom-call | tf_op jit(solution)/shard_map/cond/branch_0_fun/jit(cholesky)/cholesky | solution.py:198
  445.5 11.7 %cholesky.181 = f32[128,128]{1,0:T(8,128)S(1)} custom-call(f32[128,128]{1,0:T(8,128)S(1)} %convolution_subtract_fusion.2), custom_call_target="Cholesky" | custom-call | tf_op jit(solution)/shard_map/cond/branch_0_fun/jit(cholesky)/cholesky | solution.py:198
  457.2 0.6 compare_reduce_fusion
  457.8 0.7 compare_reduce_fusion.1
  459.8 1.2 fusion.11
  461.1 4.1 while.5
  461.1 0.7 fusion.73
  461.8 1.3 bitcast_dynamic-update-slice_fusion.5
  463.1 0.7 fusion.73
  463.8 1.3 bitcast_dynamic-update-slice_fusion.5
  465.1 19.9 %custom-call.16 = f32[2,128,128]{1,2,0:T(8,128)S(1)} custom-call(f32[2,128,128]{2,1,0:T(8,128)S(1)} %get-tuple-element.58), custom_call_target="InvertDiagBlocksLowerTriangular" | custom-call | tf_op jit(solution)/shard_map/cond/branch_0_fun/jit(_solve_triangular)/triangular_solve | solution.py:199
  486.0 0.8 copy.37
  (63 shorter events, 3.9 us)
Async XLA Ops:
  0.6 13.2 %copy-start = (bf16[3072,256]{1,0:T(8,128)(2,1)S(1)}, bf16[3072,256]{1,0:T(8,128)(2,1)}, u32[]{:S(2)}) copy-start(bf16[3072,256]{1,0:T(8,128)(2,1)} %param.8) | copy-start | bytes 4718596
  0.6 13.2 %copy-start.3 = (bf16[256,256]{1,0:T(8,128)(2,1)S(1)}, bf16[256,256]{1,0:T(8,128)(2,1)}, u32[]{:S(2)}) copy-start(bf16[256,256]{1,0:T(8,128)(2,1)} %basis_ref.1) | copy-start | bytes 393220
  0.6 10.5 %copy-start.4 = (s32[32]{0:T(128)S(1)}, s32[32]{0:T(128)}, u32[]{:S(2)}) copy-start(s32[32]{0:T(128)} %param.9) | copy-start | bytes 388
  2.3 11.9 %collective-permute-start = (f16[8,192,256]{2,1,0:T(8,128)(2,1)S(1)}, f16[8,192,256]{2,1,0:T(8,128)(2,1)}, u32[]{:S(2)}, u32[]{:S(2)}) collective-permute-start(f16[8,192,256]{2,1,0:T(8,128)(2,1)S(1)} %multiply_convert_fusion), channel_id=1, source_target_pairs={{0,1},{1,0},{2,3},{3,2},{4,5},{5,4},{6,7},{7,6},{8,9},{9,8},{10,11... | collective-permute-start | bytes 2359304 | tf_op jit(solution)/shard_map/ppermute | solution.py:31
  98.4 6.2 %collective-permute-start.1 = (f32[16,384]{1,0:T(8,128)S(1)}, f32[16,384]{1,0:T(8,128)S(1)}, u32[]{:S(2)}, u32[]{:S(2)}) collective-permute-start(f32[16,384]{1,0:T(8,128)S(1)} %get-tuple-element.34), channel_id=1, source_target_pairs={{0,1},{1,0},{2,3},{3,2},{4,5},{5,4},{6,7},{7,6},{8,9},{9,8},{10,11... | collective-permute-start | bytes 73736 | tf_op jit(solution)/shard_map/ppermute | solution.py:31
  117.7 11.2 %all-to-all-start.12 = ((f32[8,16,384]{2,1,0:T(8,128)}), f32[8,16,384]{2,1,0:T(8,128)S(1)}, u32[]{:S(2)}, u32[]{:S(2)}) async-start(f32[8,16,384]{2,1,0:T(8,128)} %broadcast_in_dim.39), calls=%async_computation.12 | async-start | bytes 393216 | tf_op jit(solution)/shard_map/all_to_all | solution.py:50
  142.1 4.3 copy-start.1
  146.4 75.5 %all-to-all-start = ((f32[16,192,256]{2,1,0:T(8,128)}), f32[16,192,256]{2,1,0:T(8,128)S(1)}, u32[]{:S(2)}, u32[]{:S(2)}) async-start(f32[16,192,256]{2,1,0:T(8,128)} %bitcast.116), calls=%async_computation | async-start | bytes 6291456 | tf_op jit(solution)/shard_map/cond/branch_0_fun/all_to_all | solution.py:55
  222.3 45.2 %copy-start.2 = (bf16[3072,256]{1,0:T(8,128)(2,1)S(1)}, bf16[3072,256]{1,0:T(8,128)(2,1)}, u32[]{:S(2)}) copy-start(bf16[3072,256]{1,0:T(8,128)(2,1)} %copy-done.1) | copy-start | bytes 4718596 | tf_op jit(solution)/shard_map/cond
  284.7 16.0 %all-to-all-start.3 = ((f32[32,8,256]{2,1,0:T(8,128)}), f32[32,8,256]{2,1,0:T(8,128)S(1)}, u32[]{:S(2)}, u32[]{:S(2)}) async-start(f32[32,8,256]{2,1,0:T(8,128)} %broadcast_in_dim.26), calls=%async_computation.3 | async-start | bytes 524288 | tf_op jit(solution)/shard_map/cond/branch_0_fun/all_to_all | solution.py:50
  318.0 14.9 %all-to-all-start.5 = ((f32[16,16,256]{2,1,0:T(8,128)}), f32[16,16,256]{2,1,0:T(8,128)S(1)}, u32[]{:S(2)}, u32[]{:S(2)}) async-start(f32[16,16,256]{2,1,0:T(8,128)} %broadcast_in_dim.27), calls=%async_computation.5 | async-start | bytes 524288 | tf_op jit(solution)/shard_map/cond/branch_0_fun/all_to_all | solution.py:50

commit v5 on v4

--- a/solution.py
+++ b/solution.py
@@ -17,6 +17,8 @@
 F16 = jnp.float16
 
 LIFT = 16.0
+TERMS = 32768.0
+LIFT_STEP = 4.0
 FLOOR = 1e-4
 CLOSE = 4e-6
 STEPS = 14
@@ -61,28 +63,39 @@
 def sum_images(data, basis, core, beside):
     chips = lax.axis_size("feat") // CORES
     rows, columns = data.shape
-    split = data.reshape(chips, CORES, rows // (chips * CORES), columns)
-
-    def part(which):
-        picked = lax.dynamic_index_in_dim(split, which, 1, False)
+    here = rows // (chips * CORES)
+    split = data.reshape(chips, CORES, here, columns)
+
+    def half(which):
+        return lax.dynamic_index_in_dim(split, which, 1, False)
+
+    def times(left, right):
         return lax.dot_general(
-            picked, basis, (((2,), (0,)), ((), ())), preferred_element_type=F32
+            left, right, (((2,), (0,)), ((), ())), preferred_element_type=F32
         )
 
-    theirs = core_swap((part(1 - core) * LIFT).astype(F16))
-    mine, theirs, beside = lax.optimization_barrier((part(core), theirs, beside))
+    theirs = core_swap(
+        jnp.concatenate([half(1 - core).reshape(chips * here, columns), basis])
+    )
+    mine, theirs, beside = lax.optimization_barrier(
+        (times(half(core), basis), theirs, beside)
+    )
+    rows_there = theirs[: chips * here].reshape(chips, here, columns)
+    pair = mine + times(rows_there, theirs[chips * here :])
     pieces = lax.all_to_all(
-        (mine * LIFT + theirs.astype(F32)).astype(F16),
-        "feat",
-        0,
-        0,
-        axis_index_groups=groups_z(),
+        (pair * LIFT).astype(F16), "feat", 0, 0, axis_index_groups=groups_z()
     )
     return jnp.sum(pieces.astype(F32), axis=0), beside
 
 
-def gram_kernel(place_ref, step_ref, basis_ref, updated_ref, mine_ref, theirs_ref, packed):
-    updated = basis_ref[...].astype(F32) + step_ref[...]
+def gram_kernel(
+    place_ref, counts_ref, step_ref, basis_ref, updated_ref, mine_ref, theirs_ref, packed
+):
+    count = counts_ref[0]
+    for i in range(1, counts_ref.shape[0]):
+        count += counts_ref[i]
+    row_total = jnp.full((1, 1), count * BLOCK, jnp.int32).astype(F32)
+    updated = basis_ref[...].astype(F32) + step_ref[...] * (TERMS / LIFT_STEP) / row_total
     updated_ref[...] = updated
     half = packed.shape[0]
     share = mine_ref.shape[0]
@@ -101,20 +114,21 @@
     theirs_ref[...] = packed[pl.ds(theirs, share), :]
 
 
-def gram_share(place, step, basis):
+def gram_share(place, counts, step, basis):
     rank = basis.shape[1]
     half = rank // 2
     share = jax.ShapeDtypeStruct((half // (X * CORES), rank + half), F32)
     vmem = pl.BlockSpec(memory_space=pltpu.VMEM)
+    smem = pl.BlockSpec(memory_space=pltpu.SMEM)
     return pl.pallas_call(
         gram_kernel,
         out_shape=(jax.ShapeDtypeStruct(basis.shape, F32), share, share),
-        in_specs=[pl.BlockSpec(memory_space=pltpu.SMEM), vmem, vmem],
+        in_specs=[smem, smem, vmem, vmem],
         out_specs=(vmem, vmem, vmem),
         scratch_shapes=[pltpu.VMEM((half, rank + half), F32)],
         compiler_params=pltpu.CompilerParams(vmem_limit_bytes=32 * 1024 * 1024),
         name="gram_share",
-    )(place, step, basis)
+    )(place, counts, step, basis)
 
 
 def sum_gram(mine, theirs):
@@ -135,6 +149,10 @@
         lax.dot_general, dimension_numbers=dims, preferred_element_type=F32
     )
     return dot(left[0], right[0]) + (dot(left[0], right[1]) + dot(left[1], right[0]))
+
+
+def coarse(left, right, dims):
+    return lax.dot_general(left[0], right[0], dims, preferred_element_type=F32)
 
 
 def factor_kernel(packed_ref, matrix_ref, basis_ref, upper_ref, done_ref, inverse):
@@ -155,15 +173,15 @@
     unit_parts = halves(unit)
     inverse[...] = eye - (unit - eye) * keep
 
-    def improve():
+    def improve(multiply=product):
         now = inverse[...]
         parts = halves(now)
-        moved = product(parts, unit_parts, PLAIN)
-        excess = product(halves(moved), parts, OUTER) - eye
-        inverse[...] = now - product(halves(excess * keep), parts, PLAIN)
+        moved = multiply(parts, unit_parts, PLAIN)
+        excess = multiply(halves(moved), parts, OUTER) - eye
+        inverse[...] = now - multiply(halves(excess * keep), parts, PLAIN)
         return jnp.sum(excess * excess)
 
-    improve()
+    improve(coarse)
     _, error = lax.while_loop(
         lambda state: jnp.logical_and(state[0] < STEPS, jnp.logical_not(state[1] < CLOSE)),
         lambda state: (state[0] + 1, improve()),
@@ -228,21 +246,20 @@
     active = lax.dynamic_index_in_dim(block_counts, dp, 0, False)
     row_ids = feat * here + lax.broadcasted_iota(jnp.int32, (here, 1), 0)
     valid = jnp.where(row_ids < active * BLOCK, 1.0, 0.0)
-    row_total = (jnp.sum(block_counts) * BLOCK).astype(F32)
-    beside = (valid, row_total, jnp.stack([dp % X, core]))
+    beside = (valid, jnp.stack([dp % X, core]))
     images, beside = sum_images(data, basis, core, beside)
-    valid, row_total, place = beside
-    images = (images * valid).astype(F16)
+    valid, place = beside
+    images = lax.reduce_precision(images * valid, 8, 7).astype(F16)
     images = lax.all_gather(images, "feat", tiled=True).astype(BF16)
 
     terms = lax.dot_general(
         data, images, (((0,), (0,)), ((), ())), preferred_element_type=F32
     )
-    terms = (terms / row_total).astype(F16)
+    terms = (terms / TERMS).astype(F16)
     pieces = lax.all_to_all(terms.reshape(dp_size, columns // dp_size, rank), "dp", 0, 0)
-    piece = jnp.sum(pieces.astype(F32), axis=0) / LIFT
-    step = spread(piece, "dp", None, dp_size).reshape(columns, rank)
-    updated, mine, theirs = gram_share(place, step, basis)
+    piece = (jnp.sum(pieces.astype(F32), axis=0) * (LIFT_STEP / LIFT)).astype(F16)
+    step = spread(piece, "dp", None, dp_size).reshape(columns, rank).astype(F32)
+    updated, mine, theirs = gram_share(place, block_counts, step, basis)
     basis_scaled, upper, done = factor(sum_gram(mine, theirs), updated)
     return lax.cond(
         done[0] == 1,

time: 497 us -> 495 us (level)
  transfers between devices with their start and end apart: 6 -> 6, of which waited for: 5 -> 6; matrix products, arithmetic and copies ran while one was open for 1% -> 0% of each run, Pallas kernels for 0% -> 0%
where the time goes in v5:
time: 495 us; the launch traced here: 487 us
  blocking collectives  197 us (40%)
  other arithmetic  111 us (22%)
  waiting for transfers between devices  101 us (20%)
  starting transfers between devices  31 us (6%)
  local copies, waits for them, and re-layouts  15.7 us (3%)
  Pallas kernels  13.1 us (3%)
  matrix products  10.7 us (2%)
    all_to_all x4, blocking collectives, spread(): return lax.all_to_all(copies, axis, 0, 0, axis_index_groups=groups)  84.7 us
    all_to_all x1, waiting for transfers between devices, total(): lax.all_to_all(value.reshape((size, value.shape[0] // size) + value.shape...  71.1 us
    another operation x13, other arithmetic, orthonormal(): lower = jnp.linalg.cholesky(gram_total)  68.7 us
    all_to_all x3, blocking collectives, total(): lax.all_to_all(value.reshape((size, value.shape[0] // size) + value.shape...  45.2 us
    another operation x5, other arithmetic, orthonormal(): solved = jax.scipy.linalg.solve_triangular(lower, matrix.T, lower=True)  39.6 us
    all_to_all x3, waiting for transfers between devices, spread(): return lax.all_to_all(copies, axis, 0, 0, axis_index_groups=groups)  28.1 us
    all_to_all x1, blocking collectives, sum_images(): lax.all_to_all((pair * LIFT).astype(F16), 'feat', 0, 0, axis_index_groups...  26.7 us
    all_gather x1, blocking collectives, on_device(): images = lax.all_gather(images, 'feat', tiled=True).astype(BF16)  21.1 us
  transfers between devices with their start and end apart: 6, of which 6 were waited for; matrix products, arithmetic and copies ran while one was open for 0% of the time, Pallas kernels for 0%

profile of v5, /device:TPU:1, one launch (start us, length us, event | category | flops | bytes accessed | tf_op | source)
XLA Modules:
  0.0 487.0 jit_solution(9991636040855197881)
XLA Ops:
  0.7 1.3 constant_dynamic-slice_fusion.2
  2.0 1.0 pad_maximum_fusion
  3.0 8.8 %collective-permute-start = (bf16[1792,256]{1,0:T(8,128)(2,1)}, bf16[1792,256]{1,0:T(8,128)(2,1)}, u32[]{:S(2)}, u32[]{:S(2)}) collective-permute-start(bf16[1792,256]{1,0:T(8,128)(2,1)} %pad_maximum_fusion), channel_id=1, source_target_pairs={{0,1},{1,0},{2,3},{3,2},{4,5},{5,4},{6,7},{7,6},{8,9},{9,8},{10,11... | collective-permute-start | bytes 2752520 | tf_op jit(solution)/shard_map/ppermute | solution.py:33
  11.8 0.6 dynamic_slice.16
  13.1 0.4 fusion.51
  13.4 0.8 collective-permute-done
  14.2 1.2 slice.39
  15.4 1.3 fusion.54
  16.9 26.7 %all_to_all.58 = f16[8,192,256]{2,1,0:T(8,128)(2,1)S(1)} all-to-all(f16[8,192,256]{2,1,0:T(8,128)(2,1)S(1)} %multiply_convert_fusion), channel_id=1, replica_groups={{0,2,4,6,8,10,12,14},{1,3,5,7,9,11,13,15},{16,18,20,22,24,26,28,30},{17..., dimensions={0} | all-to-all | bytes 1572864 | tf_op jit(solution)/shard_map/all_to_all | solution.py:85
  43.8 21.1 %all-gather.1 = f16[3072,256]{1,0:T(8,128)(2,1)S(1)} all-gather(f16[192,256]{1,0:T(8,128)(2,1)S(1)} %reduce-precision_convert_fusion), channel_id=1, replica_groups=mesh['dp'=32,'feat'=16] {'feat'}, dimensions={0}, use_global_device_ids=true | all-gather | bytes 1671168 | tf_op jit(solution)/shard_map/all_gather | solution.py:253
  65.0 0.8 fusion.48
  65.8 19.2 %all_to_all.59 = f16[32,8,256]{2,1,0:T(8,128)(2,1)S(1)} all-to-all(f16[32,8,256]{2,1,0:T(8,128)(2,1)S(1)} %fusion.48), channel_id=1, replica_groups=mesh['dp'=32,'feat'=16] {'dp'}, dimensions={0} | all-to-all | bytes 262144 | tf_op jit(solution)/shard_map/all_to_all | solution.py:259
  85.1 12.7 %all_to_all.60 = f16[32,8,256]{2,1,0:T(8,128)(2,1)S(1)} all-to-all(f16[32,8,256]{2,1,0:T(8,128)(2,1)S(1)} %broadcast_in_dim.36), channel_id=1, replica_groups=mesh['dp'=32,'feat'=16] {'dp'}, dimensions={0} | all-to-all | bytes 262144 | tf_op jit(solution)/shard_map/all_to_all | solution.py:52
  97.8 1.0 gram_share.1
  98.8 4.7 collective-permute-start.1
  103.5 0.8 collective-permute-done.1
  104.4 12.3 %all_to_all.61 = f32[8,16,384]{2,1,0:T(8,128)S(1)} all-to-all(f32[8,16,384]{2,1,0:T(8,128)S(1)} %broadcast_in_dim.38), channel_id=1, replica_groups={{0,2,4,6,8,10,12,14},{1,3,5,7,9,11,13,15},{16,18,20,22,24,26,28,30},{17..., dimensions={0} | all-to-all | bytes 393216 | tf_op jit(solution)/shard_map/all_to_all | solution.py:52
  116.7 0.7 broadcast_in_dim.39
  117.4 5.3 %all-to-all-start.12 = ((f32[8,16,384]{2,1,0:T(8,128)}), f32[8,16,384]{2,1,0:T(8,128)S(1)}, u32[]{:S(2)}, u32[]{:S(2)}) async-start(f32[8,16,384]{2,1,0:T(8,128)} %broadcast_in_dim.39), calls=%async_computation.12 | async-start | bytes 393216 | tf_op jit(solution)/shard_map/all_to_all | solution.py:52
  122.6 5.9 %all-to-all-done.12 = f32[8,16,384]{2,1,0:T(8,128)S(1)} async-done(((f32[8,16,384]{2,1,0:T(8,128)}), f32[8,16,384]{2,1,0:T(8,128)S(1)}, u32[]{:S(2)}, u32[]{:S(2)}) %all-to-all-start.12) | async-done | bytes 196640 | tf_op jit(solution)/shard_map/all_to_all | solution.py:52
  128.5 12.1 %factor.1 = (f32[256,256]{1,0:T(8,128)}, f32[256,256]{1,0:T(8,128)}, s32[1]{0:T(128)}) custom-call(f32[128,384]{1,0:T(8,128)S(1)} %bitcast.117, f32[256,256]{1,0:T(8,128)S(1)} %get-tuple-element.33.matrix_ref), custom_call_target="tpu_custom_call" | custom-call | tf_op jit(solution)/shard_map/factor/pallas_call | solution.py:202
  141.4 344.6 %conditional.1 = (f32[256,256]{1,0:T(8,128)}, f32[256,256]{1,0:T(8,128)}) conditional(s32[]{:T(128)} %bitcast.36, (bf16[256,256]{1,0:T(8,128)(2,1)S(1)}, s32[32]{0:T(128)S(1)}, bf16[3072,256]{1,0:T(8,128)(2,1)S(1)}) %tuple.82, (f32[256,256]{1,0:T(8,128)}, f32[256,256]{1,0:T(8,128)}) %tuple.19), branch_computations={%region_3.15_spmd, %region_13.16_spmd} | conditional | flops 1815717376 | bytes 57568040 | solution.py:264
  141.4 0.8 dynamic_slice.10
  142.9 2.8 convolution_select_fusion
  145.7 4.5 all-to-all-start
  150.1 71.1 %all-to-all-done = f32[16,192,256]{2,1,0:T(8,128)S(1)} async-done(((f32[16,192,256]{2,1,0:T(8,128)}), f32[16,192,256]{2,1,0:T(8,128)S(1)}, u32[]{:S(2)}, u32[]{:S(2)}) %all-to-all-start) | async-done | bytes 3145760 | tf_op jit(solution)/shard_map/cond/branch_0_fun/all_to_all | solution.py:57
  221.6 45.2 %all_to_all.57 = bf16[16,192,256]{2,1,0:T(8,128)(2,1)S(1)} all-to-all(bf16[16,192,256]{2,1,0:T(8,128)(2,1)S(1)} %broadcast_in_dim.25), channel_id=1, replica_groups=mesh['dp'=32,'feat'=16] {'feat'}, dimensions={0} | all-to-all | bytes 3145728 | tf_op jit(solution)/shard_map/cond/branch_0_fun/all_to_all | solution.py:52
  266.7 0.7 convolution_bitcast_fusion
  267.5 15.7 %all_to_all.62 = f32[32,8,256]{2,1,0:T(8,128)S(1)} all-to-all(f32[32,8,256]{2,1,0:T(8,128)S(1)} %convolution_bitcast_fusion), channel_id=1, replica_groups=mesh['dp'=32,'feat'=16] {'dp'}, dimensions={0} | all-to-all | bytes 524288 | tf_op jit(solution)/shard_map/cond/branch_0_fun/all_to_all | solution.py:57
  283.2 0.7 broadcast_in_dim.26
  283.9 3.9 all-to-all-start.3
  287.8 0.7 reduce_sum.66
  289.2 11.3 %all-to-all-done.3 = f32[32,8,256]{2,1,0:T(8,128)S(1)} async-done(((f32[32,8,256]{2,1,0:T(8,128)}), f32[32,8,256]{2,1,0:T(8,128)S(1)}, u32[]{:S(2)}, u32[]{:S(2)}) %all-to-all-start.3) | async-done | bytes 262176 | tf_op jit(solution)/shard_map/cond/branch_0_fun/all_to_all | solution.py:52
  300.7 0.4 fusion.15
  301.1 14.9 %all_to_all.63 = f32[16,16,256]{2,1,0:T(8,128)S(1)} all-to-all(f32[16,16,256]{2,1,0:T(8,128)S(1)} %bitcast.126), channel_id=1, replica_groups=mesh['dp'=32,'feat'=16] {'feat'}, dimensions={0} | all-to-all | bytes 524288 | tf_op jit(solution)/shard_map/cond/branch_0_fun/all_to_all | solution.py:57
  316.1 0.7 broadcast_in_dim.27
  316.8 4.0 all-to-all-start.5
  320.8 10.9 %all-to-all-done.5 = f32[16,16,256]{2,1,0:T(8,128)S(1)} async-done(((f32[16,16,256]{2,1,0:T(8,128)}), f32[16,16,256]{2,1,0:T(8,128)S(1)}, u32[]{:S(2)}, u32[]{:S(2)}) %all-to-all-start.5) | async-done | bytes 262176 | tf_op jit(solution)/shard_map/cond/branch_0_fun/all_to_all | solution.py:52
  331.9 11.7 %cholesky.130 = f32[128,128]{1,0:T(8,128)S(1)} custom-call(f32[128,128]{1,0:T(8,128)S(1)} %cholesky.194), custom_call_target="Cholesky" | custom-call | tf_op jit(solution)/shard_map/cond/branch_0_fun/jit(cholesky)/cholesky | solution.py:216
  343.6 9.8 %custom-call.13 = f32[1,128,128]{1,2,0:T(8,128)S(1)} custom-call(f32[1,128,128]{2,1,0:T(8,128)S(1)} %get-tuple-element.107), custom_call_target="InvertDiagBlocksLowerTriangular" | custom-call | tf_op jit(solution)/shard_map/cond/branch_0_fun/jit(cholesky)/cholesky | solution.py:216
  354.0 11.7 %cholesky.147 = f32[128,128]{1,0:T(8,128)S(1)} custom-call(f32[128,128]{1,0:T(8,128)S(1)} %convolution_subtract_fusion.3), custom_call_target="Cholesky" | custom-call | tf_op jit(solution)/shard_map/cond/branch_0_fun/jit(cholesky)/cholesky | solution.py:216
  365.7 0.7 compare_reduce_fusion.2
  367.8 4.1 while.4
  367.8 0.7 fusion.78
  368.5 1.3 bitcast_dynamic-update-slice_fusion.4
  369.9 0.7 fusion.78
  370.5 1.3 bitcast_dynamic-update-slice_fusion.4
  371.9 19.7 %custom-call.14 = f32[2,128,128]{1,2,0:T(8,128)S(1)} custom-call(f32[2,128,128]{2,1,0:T(8,128)S(1)} %get-tuple-element.55), custom_call_target="InvertDiagBlocksLowerTriangular" | custom-call | tf_op jit(solution)/shard_map/cond/branch_0_fun/jit(_solve_triangular)/triangular_solve | solution.py:217
  392.5 0.4 fusion
  392.9 14.6 %all_to_all.64 = f32[16,16,256]{2,1,0:T(8,128)S(1)} all-to-all(f32[16,16,256]{2,1,0:T(8,128)S(1)} %bitcast.127), channel_id=1, replica_groups=mesh['dp'=32,'feat'=16] {'feat'}, dimensions={0} | all-to-all | bytes 524288 | tf_op jit(solution)/shard_map/cond/branch_0_fun/all_to_all | solution.py:57
  407.5 14.6 %all_to_all.65 = f32[16,16,256]{2,1,0:T(8,128)S(1)} all-to-all(f32[16,16,256]{2,1,0:T(8,128)S(1)} %broadcast_in_dim.28), channel_id=1, replica_groups=mesh['dp'=32,'feat'=16] {'feat'}, dimensions={0} | all-to-all | bytes 524288 | tf_op jit(solution)/shard_map/cond/branch_0_fun/all_to_all | solution.py:52
  422.3 11.7 %cholesky.164 = f32[128,128]{1,0:T(8,128)S(1)} custom-call(f32[128,128]{1,0:T(8,128)S(1)} %cholesky.197), custom_call_target="Cholesky" | custom-call | tf_op jit(solution)/shard_map/cond/branch_0_fun/jit(cholesky)/cholesky | solution.py:216
  434.0 9.8 %custom-call.15 = f32[1,128,128]{1,2,0:T(8,128)S(1)} custom-call(f32[1,128,128]{2,1,0:T(8,128)S(1)} %get-tuple-element.103), custom_call_target="InvertDiagBlocksLowerTriangular" | custom-call | tf_op jit(solution)/shard_map/cond/branch_0_fun/jit(cholesky)/cholesky | solution.py:216
  444.3 11.7 %cholesky.181 = f32[128,128]{1,0:T(8,128)S(1)} custom-call(f32[128,128]{1,0:T(8,128)S(1)} %convolution_subtract_fusion.2), custom_call_target="Cholesky" | custom-call | tf_op jit(solution)/shard_map/cond/branch_0_fun/jit(cholesky)/cholesky | solution.py:216
  456.1 0.6 compare_reduce_fusion
  456.7 0.7 compare_reduce_fusion.1
  458.7 1.2 fusion.11
  459.9 4.1 while.5
  460.0 0.7 fusion.79
  460.6 1.3 bitcast_dynamic-update-slice_fusion.5
  462.0 0.7 fusion.79
  462.7 1.3 bitcast_dynamic-update-slice_fusion.5
  464.0 19.9 %custom-call.16 = f32[2,128,128]{1,2,0:T(8,128)S(1)} custom-call(f32[2,128,128]{2,1,0:T(8,128)S(1)} %get-tuple-element.56), custom_call_target="InvertDiagBlocksLowerTriangular" | custom-call | tf_op jit(solution)/shard_map/cond/branch_0_fun/jit(_solve_triangular)/triangular_solve | solution.py:217
  484.8 0.8 copy.35
  (66 shorter events, 4.8 us)
Async XLA Ops:
  0.6 1.4 copy-start.3
  0.7 11.1 %copy-start.4 = (s32[32]{0:T(128)S(1)}, s32[32]{0:T(128)}, u32[]{:S(2)}) copy-start(s32[32]{0:T(128)} %counts_ref.1) | copy-start | bytes 388
  0.7 12.4 %copy-start = (bf16[3072,256]{1,0:T(8,128)(2,1)S(1)}, bf16[3072,256]{1,0:T(8,128)(2,1)}, u32[]{:S(2)}) copy-start(bf16[3072,256]{1,0:T(8,128)(2,1)} %param.8) | copy-start | bytes 4718596
  3.0 11.2 %collective-permute-start = (bf16[1792,256]{1,0:T(8,128)(2,1)}, bf16[1792,256]{1,0:T(8,128)(2,1)}, u32[]{:S(2)}, u32[]{:S(2)}) collective-permute-start(bf16[1792,256]{1,0:T(8,128)(2,1)} %pad_maximum_fusion), channel_id=1, source_target_pairs={{0,1},{1,0},{2,3},{3,2},{4,5},{5,4},{6,7},{7,6},{8,9},{9,8},{10,11... | collective-permute-start | bytes 2752520 | tf_op jit(solution)/shard_map/ppermute | solution.py:33
  98.8 5.5 %collective-permute-start.1 = (f32[16,384]{1,0:T(8,128)S(1)}, f32[16,384]{1,0:T(8,128)S(1)}, u32[]{:S(2)}, u32[]{:S(2)}) collective-permute-start(f32[16,384]{1,0:T(8,128)S(1)} %get-tuple-element.32), channel_id=1, source_target_pairs={{0,1},{1,0},{2,3},{3,2},{4,5},{5,4},{6,7},{7,6},{8,9},{9,8},{10,11... | collective-permute-start | bytes 73736 | tf_op jit(solution)/shard_map/ppermute | solution.py:33
  117.4 11.2 %all-to-all-start.12 = ((f32[8,16,384]{2,1,0:T(8,128)}), f32[8,16,384]{2,1,0:T(8,128)S(1)}, u32[]{:S(2)}, u32[]{:S(2)}) async-start(f32[8,16,384]{2,1,0:T(8,128)} %broadcast_in_dim.39), calls=%async_computation.12 | async-start | bytes 393216 | tf_op jit(solution)/shard_map/all_to_all | solution.py:52
  141.4 4.3 copy-start.1
  145.7 75.5 %all-to-all-start = ((f32[16,192,256]{2,1,0:T(8,128)}), f32[16,192,256]{2,1,0:T(8,128)S(1)}, u32[]{:S(2)}, u32[]{:S(2)}) async-start(f32[16,192,256]{2,1,0:T(8,128)} %bitcast.118), calls=%async_computation | async-start | bytes 6291456 | tf_op jit(solution)/shard_map/cond/branch_0_fun/all_to_all | solution.py:57
  221.5 45.2 %copy-start.2 = (bf16[3072,256]{1,0:T(8,128)(2,1)S(1)}, bf16[3072,256]{1,0:T(8,128)(2,1)}, u32[]{:S(2)}) copy-start(bf16[3072,256]{1,0:T(8,128)(2,1)} %copy-done.1) | copy-start | bytes 4718596 | tf_op jit(solution)/shard_map/cond
  283.9 16.6 %all-to-all-start.3 = ((f32[32,8,256]{2,1,0:T(8,128)}), f32[32,8,256]{2,1,0:T(8,128)S(1)}, u32[]{:S(2)}, u32[]{:S(2)}) async-start(f32[32,8,256]{2,1,0:T(8,128)} %broadcast_in_dim.26), calls=%async_computation.3 | async-start | bytes 524288 | tf_op jit(solution)/shard_map/cond/branch_0_fun/all_to_all | solution.py:52
  316.8 14.9 %all-to-all-start.5 = ((f32[16,16,256]{2,1,0:T(8,128)}), f32[16,16,256]{2,1,0:T(8,128)S(1)}, u32[]{:S(2)}, u32[]{:S(2)}) async-start(f32[16,16,256]{2,1,0:T(8,128)} %broadcast_in_dim.27), calls=%async_computation.5 | async-start | bytes 524288 | tf_op jit(solution)/shard_map/cond/branch_0_fun/all_to_all | solution.py:52

commit v6 on v5

--- a/solution.py
+++ b/solution.py
@@ -74,14 +74,15 @@
             left, right, (((2,), (0,)), ((), ())), preferred_element_type=F32
         )
 
+    whole = times(split.reshape(chips, CORES * here, columns), basis)
+    whole = whole.reshape(chips, CORES, here, -1)
     theirs = core_swap(
-        jnp.concatenate([half(1 - core).reshape(chips * here, columns), basis])
+        (lax.dynamic_index_in_dim(whole, 1 - core, 1, False) * LIFT).astype(F16)
     )
     mine, theirs, beside = lax.optimization_barrier(
-        (times(half(core), basis), theirs, beside)
-    )
-    rows_there = theirs[: chips * here].reshape(chips, here, columns)
-    pair = mine + times(rows_there, theirs[chips * here :])
+        (lax.dynamic_index_in_dim(whole, core, 1, False), theirs, beside)
+    )
+    pair = mine + theirs.astype(F32) / LIFT
     pieces = lax.all_to_all(
         (pair * LIFT).astype(F16), "feat", 0, 0, axis_index_groups=groups_z()
     )
@@ -260,7 +261,10 @@
     piece = (jnp.sum(pieces.astype(F32), axis=0) * (LIFT_STEP / LIFT)).astype(F16)
     step = spread(piece, "dp", None, dp_size).reshape(columns, rank).astype(F32)
     updated, mine, theirs = gram_share(place, block_counts, step, basis)
-    basis_scaled, upper, done = factor(sum_gram(mine, theirs), updated)
+    gram, data, block_counts, basis = lax.optimization_barrier(
+        (sum_gram(mine, theirs), data, block_counts, basis)
+    )
+    basis_scaled, upper, done = factor(gram, updated)
     return lax.cond(
         done[0] == 1,
         lambda: (basis_scaled, upper),

time: 495 us -> 491 us (level)
  blocking collectives: 197 us -> 207 us
  waiting for transfers between devices: 101 us -> 94.7 us
  starting transfers between devices: 31 us -> 25.8 us
    all_to_all x4 -> x5, blocking collectives: 84.7 us -> 95 us  [spread(): return lax.all_to_all(copies, axis, 0, 0, axis_index_groups=groups)]
    all_to_all x3 -> x2, waiting for transfers between devices: 28.1 us -> 22.3 us  [spread(): return lax.all_to_all(copies, axis, 0, 0, axis_index_groups=groups)]
    all_to_all x3 -> x2, starting transfers between devices: 13.1 us -> 7.82 us  [spread(): return lax.all_to_all(copies, axis, 0, 0, axis_index_groups=groups)]
  transfers between devices with their start and end apart: 6 -> 5, of which waited for: 6 -> 5; matrix products, arithmetic and copies ran while one was open for 0% -> 0% of each run, Pallas kernels for 0% -> 0%
where the time goes in v6:
time: 491 us; the launch traced here: 483 us
  blocking collectives  207 us (42%)
  other arithmetic  110 us (22%)
  waiting for transfers between devices  94.7 us (19%)
  starting transfers between devices  25.8 us (5%)
  Pallas kernels  13.1 us (3%)
  local copies, waits for them, and re-layouts  12.6 us (3%)
  matrix products  11.1 us (2%)
    all_to_all x5, blocking collectives, spread(): return lax.all_to_all(copies, axis, 0, 0, axis_index_groups=groups)  95 us
    all_to_all x1, waiting for transfers between devices, total(): lax.all_to_all(value.reshape((size, value.shape[0] // size) + value.shape...  71.1 us
    another operation x13, other arithmetic, orthonormal(): lower = jnp.linalg.cholesky(gram_total)  68.7 us
    all_to_all x3, blocking collectives, total(): lax.all_to_all(value.reshape((size, value.shape[0] // size) + value.shape...  45.1 us
    another operation x5, other arithmetic, orthonormal(): solved = jax.scipy.linalg.solve_triangular(lower, matrix.T, lower=True)  39.6 us
    all_to_all x1, blocking collectives, sum_images(): lax.all_to_all((pair * LIFT).astype(F16), 'feat', 0, 0, axis_index_groups...  26.8 us
    all_to_all x2, waiting for transfers between devices, spread(): return lax.all_to_all(copies, axis, 0, 0, axis_index_groups=groups)  22.3 us
    all_gather x1, blocking collectives, on_device(): images = lax.all_gather(images, 'feat', tiled=True).astype(BF16)  21.1 us
  transfers between devices with their start and end apart: 5, of which 5 were waited for; matrix products, arithmetic and copies ran while one was open for 0% of the time, Pallas kernels for 0%

profile of v6, /device:TPU:1, one launch (start us, length us, event | category | flops | bytes accessed | tf_op | source)
XLA Modules:
  0.0 482.6 jit_solution(12878845755305546096)
XLA Ops:
  0.7 2.0 fusion.52
  2.6 0.3 fusion.51
  2.9 8.8 %collective-permute-start = (f16[8,192,256]{2,1,0:T(8,128)(2,1)S(1)}, f16[8,192,256]{2,1,0:T(8,128)(2,1)S(1)}, u32[]{:S(2)}, u32[]{:S(2)}) collective-permute-start(f16[8,192,256]{2,1,0:T(8,128)(2,1)S(1)} %get-tuple-element.122), channel_id=1, source_target_pairs={{0,1},{1,0},{2,3},{3,2},{4,5},{5,4},{6,7},{7,6},{8,9},{9,8},{10,11... | collective-permute-start | bytes 2359304 | tf_op jit(solution)/shard_map/ppermute | solution.py:33
  11.8 0.7 dynamic_slice.16
  13.2 0.4 collective-permute-done
  13.6 0.3 multiply_convert_fusion
  13.9 26.8 %all_to_all.58 = f16[8,192,256]{2,1,0:T(8,128)(2,1)S(1)} all-to-all(f16[8,192,256]{2,1,0:T(8,128)(2,1)S(1)} %multiply_convert_fusion), channel_id=1, replica_groups={{0,2,4,6,8,10,12,14},{1,3,5,7,9,11,13,15},{16,18,20,22,24,26,28,30},{17..., dimensions={0} | all-to-all | bytes 1572864 | tf_op jit(solution)/shard_map/all_to_all | solution.py:86
  40.9 21.1 %all-gather.1 = f16[3072,256]{1,0:T(8,128)(2,1)S(1)} all-gather(f16[192,256]{1,0:T(8,128)(2,1)S(1)} %reduce-precision_convert_fusion), channel_id=1, replica_groups=mesh['dp'=32,'feat'=16] {'feat'}, dimensions={0}, use_global_device_ids=true | all-gather | bytes 1671168 | tf_op jit(solution)/shard_map/all_gather | solution.py:254
  62.0 0.8 fusion.48
  62.9 19.3 %all_to_all.59 = f16[32,8,256]{2,1,0:T(8,128)(2,1)S(1)} all-to-all(f16[32,8,256]{2,1,0:T(8,128)(2,1)S(1)} %fusion.48), channel_id=1, replica_groups=mesh['dp'=32,'feat'=16] {'dp'}, dimensions={0} | all-to-all | bytes 262144 | tf_op jit(solution)/shard_map/all_to_all | solution.py:260
  82.2 12.7 %all_to_all.60 = f16[32,8,256]{2,1,0:T(8,128)(2,1)S(1)} all-to-all(f16[32,8,256]{2,1,0:T(8,128)(2,1)S(1)} %broadcast_in_dim.36), channel_id=1, replica_groups=mesh['dp'=32,'feat'=16] {'dp'}, dimensions={0} | all-to-all | bytes 262144 | tf_op jit(solution)/shard_map/all_to_all | solution.py:52
  94.9 1.0 gram_share.1
  95.9 4.7 collective-permute-start.1
  100.6 0.8 collective-permute-done.1
  101.5 12.3 %all_to_all.61 = f32[8,16,384]{2,1,0:T(8,128)S(1)} all-to-all(f32[8,16,384]{2,1,0:T(8,128)S(1)} %broadcast_in_dim.38), channel_id=1, replica_groups={{0,2,4,6,8,10,12,14},{1,3,5,7,9,11,13,15},{16,18,20,22,24,26,28,30},{17..., dimensions={0} | all-to-all | bytes 393216 | tf_op jit(solution)/shard_map/all_to_all | solution.py:52
  113.9 10.3 %all_to_all.62 = f32[8,16,384]{2,1,0:T(8,128)S(1)} all-to-all(f32[8,16,384]{2,1,0:T(8,128)S(1)} %broadcast_in_dim.39), channel_id=1, replica_groups={{0,1,16,17,32,33,48,49},{2,3,18,19,34,35,50,51},{4,5,20,21,36,37,52,53}..., dimensions={0} | all-to-all | bytes 393216 | tf_op jit(solution)/shard_map/all_to_all | solution.py:52
  124.2 12.1 %factor.1 = (f32[256,256]{1,0:T(8,128)}, f32[256,256]{1,0:T(8,128)}, s32[1]{0:T(128)}) custom-call(f32[128,384]{1,0:T(8,128)S(1)} %bitcast.111, f32[256,256]{1,0:T(8,128)S(1)} %get-tuple-element.38.matrix_ref), custom_call_target="tpu_custom_call" | custom-call | tf_op jit(solution)/shard_map/factor/pallas_call | solution.py:203
  137.0 344.6 %conditional.1 = (f32[256,256]{1,0:T(8,128)}, f32[256,256]{1,0:T(8,128)}) conditional(s32[]{:T(128)} %bitcast.35, (bf16[256,256]{1,0:T(8,128)(2,1)S(1)}, s32[32]{0:T(128)S(1)}, bf16[3072,256]{1,0:T(8,128)(2,1)S(1)}) %tuple.85, (f32[256,256]{1,0:T(8,128)}, f32[256,256]{1,0:T(8,128)}) %tuple.21), branch_computations={%region_3.15_spmd, %region_13.16_spmd} | conditional | flops 1815717376 | bytes 57568040 | solution.py:268
  137.0 0.8 dynamic_slice.10
  138.5 2.8 convolution_select_fusion
  141.3 4.5 all-to-all-start
  145.8 71.1 %all-to-all-done = f32[16,192,256]{2,1,0:T(8,128)S(1)} async-done(((f32[16,192,256]{2,1,0:T(8,128)}), f32[16,192,256]{2,1,0:T(8,128)S(1)}, u32[]{:S(2)}, u32[]{:S(2)}) %all-to-all-start) | async-done | bytes 3145760 | tf_op jit(solution)/shard_map/cond/branch_0_fun/all_to_all | solution.py:57
  217.2 45.2 %all_to_all.57 = bf16[16,192,256]{2,1,0:T(8,128)(2,1)S(1)} all-to-all(bf16[16,192,256]{2,1,0:T(8,128)(2,1)S(1)} %broadcast_in_dim.25), channel_id=1, replica_groups=mesh['dp'=32,'feat'=16] {'feat'}, dimensions={0} | all-to-all | bytes 3145728 | tf_op jit(solution)/shard_map/cond/branch_0_fun/all_to_all | solution.py:52
  262.4 0.7 convolution_bitcast_fusion
  263.1 15.7 %all_to_all.63 = f32[32,8,256]{2,1,0:T(8,128)S(1)} all-to-all(f32[32,8,256]{2,1,0:T(8,128)S(1)} %convolution_bitcast_fusion), channel_id=1, replica_groups=mesh['dp'=32,'feat'=16] {'dp'}, dimensions={0} | all-to-all | bytes 524288 | tf_op jit(solution)/shard_map/cond/branch_0_fun/all_to_all | solution.py:57
  278.8 0.7 broadcast_in_dim.26
  279.5 3.9 all-to-all-start.3
  283.4 0.7 reduce_sum.66
  284.8 11.3 %all-to-all-done.3 = f32[32,8,256]{2,1,0:T(8,128)S(1)} async-done(((f32[32,8,256]{2,1,0:T(8,128)}), f32[32,8,256]{2,1,0:T(8,128)S(1)}, u32[]{:S(2)}, u32[]{:S(2)}) %all-to-all-start.3) | async-done | bytes 262176 | tf_op jit(solution)/shard_map/cond/branch_0_fun/all_to_all | solution.py:52
  296.3 0.4 fusion.15
  296.7 14.9 %all_to_all.64 = f32[16,16,256]{2,1,0:T(8,128)S(1)} all-to-all(f32[16,16,256]{2,1,0:T(8,128)S(1)} %bitcast.117), channel_id=1, replica_groups=mesh['dp'=32,'feat'=16] {'feat'}, dimensions={0} | all-to-all | bytes 524288 | tf_op jit(solution)/shard_map/cond/branch_0_fun/all_to_all | solution.py:57
  311.7 0.7 broadcast_in_dim.27
  312.4 4.0 all-to-all-start.5
  316.4 11.0 %all-to-all-done.5 = f32[16,16,256]{2,1,0:T(8,128)S(1)} async-done(((f32[16,16,256]{2,1,0:T(8,128)}), f32[16,16,256]{2,1,0:T(8,128)S(1)}, u32[]{:S(2)}, u32[]{:S(2)}) %all-to-all-start.5) | async-done | bytes 262176 | tf_op jit(solution)/shard_map/cond/branch_0_fun/all_to_all | solution.py:52
  327.6 11.7 %cholesky.130 = f32[128,128]{1,0:T(8,128)S(1)} custom-call(f32[128,128]{1,0:T(8,128)S(1)} %cholesky.194), custom_call_target="Cholesky" | custom-call | tf_op jit(solution)/shard_map/cond/branch_0_fun/jit(cholesky)/cholesky | solution.py:217
  339.4 9.8 %custom-call.13 = f32[1,128,128]{1,2,0:T(8,128)S(1)} custom-call(f32[1,128,128]{2,1,0:T(8,128)S(1)} %get-tuple-element.115), custom_call_target="InvertDiagBlocksLowerTriangular" | custom-call | tf_op jit(solution)/shard_map/cond/branch_0_fun/jit(cholesky)/cholesky | solution.py:217
  349.7 11.7 %cholesky.147 = f32[128,128]{1,0:T(8,128)S(1)} custom-call(f32[128,128]{1,0:T(8,128)S(1)} %convolution_subtract_fusion.3), custom_call_target="Cholesky" | custom-call | tf_op jit(solution)/shard_map/cond/branch_0_fun/jit(cholesky)/cholesky | solution.py:217
  361.4 0.7 compare_reduce_fusion.2
  363.5 4.1 while.4
  363.6 0.7 fusion.73
  364.2 1.3 bitcast_dynamic-update-slice_fusion.4
  365.6 0.7 fusion.73
  366.3 1.3 bitcast_dynamic-update-slice_fusion.4
  367.6 19.7 %custom-call.14 = f32[2,128,128]{1,2,0:T(8,128)S(1)} custom-call(f32[2,128,128]{2,1,0:T(8,128)S(1)} %get-tuple-element.63), custom_call_target="InvertDiagBlocksLowerTriangular" | custom-call | tf_op jit(solution)/shard_map/cond/branch_0_fun/jit(_solve_triangular)/triangular_solve | solution.py:218
  387.3 0.3 fusion.16
  387.9 0.3 fusion.28
  388.2 0.4 fusion
  388.6 14.5 %all_to_all.65 = f32[16,16,256]{2,1,0:T(8,128)S(1)} all-to-all(f32[16,16,256]{2,1,0:T(8,128)S(1)} %bitcast.118), channel_id=1, replica_groups=mesh['dp'=32,'feat'=16] {'feat'}, dimensions={0} | all-to-all | bytes 524288 | tf_op jit(solution)/shard_map/cond/branch_0_fun/all_to_all | solution.py:57
  403.1 14.6 %all_to_all.66 = f32[16,16,256]{2,1,0:T(8,128)S(1)} all-to-all(f32[16,16,256]{2,1,0:T(8,128)S(1)} %broadcast_in_dim.28), channel_id=1, replica_groups=mesh['dp'=32,'feat'=16] {'feat'}, dimensions={0} | all-to-all | bytes 524288 | tf_op jit(solution)/shard_map/cond/branch_0_fun/all_to_all | solution.py:52
  417.9 11.7 %cholesky.164 = f32[128,128]{1,0:T(8,128)S(1)} custom-call(f32[128,128]{1,0:T(8,128)S(1)} %cholesky.197), custom_call_target="Cholesky" | custom-call | tf_op jit(solution)/shard_map/cond/branch_0_fun/jit(cholesky)/cholesky | solution.py:217
  429.7 9.8 %custom-call.15 = f32[1,128,128]{1,2,0:T(8,128)S(1)} custom-call(f32[1,128,128]{2,1,0:T(8,128)S(1)} %get-tuple-element.111), custom_call_target="InvertDiagBlocksLowerTriangular" | custom-call | tf_op jit(solution)/shard_map/cond/branch_0_fun/jit(cholesky)/cholesky | solution.py:217
  440.0 11.7 %cholesky.181 = f32[128,128]{1,0:T(8,128)S(1)} custom-call(f32[128,128]{1,0:T(8,128)S(1)} %convolution_subtract_fusion.2), custom_call_target="Cholesky" | custom-call | tf_op jit(solution)/shard_map/cond/branch_0_fun/jit(cholesky)/cholesky | solution.py:217
  451.7 0.6 compare_reduce_fusion
  452.3 0.7 compare_reduce_fusion.1
  454.4 1.2 fusion.11
  455.6 4.1 while.5
  455.6 0.7 fusion.74
  456.3 1.3 bitcast_dynamic-update-slice_fusion.5
  457.6 0.7 fusion.74
  458.3 1.3 bitcast_dynamic-update-slice_fusion.5
  459.7 19.9 %custom-call.16 = f32[2,128,128]{1,2,0:T(8,128)S(1)} custom-call(f32[2,128,128]{2,1,0:T(8,128)S(1)} %get-tuple-element.64), custom_call_target="InvertDiagBlocksLowerTriangular" | custom-call | tf_op jit(solution)/shard_map/cond/branch_0_fun/jit(_solve_triangular)/triangular_solve | solution.py:218
  479.5 0.3 fusion.24
  480.1 0.3 fusion.23
  480.5 0.8 copy.30
  (62 shorter events, 3.3 us)
Async XLA Ops:
  2.6 9.1 %copy-start.4 = (s32[32]{0:T(128)S(1)}, s32[32]{0:T(128)}, u32[]{:S(2)}) copy-start(s32[32]{0:T(128)} %counts_ref.1) | copy-start | bytes 388
  2.9 10.7 %collective-permute-start = (f16[8,192,256]{2,1,0:T(8,128)(2,1)S(1)}, f16[8,192,256]{2,1,0:T(8,128)(2,1)S(1)}, u32[]{:S(2)}, u32[]{:S(2)}) collective-permute-start(f16[8,192,256]{2,1,0:T(8,128)(2,1)S(1)} %get-tuple-element.122), channel_id=1, source_target_pairs={{0,1},{1,0},{2,3},{3,2},{4,5},{5,4},{6,7},{7,6},{8,9},{9,8},{10,11... | collective-permute-start | bytes 2359304 | tf_op jit(solution)/shard_map/ppermute | solution.py:33
  40.7 21.3 %copy-start = (bf16[3072,256]{1,0:T(8,128)(2,1)S(1)}, bf16[3072,256]{1,0:T(8,128)(2,1)}, u32[]{:S(2)}) copy-start(bf16[3072,256]{1,0:T(8,128)(2,1)} %param.8) | copy-start | bytes 4718596
  62.0 32.9 %copy-start.3 = (bf16[256,256]{1,0:T(8,128)(2,1)S(1)}, bf16[256,256]{1,0:T(8,128)(2,1)}, u32[]{:S(2)}) copy-start(bf16[256,256]{1,0:T(8,128)(2,1)} %basis_ref.1) | copy-start | bytes 393220
  95.9 5.5 %collective-permute-start.1 = (f32[16,384]{1,0:T(8,128)S(1)}, f32[16,384]{1,0:T(8,128)S(1)}, u32[]{:S(2)}, u32[]{:S(2)}) collective-permute-start(f32[16,384]{1,0:T(8,128)S(1)} %get-tuple-element.36), channel_id=1, source_target_pairs={{0,1},{1,0},{2,3},{3,2},{4,5},{5,4},{6,7},{7,6},{8,9},{9,8},{10,11... | collective-permute-start | bytes 73736 | tf_op jit(solution)/shard_map/ppermute | solution.py:33
  137.0 4.3 copy-start.1
  141.3 75.5 %all-to-all-start = ((f32[16,192,256]{2,1,0:T(8,128)}), f32[16,192,256]{2,1,0:T(8,128)S(1)}, u32[]{:S(2)}, u32[]{:S(2)}) async-start(f32[16,192,256]{2,1,0:T(8,128)} %bitcast.112), calls=%async_computation | async-start | bytes 6291456 | tf_op jit(solution)/shard_map/cond/branch_0_fun/all_to_all | solution.py:57
  217.2 45.2 %copy-start.2 = (bf16[3072,256]{1,0:T(8,128)(2,1)S(1)}, bf16[3072,256]{1,0:T(8,128)(2,1)}, u32[]{:S(2)}) copy-start(bf16[3072,256]{1,0:T(8,128)(2,1)} %copy-done.1) | copy-start | bytes 4718596 | tf_op jit(solution)/shard_map/cond
  279.5 16.6 %all-to-all-start.3 = ((f32[32,8,256]{2,1,0:T(8,128)}), f32[32,8,256]{2,1,0:T(8,128)S(1)}, u32[]{:S(2)}, u32[]{:S(2)}) async-start(f32[32,8,256]{2,1,0:T(8,128)} %broadcast_in_dim.26), calls=%async_computation.3 | async-start | bytes 524288 | tf_op jit(solution)/shard_map/cond/branch_0_fun/all_to_all | solution.py:52
  312.4 15.0 %all-to-all-start.5 = ((f32[16,16,256]{2,1,0:T(8,128)}), f32[16,16,256]{2,1,0:T(8,128)S(1)}, u32[]{:S(2)}, u32[]{:S(2)}) async-start(f32[16,16,256]{2,1,0:T(8,128)} %broadcast_in_dim.27), calls=%async_computation.5 | async-start | bytes 524288 | tf_op jit(solution)/shard_map/cond/branch_0_fun/all_to_all | solution.py:52

commit v7 on v6

--- a/solution.py
+++ b/solution.py
@@ -60,38 +60,37 @@
     return spread(jnp.sum(pieces, axis=0), axis, None, size).reshape(value.shape)
 
 
-def sum_images(data, basis, core, beside):
-    chips = lax.axis_size("feat") // CORES
-    rows, columns = data.shape
-    here = rows // (chips * CORES)
-    split = data.reshape(chips, CORES, here, columns)
-
-    def half(which):
-        return lax.dynamic_index_in_dim(split, which, 1, False)
-
-    def times(left, right):
+def half_images(data, basis, active, core):
+    half = data.shape[0] // CORES
+    whole = jnp.dot(data, basis, preferred_element_type=F32).reshape(CORES, half, -1)
+    theirs = core_swap(
+        (lax.dynamic_index_in_dim(whole, 1 - core, 0, False) * LIFT).astype(F16)
+    )
+    row_ids = core * half + lax.broadcasted_iota(jnp.int32, (half, 1), 0)
+    valid = jnp.where(row_ids < active * BLOCK, 1.0, 0.0)
+    mine, theirs, valid = lax.optimization_barrier(
+        (lax.dynamic_index_in_dim(whole, core, 0, False) * LIFT, theirs, valid)
+    )
+    pair = ((mine + theirs.astype(F32)) * valid).astype(F16)
+    return lax.psum(pair, "feat", axis_index_groups=groups_z())
+
+
+def column_terms(data, basis, active, core):
+    half = data.shape[0] // CORES
+    split = data.reshape(CORES, half, -1)
+
+    def terms(which, images):
+        rows = lax.dynamic_index_in_dim(split, which, 0, False)
         return lax.dot_general(
-            left, right, (((2,), (0,)), ((), ())), preferred_element_type=F32
+            rows, images.astype(BF16), ROWS, preferred_element_type=F32
         )
 
-    whole = times(split.reshape(chips, CORES * here, columns), basis)
-    whole = whole.reshape(chips, CORES, here, -1)
-    theirs = core_swap(
-        (lax.dynamic_index_in_dim(whole, 1 - core, 1, False) * LIFT).astype(F16)
-    )
-    mine, theirs, beside = lax.optimization_barrier(
-        (lax.dynamic_index_in_dim(whole, core, 1, False), theirs, beside)
-    )
-    pair = mine + theirs.astype(F32) / LIFT
-    pieces = lax.all_to_all(
-        (pair * LIFT).astype(F16), "feat", 0, 0, axis_index_groups=groups_z()
-    )
-    return jnp.sum(pieces.astype(F32), axis=0), beside
-
-
-def gram_kernel(
-    place_ref, counts_ref, step_ref, basis_ref, updated_ref, mine_ref, theirs_ref, packed
-):
+    images = half_images(data, basis, active, core)
+    own, theirs = lax.optimization_barrier((terms(core, images), core_swap(images)))
+    return ((own + terms(1 - core, theirs)) / TERMS).astype(F16)
+
+
+def gram_kernel(counts_ref, step_ref, basis_ref, updated_ref, mine_ref, theirs_ref, packed):
     count = counts_ref[0]
     for i in range(1, counts_ref.shape[0]):
         count += counts_ref[i]
@@ -108,14 +107,15 @@
     )
     packed[:, : 2 * half] = dot(updated[:, :half], updated)
     packed[:, 2 * half :] = dot(updated[:, half:], updated[:, half:])
-    first = place_ref[0] * CORES
-    mine = pl.multiple_of((first + place_ref[1]) * share, share)
-    theirs = pl.multiple_of((first + 1 - place_ref[1]) * share, share)
+    first = lax.rem(lax.axis_index("dp"), X) * CORES
+    core = lax.rem(lax.axis_index("feat"), CORES)
+    mine = pl.multiple_of((first + core) * share, share)
+    theirs = pl.multiple_of((first + 1 - core) * share, share)
     mine_ref[...] = packed[pl.ds(mine, share), :]
     theirs_ref[...] = packed[pl.ds(theirs, share), :]
 
 
-def gram_share(place, counts, step, basis):
+def gram_share(counts, step, basis):
     rank = basis.shape[1]
     half = rank // 2
     share = jax.ShapeDtypeStruct((half // (X * CORES), rank + half), F32)
@@ -124,12 +124,12 @@
     return pl.pallas_call(
         gram_kernel,
         out_shape=(jax.ShapeDtypeStruct(basis.shape, F32), share, share),
-        in_specs=[smem, smem, vmem, vmem],
+        in_specs=[smem, vmem, vmem],
         out_specs=(vmem, vmem, vmem),
         scratch_shapes=[pltpu.VMEM((half, rank + half), F32)],
         compiler_params=pltpu.CompilerParams(vmem_limit_bytes=32 * 1024 * 1024),
         name="gram_share",
-    )(place, counts, step, basis)
+    )(counts, step, basis)
 
 
 def sum_gram(mine, theirs):
@@ -179,7 +179,7 @@
         parts = halves(now)
         moved = multiply(parts, unit_parts, PLAIN)
         excess = multiply(halves(moved), parts, OUTER) - eye
-        inverse[...] = now - multiply(halves(excess * keep), parts, PLAIN)
+        inverse[...] = now - coarse(halves(excess * keep), parts, PLAIN)
         return jnp.sum(excess * excess)
 
     improve(coarse)
@@ -242,25 +242,12 @@
     dp = lax.axis_index("dp")
     feat = lax.axis_index("feat")
     dp_size = lax.axis_size("dp")
-    core = feat % CORES
-    here = rows // lax.axis_size("feat")
     active = lax.dynamic_index_in_dim(block_counts, dp, 0, False)
-    row_ids = feat * here + lax.broadcasted_iota(jnp.int32, (here, 1), 0)
-    valid = jnp.where(row_ids < active * BLOCK, 1.0, 0.0)
-    beside = (valid, jnp.stack([dp % X, core]))
-    images, beside = sum_images(data, basis, core, beside)
-    valid, place = beside
-    images = lax.reduce_precision(images * valid, 8, 7).astype(F16)
-    images = lax.all_gather(images, "feat", tiled=True).astype(BF16)
-
-    terms = lax.dot_general(
-        data, images, (((0,), (0,)), ((), ())), preferred_element_type=F32
-    )
-    terms = (terms / TERMS).astype(F16)
+    terms = column_terms(data, basis, active, feat % CORES)
     pieces = lax.all_to_all(terms.reshape(dp_size, columns // dp_size, rank), "dp", 0, 0)
     piece = (jnp.sum(pieces.astype(F32), axis=0) * (LIFT_STEP / LIFT)).astype(F16)
     step = spread(piece, "dp", None, dp_size).reshape(columns, rank).astype(F32)
-    updated, mine, theirs = gram_share(place, block_counts, step, basis)
+    updated, mine, theirs = gram_share(block_counts, step, basis)
     gram, data, block_counts, basis = lax.optimization_barrier(
         (sum_gram(mine, theirs), data, block_counts, basis)
     )

time: 491 us -> 485 us (0.988)
  blocking collectives: 207 us -> 191 us
  starting transfers between devices: 25.8 us -> 35.8 us
    psum x0 -> x1, blocking collectives: none -> 31.2 us  [half_images(): return lax.psum(pair, 'feat', axis_index_groups=groups_z())]
    all_to_all x1 -> x0, blocking collectives: 26.8 us -> none  [sum_images(): lax.all_to_all((pair * LIFT).astype(F16), 'feat', 0, 0, axis_index_groups...]
    all_gather x1 -> x0, blocking collectives: 21.1 us -> none  [on_device(): images = lax.all_gather(images, 'feat', tiled=True).astype(BF16)]
    ppermute x2 -> x3, starting transfers between devices: 13.5 us -> 22.8 us  [core_swap(): return lax.ppermute(value, 'feat', [(i, i ^ 1) for i in range(count)])]
  transfers between devices with their start and end apart: 5 -> 6, of which waited for: 5 -> 6; matrix products, arithmetic and copies ran while one was open for 0% -> 0% of each run, Pallas kernels for 0% -> 0%
where the time goes in v7:
time: 485 us; the launch traced here: 477 us
  blocking collectives  191 us (39%)
  other arithmetic  112 us (23%)
  waiting for transfers between devices  96.3 us (20%)
  starting transfers between devices  35.8 us (7%)
  local copies, waits for them, and re-layouts  12.2 us (3%)
  Pallas kernels  12 us (2%)
  matrix products  10.4 us (2%)
    all_to_all x5, blocking collectives, spread(): return lax.all_to_all(copies, axis, 0, 0, axis_index_groups=groups)  95.8 us
    all_to_all x1, waiting for transfers between devices, total(): lax.all_to_all(value.reshape((size, value.shape[0] // size) + value.shape...  71.2 us
    another operation x13, other arithmetic, orthonormal(): lower = jnp.linalg.cholesky(gram_total)  68.6 us
    all_to_all x3, blocking collectives, total(): lax.all_to_all(value.reshape((size, value.shape[0] // size) + value.shape...  45 us
    another operation x5, other arithmetic, orthonormal(): solved = jax.scipy.linalg.solve_triangular(lower, matrix.T, lower=True)  39.6 us
    psum x1, blocking collectives, half_images(): return lax.psum(pair, 'feat', axis_index_groups=groups_z())  31.2 us
    ppermute x3, starting transfers between devices, core_swap(): return lax.ppermute(value, 'feat', [(i, i ^ 1) for i in range(count)])  22.8 us
    all_to_all x2, waiting for transfers between devices, spread(): return lax.all_to_all(copies, axis, 0, 0, axis_index_groups=groups)  22.3 us
  transfers between devices with their start and end apart: 6, of which 6 were waited for; matrix products, arithmetic and copies ran while one was open for 0% of the time, Pallas kernels for 0%

profile of v7, /device:TPU:1, one launch (start us, length us, event | category | flops | bytes accessed | tf_op | source)
XLA Modules:
  0.0 476.7 jit_solution(11351171908554191161)
XLA Ops:
  0.7 2.0 fusion.54
  2.9 8.8 %collective-permute-start = (f16[1536,256]{1,0:T(8,128)(2,1)S(1)}, f16[1536,256]{1,0:T(8,128)(2,1)S(1)}, u32[]{:S(2)}, u32[]{:S(2)}) collective-permute-start(f16[1536,256]{1,0:T(8,128)(2,1)S(1)} %get-tuple-element.124), channel_id=1, source_target_pairs={{0,1},{1,0},{2,3},{3,2},{4,5},{5,4},{6,7},{7,6},{8,9},{9,8},{10,11... | collective-permute-start | bytes 2359304 | tf_op jit(solution)/shard_map/ppermute | solution.py:33
  11.7 0.6 dynamic_slice.24
  13.0 0.6 collective-permute-done
  14.0 31.2 %all-reduce.2 = u32[4,49152]{1,0:T(4,128)S(1)} all-reduce(u32[4,49152]{1,0:T(4,128)S(1)} %bitcast.115), channel_id=1, replica_groups={{0,2,4,6,8,10,12,14},{1,3,5,7,9,11,13,15},{16,18,20,22,24,26,28,30},{17..., use_global_device_ids=true, to_apply=%region_0.1.clone | all-reduce | flops 196608 | bytes 1572864 | tf_op jit(solution)/shard_map/psum | solution.py:75
  45.2 9.2 %collective-permute-start.1 = (f16[1536,256]{1,0:T(8,128)(2,1)S(1)}, f16[1536,256]{1,0:T(8,128)(2,1)S(1)}, u32[]{:S(2)}, u32[]{:S(2)}) collective-permute-start(f16[1536,256]{1,0:T(8,128)(2,1)S(1)} %bitcast.121), channel_id=1, source_target_pairs={{0,1},{1,0},{2,3},{3,2},{4,5},{5,4},{6,7},{7,6},{8,9},{9,8},{10,11... | collective-permute-start | bytes 2359304 | tf_op jit(solution)/shard_map/ppermute | solution.py:33
  54.4 0.4 fusion.43
  54.8 1.4 collective-permute-done.1
  56.3 0.4 fusion.41
  56.8 18.8 %all_to_all.53 = f16[32,8,256]{2,1,0:T(8,128)(2,1)S(1)} all-to-all(f16[32,8,256]{2,1,0:T(8,128)(2,1)S(1)} %fusion.49), channel_id=1, replica_groups=mesh['dp'=32,'feat'=16] {'dp'}, dimensions={0} | all-to-all | bytes 262144 | tf_op jit(solution)/shard_map/all_to_all | solution.py:247
  75.7 13.0 %all_to_all.54 = f16[32,8,256]{2,1,0:T(8,128)(2,1)S(1)} all-to-all(f16[32,8,256]{2,1,0:T(8,128)(2,1)S(1)} %broadcast_in_dim.36), channel_id=1, replica_groups=mesh['dp'=32,'feat'=16] {'dp'}, dimensions={0} | all-to-all | bytes 262144 | tf_op jit(solution)/shard_map/all_to_all | solution.py:52
  88.7 1.0 gram_share.1
  89.7 4.8 %collective-permute-start.2 = (f32[16,384]{1,0:T(8,128)S(1)}, f32[16,384]{1,0:T(8,128)S(1)}, u32[]{:S(2)}, u32[]{:S(2)}) collective-permute-start(f32[16,384]{1,0:T(8,128)S(1)} %get-tuple-element.38), channel_id=1, source_target_pairs={{0,1},{1,0},{2,3},{3,2},{4,5},{5,4},{6,7},{7,6},{8,9},{9,8},{10,11... | collective-permute-start | bytes 73736 | tf_op jit(solution)/shard_map/ppermute | solution.py:33
  94.6 0.8 collective-permute-done.2
  95.4 12.9 %all_to_all.55 = f32[8,16,384]{2,1,0:T(8,128)S(1)} all-to-all(f32[8,16,384]{2,1,0:T(8,128)S(1)} %broadcast_in_dim.38), channel_id=1, replica_groups={{0,2,4,6,8,10,12,14},{1,3,5,7,9,11,13,15},{16,18,20,22,24,26,28,30},{17..., dimensions={0} | all-to-all | bytes 393216 | tf_op jit(solution)/shard_map/all_to_all | solution.py:52
  108.4 10.3 %all_to_all.56 = f32[8,16,384]{2,1,0:T(8,128)S(1)} all-to-all(f32[8,16,384]{2,1,0:T(8,128)S(1)} %broadcast_in_dim.39), channel_id=1, replica_groups={{0,1,16,17,32,33,48,49},{2,3,18,19,34,35,50,51},{4,5,20,21,36,37,52,53}..., dimensions={0} | all-to-all | bytes 393216 | tf_op jit(solution)/shard_map/all_to_all | solution.py:52
  118.7 11.0 %factor.1 = (f32[256,256]{1,0:T(8,128)S(1)}, f32[256,256]{1,0:T(8,128)S(1)}, s32[1]{0:T(128)}) custom-call(f32[128,384]{1,0:T(8,128)S(1)} %bitcast.110, f32[256,256]{1,0:T(8,128)S(1)} %get-tuple-element.40.matrix_ref), custom_call_target="tpu_custom_call" | custom-call | tf_op jit(solution)/shard_map/factor/pallas_call | solution.py:203
  130.3 345.3 %conditional.1 = (f32[256,256]{1,0:T(8,128)S(1)}, f32[256,256]{1,0:T(8,128)S(1)}) conditional(s32[]{:T(128)} %bitcast.32, (bf16[256,256]{1,0:T(8,128)(2,1)S(1)}, s32[32]{0:T(128)S(1)}, bf16[3072,256]{1,0:T(8,128)(2,1)S(1)}) %tuple.87, (f32[256,256]{1,0:T(8,128)S(1)}, f32[256,256]{1,0:T(8,128)S(1)}) %tuple.23), branch_computations={%region_3.15_spmd, %region_13.16_spmd} | conditional | flops 1815717376 | bytes 44985072 | solution.py:255
  130.3 0.6 dynamic_slice.15
  131.6 2.8 convolution_select_fusion
  134.4 5.2 %all-to-all-start = ((f32[16,192,256]{2,1,0:T(8,128)}), f32[16,192,256]{2,1,0:T(8,128)}, u32[]{:S(2)}, u32[]{:S(2)}) async-start(f32[16,192,256]{2,1,0:T(8,128)} %bitcast.114), calls=%async_computation | async-start | bytes 6291456 | tf_op jit(solution)/shard_map/cond/branch_0_fun/all_to_all | solution.py:57
  139.6 71.2 %all-to-all-done = f32[16,192,256]{2,1,0:T(8,128)} async-done(((f32[16,192,256]{2,1,0:T(8,128)}), f32[16,192,256]{2,1,0:T(8,128)}, u32[]{:S(2)}, u32[]{:S(2)}) %all-to-all-start) | async-done | bytes 3145760 | tf_op jit(solution)/shard_map/cond/branch_0_fun/all_to_all | solution.py:57
  210.7 2.1 reduce_sum.56
  213.0 45.0 %all_to_all.52 = bf16[16,192,256]{2,1,0:T(8,128)(2,1)S(1)} all-to-all(bf16[16,192,256]{2,1,0:T(8,128)(2,1)S(1)} %broadcast_in_dim.25), channel_id=1, replica_groups=mesh['dp'=32,'feat'=16] {'feat'}, dimensions={0} | all-to-all | bytes 3145728 | tf_op jit(solution)/shard_map/cond/branch_0_fun/all_to_all | solution.py:52
  258.0 0.7 convolution_bitcast_fusion
  258.7 15.7 %all_to_all.57 = f32[32,8,256]{2,1,0:T(8,128)S(1)} all-to-all(f32[32,8,256]{2,1,0:T(8,128)S(1)} %convolution_bitcast_fusion), channel_id=1, replica_groups=mesh['dp'=32,'feat'=16] {'dp'}, dimensions={0} | all-to-all | bytes 524288 | tf_op jit(solution)/shard_map/cond/branch_0_fun/all_to_all | solution.py:57
  274.5 0.7 broadcast_in_dim.26
  275.2 3.9 all-to-all-start.3
  279.1 0.7 reduce_sum.58
  280.6 11.2 %all-to-all-done.3 = f32[32,8,256]{2,1,0:T(8,128)S(1)} async-done(((f32[32,8,256]{2,1,0:T(8,128)}), f32[32,8,256]{2,1,0:T(8,128)S(1)}, u32[]{:S(2)}, u32[]{:S(2)}) %all-to-all-start.3) | async-done | bytes 262176 | tf_op jit(solution)/shard_map/cond/branch_0_fun/all_to_all | solution.py:52
  292.0 0.4 fusion.15
  292.4 14.9 %all_to_all.58 = f32[16,16,256]{2,1,0:T(8,128)S(1)} all-to-all(f32[16,16,256]{2,1,0:T(8,128)S(1)} %bitcast.119), channel_id=1, replica_groups=mesh['dp'=32,'feat'=16] {'feat'}, dimensions={0} | all-to-all | bytes 524288 | tf_op jit(solution)/shard_map/cond/branch_0_fun/all_to_all | solution.py:57
  307.3 0.7 broadcast_in_dim.27
  308.1 4.0 all-to-all-start.5
  312.1 11.0 %all-to-all-done.5 = f32[16,16,256]{2,1,0:T(8,128)S(1)} async-done(((f32[16,16,256]{2,1,0:T(8,128)}), f32[16,16,256]{2,1,0:T(8,128)S(1)}, u32[]{:S(2)}, u32[]{:S(2)}) %all-to-all-start.5) | async-done | bytes 262176 | tf_op jit(solution)/shard_map/cond/branch_0_fun/all_to_all | solution.py:52
  323.3 11.7 %cholesky.130 = f32[128,128]{1,0:T(8,128)S(1)} custom-call(f32[128,128]{1,0:T(8,128)S(1)} %cholesky.194), custom_call_target="Cholesky" | custom-call | tf_op jit(solution)/shard_map/cond/branch_0_fun/jit(cholesky)/cholesky | solution.py:217
  335.0 9.8 %custom-call.13 = f32[1,128,128]{1,2,0:T(8,128)S(1)} custom-call(f32[1,128,128]{2,1,0:T(8,128)S(1)} %get-tuple-element.117), custom_call_target="InvertDiagBlocksLowerTriangular" | custom-call | tf_op jit(solution)/shard_map/cond/branch_0_fun/jit(cholesky)/cholesky | solution.py:217
  345.4 11.7 %cholesky.147 = f32[128,128]{1,0:T(8,128)S(1)} custom-call(f32[128,128]{1,0:T(8,128)S(1)} %convolution_subtract_fusion.3), custom_call_target="Cholesky" | custom-call | tf_op jit(solution)/shard_map/cond/branch_0_fun/jit(cholesky)/cholesky | solution.py:217
  357.1 0.6 compare_reduce_fusion.2
  359.1 3.8 while.4
  359.1 0.6 fusion.72
  359.7 1.3 bitcast_dynamic-update-slice_fusion.4
  361.0 0.6 fusion.72
  361.6 1.3 bitcast_dynamic-update-slice_fusion.4
  362.9 19.7 %custom-call.14 = f32[2,128,128]{1,2,0:T(8,128)S(1)} custom-call(f32[2,128,128]{2,1,0:T(8,128)S(1)} %get-tuple-element.65), custom_call_target="InvertDiagBlocksLowerTriangular" | custom-call | tf_op jit(solution)/shard_map/cond/branch_0_fun/jit(_solve_triangular)/triangular_solve | solution.py:218
  383.2 0.3 fusion.28
  383.5 0.4 fusion
  383.9 14.5 %all_to_all.59 = f32[16,16,256]{2,1,0:T(8,128)S(1)} all-to-all(f32[16,16,256]{2,1,0:T(8,128)S(1)} %bitcast.120), channel_id=1, replica_groups=mesh['dp'=32,'feat'=16] {'feat'}, dimensions={0} | all-to-all | bytes 524288 | tf_op jit(solution)/shard_map/cond/branch_0_fun/all_to_all | solution.py:57
  398.4 14.6 %all_to_all.60 = f32[16,16,256]{2,1,0:T(8,128)S(1)} all-to-all(f32[16,16,256]{2,1,0:T(8,128)S(1)} %broadcast_in_dim.28), channel_id=1, replica_groups=mesh['dp'=32,'feat'=16] {'feat'}, dimensions={0} | all-to-all | bytes 524288 | tf_op jit(solution)/shard_map/cond/branch_0_fun/all_to_all | solution.py:52
  413.2 11.7 %cholesky.164 = f32[128,128]{1,0:T(8,128)S(1)} custom-call(f32[128,128]{1,0:T(8,128)S(1)} %cholesky.197), custom_call_target="Cholesky" | custom-call | tf_op jit(solution)/shard_map/cond/branch_0_fun/jit(cholesky)/cholesky | solution.py:217
  425.0 9.8 %custom-call.15 = f32[1,128,128]{1,2,0:T(8,128)S(1)} custom-call(f32[1,128,128]{2,1,0:T(8,128)S(1)} %get-tuple-element.113), custom_call_target="InvertDiagBlocksLowerTriangular" | custom-call | tf_op jit(solution)/shard_map/cond/branch_0_fun/jit(cholesky)/cholesky | solution.py:217
  435.3 11.7 %cholesky.181 = f32[128,128]{1,0:T(8,128)S(1)} custom-call(f32[128,128]{1,0:T(8,128)S(1)} %convolution_subtract_fusion.2), custom_call_target="Cholesky" | custom-call | tf_op jit(solution)/shard_map/cond/branch_0_fun/jit(cholesky)/cholesky | solution.py:217
  447.0 0.7 compare_reduce_fusion
  447.7 0.6 compare_reduce_fusion.1
  449.8 0.5 fusion.11
  450.3 4.1 while.5
  450.3 0.6 fusion.73
  450.9 1.4 bitcast_dynamic-update-slice_fusion.5
  452.4 0.6 fusion.73
  453.0 1.4 bitcast_dynamic-update-slice_fusion.5
  454.4 19.9 %custom-call.16 = f32[2,128,128]{1,2,0:T(8,128)S(1)} custom-call(f32[2,128,128]{2,1,0:T(8,128)S(1)} %get-tuple-element.66), custom_call_target="InvertDiagBlocksLowerTriangular" | custom-call | tf_op jit(solution)/shard_map/cond/branch_0_fun/jit(_solve_triangular)/triangular_solve | solution.py:218
  474.3 0.3 fusion.24
  474.9 0.3 fusion.23
  475.6 0.7 copy-done.3
  (63 shorter events, 4.1 us)
Async XLA Ops:
  2.6 9.1 %copy-start.2 = (s32[32]{0:T(128)S(1)}, s32[32]{0:T(128)}, u32[]{:S(2)}) copy-start(s32[32]{0:T(128)} %counts_ref.1) | copy-start | bytes 388
  2.9 10.7 %collective-permute-start = (f16[1536,256]{1,0:T(8,128)(2,1)S(1)}, f16[1536,256]{1,0:T(8,128)(2,1)S(1)}, u32[]{:S(2)}, u32[]{:S(2)}) collective-permute-start(f16[1536,256]{1,0:T(8,128)(2,1)S(1)} %get-tuple-element.124), channel_id=1, source_target_pairs={{0,1},{1,0},{2,3},{3,2},{4,5},{5,4},{6,7},{7,6},{8,9},{9,8},{10,11... | collective-permute-start | bytes 2359304 | tf_op jit(solution)/shard_map/ppermute | solution.py:33
  13.9 40.5 %copy-start = (bf16[3072,256]{1,0:T(8,128)(2,1)S(1)}, bf16[3072,256]{1,0:T(8,128)(2,1)}, u32[]{:S(2)}) copy-start(bf16[3072,256]{1,0:T(8,128)(2,1)} %param.8) | copy-start | bytes 4718596
  45.2 11.1 %collective-permute-start.1 = (f16[1536,256]{1,0:T(8,128)(2,1)S(1)}, f16[1536,256]{1,0:T(8,128)(2,1)S(1)}, u32[]{:S(2)}, u32[]{:S(2)}) collective-permute-start(f16[1536,256]{1,0:T(8,128)(2,1)S(1)} %bitcast.121), channel_id=1, source_target_pairs={{0,1},{1,0},{2,3},{3,2},{4,5},{5,4},{6,7},{7,6},{8,9},{9,8},{10,11... | collective-permute-start | bytes 2359304 | tf_op jit(solution)/shard_map/ppermute | solution.py:33
  54.8 33.9 %copy-start.1 = (bf16[256,256]{1,0:T(8,128)(2,1)S(1)}, bf16[256,256]{1,0:T(8,128)(2,1)}, u32[]{:S(2)}) copy-start(bf16[256,256]{1,0:T(8,128)(2,1)} %basis_ref.1) | copy-start | bytes 393220
  89.7 5.6 %collective-permute-start.2 = (f32[16,384]{1,0:T(8,128)S(1)}, f32[16,384]{1,0:T(8,128)S(1)}, u32[]{:S(2)}, u32[]{:S(2)}) collective-permute-start(f32[16,384]{1,0:T(8,128)S(1)} %get-tuple-element.38), channel_id=1, source_target_pairs={{0,1},{1,0},{2,3},{3,2},{4,5},{5,4},{6,7},{7,6},{8,9},{9,8},{10,11... | collective-permute-start | bytes 73736 | tf_op jit(solution)/shard_map/ppermute | solution.py:33
  134.4 76.3 %all-to-all-start = ((f32[16,192,256]{2,1,0:T(8,128)}), f32[16,192,256]{2,1,0:T(8,128)}, u32[]{:S(2)}, u32[]{:S(2)}) async-start(f32[16,192,256]{2,1,0:T(8,128)} %bitcast.114), calls=%async_computation | async-start | bytes 6291456 | tf_op jit(solution)/shard_map/cond/branch_0_fun/all_to_all | solution.py:57
  275.2 16.6 %all-to-all-start.3 = ((f32[32,8,256]{2,1,0:T(8,128)}), f32[32,8,256]{2,1,0:T(8,128)S(1)}, u32[]{:S(2)}, u32[]{:S(2)}) async-start(f32[32,8,256]{2,1,0:T(8,128)} %broadcast_in_dim.26), calls=%async_computation.3 | async-start | bytes 524288 | tf_op jit(solution)/shard_map/cond/branch_0_fun/all_to_all | solution.py:52
  308.1 15.0 %all-to-all-start.5 = ((f32[16,16,256]{2,1,0:T(8,128)}), f32[16,16,256]{2,1,0:T(8,128)S(1)}, u32[]{:S(2)}, u32[]{:S(2)}) async-start(f32[16,16,256]{2,1,0:T(8,128)} %broadcast_in_dim.27), calls=%async_computation.5 | async-start | bytes 524288 | tf_op jit(solution)/shard_map/cond/branch_0_fun/all_to_all | solution.py:52
  475.6 0.7 copy-start.3
  475.6 0.8 copy-start.4

commit v8 on v7

--- a/solution.py
+++ b/solution.py
@@ -12,6 +12,7 @@
 BLOCK = 512
 CORES = 2
 X = 4
+ROW_PAIR = 2
 F32 = jnp.float32
 BF16 = jnp.bfloat16
 F16 = jnp.float16
@@ -38,11 +39,12 @@
     return [list(range(c, count, CORES)) for c in range(CORES)]
 
 
-def groups_xc():
+def groups_near():
     count, width = lax.axis_size("dp"), lax.axis_size("feat")
+    near = X * ROW_PAIR
     return [
-        [(y + x) * width + z + c for x in range(X) for c in range(CORES)]
-        for y in range(0, count, X)
+        [(first + i) * width + z + c for i in range(near) for c in range(CORES)]
+        for first in range(0, count, near)
         for z in range(0, width, CORES)
     ]
 
@@ -107,7 +109,7 @@
     )
     packed[:, : 2 * half] = dot(updated[:, :half], updated)
     packed[:, 2 * half :] = dot(updated[:, half:], updated[:, half:])
-    first = lax.rem(lax.axis_index("dp"), X) * CORES
+    first = lax.rem(lax.axis_index("dp"), X * ROW_PAIR) * CORES
     core = lax.rem(lax.axis_index("feat"), CORES)
     mine = pl.multiple_of((first + core) * share, share)
     theirs = pl.multiple_of((first + 1 - core) * share, share)
@@ -118,7 +120,7 @@
 def gram_share(counts, step, basis):
     rank = basis.shape[1]
     half = rank // 2
-    share = jax.ShapeDtypeStruct((half // (X * CORES), rank + half), F32)
+    share = jax.ShapeDtypeStruct((half // (X * ROW_PAIR * CORES), rank + half), F32)
     vmem = pl.BlockSpec(memory_space=pltpu.VMEM)
     smem = pl.BlockSpec(memory_space=pltpu.SMEM)
     return pl.pallas_call(
@@ -136,7 +138,7 @@
     chips = lax.axis_size("feat") // CORES
     pair = mine + core_swap(theirs)
     summed = jnp.sum(spread(pair, "feat", groups_z(), chips), axis=0)
-    shares = spread(summed, ("dp", "feat"), groups_xc(), X * CORES)
+    shares = spread(summed, ("dp", "feat"), groups_near(), X * ROW_PAIR * CORES)
     return shares.reshape(-1, shares.shape[-1])
 
 

time: 485 us -> 489 us (level)
  starting transfers between devices: 35.8 us -> 45.2 us
    all_to_all x2, starting transfers between devices: 7.83 us -> 17.3 us  [spread(): return lax.all_to_all(copies, axis, 0, 0, axis_index_groups=groups)]
where the time goes in v8:
time: 489 us; the launch traced here: 485 us
  blocking collectives  191 us (39%)
  other arithmetic  112 us (23%)
  waiting for transfers between devices  95.4 us (20%)
  starting transfers between devices  45.2 us (9%)
  local copies, waits for them, and re-layouts  12.2 us (2%)
  Pallas kernels  12 us (2%)
  matrix products  10.4 us (2%)
    all_to_all x5, blocking collectives, spread(): return lax.all_to_all(copies, axis, 0, 0, axis_index_groups=groups)  94.8 us
    all_to_all x1, waiting for transfers between devices, total(): lax.all_to_all(value.reshape((size, value.shape[0] // size) + value.shape...  71.2 us
    another operation x13, other arithmetic, orthonormal(): lower = jnp.linalg.cholesky(gram_total)  68.6 us
    all_to_all x3, blocking collectives, total(): lax.all_to_all(value.reshape((size, value.shape[0] // size) + value.shape...  46.1 us
    another operation x5, other arithmetic, orthonormal(): solved = jax.scipy.linalg.solve_triangular(lower, matrix.T, lower=True)  39.7 us
    psum x1, blocking collectives, half_images(): return lax.psum(pair, 'feat', axis_index_groups=groups_z())  31.2 us
    ppermute x3, starting transfers between devices, core_swap(): return lax.ppermute(value, 'feat', [(i, i ^ 1) for i in range(count)])  22.8 us
    all_to_all x2, waiting for transfers between devices, spread(): return lax.all_to_all(copies, axis, 0, 0, axis_index_groups=groups)  21.4 us
  transfers between devices with their start and end apart: 6, of which 6 were waited for; matrix products, arithmetic and copies ran while one was open for 0% of the time, Pallas kernels for 0%

profile of v8, /device:TPU:1, one launch (start us, length us, event | category | flops | bytes accessed | tf_op | source)
XLA Modules:
  0.0 485.5 jit_solution(8974013650046966266)
XLA Ops:
  0.7 2.0 fusion.54
  2.9 8.8 %collective-permute-start = (f16[1536,256]{1,0:T(8,128)(2,1)S(1)}, f16[1536,256]{1,0:T(8,128)(2,1)S(1)}, u32[]{:S(2)}, u32[]{:S(2)}) collective-permute-start(f16[1536,256]{1,0:T(8,128)(2,1)S(1)} %get-tuple-element.124), channel_id=1, source_target_pairs={{0,1},{1,0},{2,3},{3,2},{4,5},{5,4},{6,7},{7,6},{8,9},{9,8},{10,11... | collective-permute-start | bytes 2359304 | tf_op jit(solution)/shard_map/ppermute | solution.py:34
  11.7 0.6 dynamic_slice.24
  13.0 0.6 collective-permute-done
  14.0 31.2 %all-reduce.2 = u32[4,49152]{1,0:T(4,128)S(1)} all-reduce(u32[4,49152]{1,0:T(4,128)S(1)} %bitcast.115), channel_id=1, replica_groups={{0,2,4,6,8,10,12,14},{1,3,5,7,9,11,13,15},{16,18,20,22,24,26,28,30},{17..., use_global_device_ids=true, to_apply=%region_0.1.clone | all-reduce | flops 196608 | bytes 1572864 | tf_op jit(solution)/shard_map/psum | solution.py:77
  45.2 9.2 %collective-permute-start.1 = (f16[1536,256]{1,0:T(8,128)(2,1)S(1)}, f16[1536,256]{1,0:T(8,128)(2,1)S(1)}, u32[]{:S(2)}, u32[]{:S(2)}) collective-permute-start(f16[1536,256]{1,0:T(8,128)(2,1)S(1)} %bitcast.121), channel_id=1, source_target_pairs={{0,1},{1,0},{2,3},{3,2},{4,5},{5,4},{6,7},{7,6},{8,9},{9,8},{10,11... | collective-permute-start | bytes 2359304 | tf_op jit(solution)/shard_map/ppermute | solution.py:34
  54.4 0.4 fusion.43
  54.8 1.4 collective-permute-done.1
  56.3 0.4 fusion.41
  56.8 18.8 %all_to_all.53 = f16[32,8,256]{2,1,0:T(8,128)(2,1)S(1)} all-to-all(f16[32,8,256]{2,1,0:T(8,128)(2,1)S(1)} %fusion.49), channel_id=1, replica_groups=mesh['dp'=32,'feat'=16] {'dp'}, dimensions={0} | all-to-all | bytes 262144 | tf_op jit(solution)/shard_map/all_to_all | solution.py:249
  75.7 13.0 %all_to_all.54 = f16[32,8,256]{2,1,0:T(8,128)(2,1)S(1)} all-to-all(f16[32,8,256]{2,1,0:T(8,128)(2,1)S(1)} %broadcast_in_dim.36), channel_id=1, replica_groups=mesh['dp'=32,'feat'=16] {'dp'}, dimensions={0} | all-to-all | bytes 262144 | tf_op jit(solution)/shard_map/all_to_all | solution.py:54
  88.7 1.0 gram_share.1
  89.7 4.8 collective-permute-start.2
  94.5 0.8 collective-permute-done.2
  95.4 10.9 %all_to_all.55 = f32[8,8,384]{2,1,0:T(8,128)S(1)} all-to-all(f32[8,8,384]{2,1,0:T(8,128)S(1)} %broadcast_in_dim.38), channel_id=1, replica_groups={{0,2,4,6,8,10,12,14},{1,3,5,7,9,11,13,15},{16,18,20,22,24,26,28,30},{17..., dimensions={0} | all-to-all | bytes 196608 | tf_op jit(solution)/shard_map/all_to_all | solution.py:54
  106.4 11.4 %all_to_all.56 = f32[16,8,384]{2,1,0:T(8,128)S(1)} all-to-all(f32[16,8,384]{2,1,0:T(8,128)S(1)} %broadcast_in_dim.39), channel_id=1, replica_groups={{0,1,16,17,32,33,48,49,64,65,80,81,96,97,112,113},{2,3,18,19,34,35,50,5..., dimensions={0} | all-to-all | bytes 393216 | tf_op jit(solution)/shard_map/all_to_all | solution.py:54
  117.8 11.0 %factor.1 = (f32[256,256]{1,0:T(8,128)S(1)}, f32[256,256]{1,0:T(8,128)S(1)}, s32[1]{0:T(128)}) custom-call(f32[128,384]{1,0:T(8,128)S(1)} %bitcast.110, f32[256,256]{1,0:T(8,128)S(1)} %get-tuple-element.40.matrix_ref), custom_call_target="tpu_custom_call" | custom-call | tf_op jit(solution)/shard_map/factor/pallas_call | solution.py:205
  129.4 354.8 %conditional.1 = (f32[256,256]{1,0:T(8,128)S(1)}, f32[256,256]{1,0:T(8,128)S(1)}) conditional(s32[]{:T(128)} %bitcast.32, (bf16[256,256]{1,0:T(8,128)(2,1)S(1)}, s32[32]{0:T(128)S(1)}, bf16[3072,256]{1,0:T(8,128)(2,1)S(1)}) %tuple.87, (f32[256,256]{1,0:T(8,128)S(1)}, f32[256,256]{1,0:T(8,128)S(1)}) %tuple.23), branch_computations={%region_3.15_spmd, %region_13.16_spmd} | conditional | flops 1815717376 | bytes 44985072 | solution.py:257
  129.4 0.6 dynamic_slice.15
  130.6 2.8 convolution_select_fusion
  133.5 5.0 %all-to-all-start = ((f32[16,192,256]{2,1,0:T(8,128)}), f32[16,192,256]{2,1,0:T(8,128)}, u32[]{:S(2)}, u32[]{:S(2)}) async-start(f32[16,192,256]{2,1,0:T(8,128)} %bitcast.114), calls=%async_computation | async-start | bytes 6291456 | tf_op jit(solution)/shard_map/cond/branch_0_fun/all_to_all | solution.py:59
  138.5 71.2 %all-to-all-done = f32[16,192,256]{2,1,0:T(8,128)} async-done(((f32[16,192,256]{2,1,0:T(8,128)}), f32[16,192,256]{2,1,0:T(8,128)}, u32[]{:S(2)}, u32[]{:S(2)}) %all-to-all-start) | async-done | bytes 3145760 | tf_op jit(solution)/shard_map/cond/branch_0_fun/all_to_all | solution.py:59
  209.7 2.1 reduce_sum.56
  211.9 45.0 %all_to_all.52 = bf16[16,192,256]{2,1,0:T(8,128)(2,1)S(1)} all-to-all(bf16[16,192,256]{2,1,0:T(8,128)(2,1)S(1)} %broadcast_in_dim.25), channel_id=1, replica_groups=mesh['dp'=32,'feat'=16] {'feat'}, dimensions={0} | all-to-all | bytes 3145728 | tf_op jit(solution)/shard_map/cond/branch_0_fun/all_to_all | solution.py:54
  256.9 0.7 convolution_bitcast_fusion
  257.7 15.8 %all_to_all.57 = f32[32,8,256]{2,1,0:T(8,128)S(1)} all-to-all(f32[32,8,256]{2,1,0:T(8,128)S(1)} %convolution_bitcast_fusion), channel_id=1, replica_groups=mesh['dp'=32,'feat'=16] {'dp'}, dimensions={0} | all-to-all | bytes 524288 | tf_op jit(solution)/shard_map/cond/branch_0_fun/all_to_all | solution.py:59
  273.5 0.7 broadcast_in_dim.26
  274.2 3.9 all-to-all-start.3
  278.1 0.7 reduce_sum.58
  279.6 10.7 %all-to-all-done.3 = f32[32,8,256]{2,1,0:T(8,128)S(1)} async-done(((f32[32,8,256]{2,1,0:T(8,128)}), f32[32,8,256]{2,1,0:T(8,128)S(1)}, u32[]{:S(2)}, u32[]{:S(2)}) %all-to-all-start.3) | async-done | bytes 262176 | tf_op jit(solution)/shard_map/cond/branch_0_fun/all_to_all | solution.py:54
  290.4 0.4 fusion.15
  290.8 15.9 %all_to_all.58 = f32[16,16,256]{2,1,0:T(8,128)S(1)} all-to-all(f32[16,16,256]{2,1,0:T(8,128)S(1)} %bitcast.119), channel_id=1, replica_groups=mesh['dp'=32,'feat'=16] {'feat'}, dimensions={0} | all-to-all | bytes 524288 | tf_op jit(solution)/shard_map/cond/branch_0_fun/all_to_all | solution.py:59
  306.8 0.7 broadcast_in_dim.27
  307.5 13.5 %all-to-all-start.5 = ((f32[16,16,256]{2,1,0:T(8,128)}), f32[16,16,256]{2,1,0:T(8,128)S(1)}, u32[]{:S(2)}, u32[]{:S(2)}) async-start(f32[16,16,256]{2,1,0:T(8,128)} %broadcast_in_dim.27), calls=%async_computation.5 | async-start | bytes 524288 | tf_op jit(solution)/shard_map/cond/branch_0_fun/all_to_all | solution.py:54
  321.1 10.7 %all-to-all-done.5 = f32[16,16,256]{2,1,0:T(8,128)S(1)} async-done(((f32[16,16,256]{2,1,0:T(8,128)}), f32[16,16,256]{2,1,0:T(8,128)S(1)}, u32[]{:S(2)}, u32[]{:S(2)}) %all-to-all-start.5) | async-done | bytes 262176 | tf_op jit(solution)/shard_map/cond/branch_0_fun/all_to_all | solution.py:54
  332.0 11.7 %cholesky.130 = f32[128,128]{1,0:T(8,128)S(1)} custom-call(f32[128,128]{1,0:T(8,128)S(1)} %cholesky.194), custom_call_target="Cholesky" | custom-call | tf_op jit(solution)/shard_map/cond/branch_0_fun/jit(cholesky)/cholesky | solution.py:219
  343.7 9.8 %custom-call.13 = f32[1,128,128]{1,2,0:T(8,128)S(1)} custom-call(f32[1,128,128]{2,1,0:T(8,128)S(1)} %get-tuple-element.117), custom_call_target="InvertDiagBlocksLowerTriangular" | custom-call | tf_op jit(solution)/shard_map/cond/branch_0_fun/jit(cholesky)/cholesky | solution.py:219
  354.0 11.7 %cholesky.147 = f32[128,128]{1,0:T(8,128)S(1)} custom-call(f32[128,128]{1,0:T(8,128)S(1)} %convolution_subtract_fusion.3), custom_call_target="Cholesky" | custom-call | tf_op jit(solution)/shard_map/cond/branch_0_fun/jit(cholesky)/cholesky | solution.py:219
  365.8 0.6 compare_reduce_fusion.2
  367.7 3.8 while.4
  367.8 0.6 fusion.72
  368.4 1.3 bitcast_dynamic-update-slice_fusion.4
  369.7 0.6 fusion.72
  370.3 1.3 bitcast_dynamic-update-slice_fusion.4
  371.6 19.7 %custom-call.14 = f32[2,128,128]{1,2,0:T(8,128)S(1)} custom-call(f32[2,128,128]{2,1,0:T(8,128)S(1)} %get-tuple-element.65), custom_call_target="InvertDiagBlocksLowerTriangular" | custom-call | tf_op jit(solution)/shard_map/cond/branch_0_fun/jit(_solve_triangular)/triangular_solve | solution.py:220
  391.3 0.3 fusion.16
  391.9 0.3 fusion.28
  392.2 0.4 fusion
  392.6 14.4 %all_to_all.59 = f32[16,16,256]{2,1,0:T(8,128)S(1)} all-to-all(f32[16,16,256]{2,1,0:T(8,128)S(1)} %bitcast.120), channel_id=1, replica_groups=mesh['dp'=32,'feat'=16] {'feat'}, dimensions={0} | all-to-all | bytes 524288 | tf_op jit(solution)/shard_map/cond/branch_0_fun/all_to_all | solution.py:59
  407.1 14.4 %all_to_all.60 = f32[16,16,256]{2,1,0:T(8,128)S(1)} all-to-all(f32[16,16,256]{2,1,0:T(8,128)S(1)} %broadcast_in_dim.28), channel_id=1, replica_groups=mesh['dp'=32,'feat'=16] {'feat'}, dimensions={0} | all-to-all | bytes 524288 | tf_op jit(solution)/shard_map/cond/branch_0_fun/all_to_all | solution.py:54
  421.7 11.7 %cholesky.164 = f32[128,128]{1,0:T(8,128)S(1)} custom-call(f32[128,128]{1,0:T(8,128)S(1)} %cholesky.197), custom_call_target="Cholesky" | custom-call | tf_op jit(solution)/shard_map/cond/branch_0_fun/jit(cholesky)/cholesky | solution.py:219
  433.4 9.8 %custom-call.15 = f32[1,128,128]{1,2,0:T(8,128)S(1)} custom-call(f32[1,128,128]{2,1,0:T(8,128)S(1)} %get-tuple-element.113), custom_call_target="InvertDiagBlocksLowerTriangular" | custom-call | tf_op jit(solution)/shard_map/cond/branch_0_fun/jit(cholesky)/cholesky | solution.py:219
  443.7 11.7 %cholesky.181 = f32[128,128]{1,0:T(8,128)S(1)} custom-call(f32[128,128]{1,0:T(8,128)S(1)} %convolution_subtract_fusion.2), custom_call_target="Cholesky" | custom-call | tf_op jit(solution)/shard_map/cond/branch_0_fun/jit(cholesky)/cholesky | solution.py:219
  455.5 0.7 compare_reduce_fusion
  456.2 0.6 compare_reduce_fusion.1
  458.2 0.5 fusion.11
  458.7 4.1 while.5
  458.8 0.6 fusion.73
  459.4 1.4 bitcast_dynamic-update-slice_fusion.5
  460.8 0.6 fusion.73
  461.4 1.4 bitcast_dynamic-update-slice_fusion.5
  462.9 19.9 %custom-call.16 = f32[2,128,128]{1,2,0:T(8,128)S(1)} custom-call(f32[2,128,128]{2,1,0:T(8,128)S(1)} %get-tuple-element.66), custom_call_target="InvertDiagBlocksLowerTriangular" | custom-call | tf_op jit(solution)/shard_map/cond/branch_0_fun/jit(_solve_triangular)/triangular_solve | solution.py:220
  483.4 0.3 fusion.23
  484.2 0.7 copy-done.3
  (63 shorter events, 4.0 us)
Async XLA Ops:
  2.6 9.1 %copy-start.2 = (s32[32]{0:T(128)S(1)}, s32[32]{0:T(128)}, u32[]{:S(2)}) copy-start(s32[32]{0:T(128)} %counts_ref.1) | copy-start | bytes 388
  2.9 10.7 %collective-permute-start = (f16[1536,256]{1,0:T(8,128)(2,1)S(1)}, f16[1536,256]{1,0:T(8,128)(2,1)S(1)}, u32[]{:S(2)}, u32[]{:S(2)}) collective-permute-start(f16[1536,256]{1,0:T(8,128)(2,1)S(1)} %get-tuple-element.124), channel_id=1, source_target_pairs={{0,1},{1,0},{2,3},{3,2},{4,5},{5,4},{6,7},{7,6},{8,9},{9,8},{10,11... | collective-permute-start | bytes 2359304 | tf_op jit(solution)/shard_map/ppermute | solution.py:34
  13.9 40.5 %copy-start = (bf16[3072,256]{1,0:T(8,128)(2,1)S(1)}, bf16[3072,256]{1,0:T(8,128)(2,1)}, u32[]{:S(2)}) copy-start(bf16[3072,256]{1,0:T(8,128)(2,1)} %param.8) | copy-start | bytes 4718596
  45.2 11.1 %collective-permute-start.1 = (f16[1536,256]{1,0:T(8,128)(2,1)S(1)}, f16[1536,256]{1,0:T(8,128)(2,1)S(1)}, u32[]{:S(2)}, u32[]{:S(2)}) collective-permute-start(f16[1536,256]{1,0:T(8,128)(2,1)S(1)} %bitcast.121), channel_id=1, source_target_pairs={{0,1},{1,0},{2,3},{3,2},{4,5},{5,4},{6,7},{7,6},{8,9},{9,8},{10,11... | collective-permute-start | bytes 2359304 | tf_op jit(solution)/shard_map/ppermute | solution.py:34
  54.8 33.8 %copy-start.1 = (bf16[256,256]{1,0:T(8,128)(2,1)S(1)}, bf16[256,256]{1,0:T(8,128)(2,1)}, u32[]{:S(2)}) copy-start(bf16[256,256]{1,0:T(8,128)(2,1)} %basis_ref.1) | copy-start | bytes 393220
  89.7 5.6 %collective-permute-start.2 = (f32[8,384]{1,0:T(8,128)S(1)}, f32[8,384]{1,0:T(8,128)S(1)}, u32[]{:S(2)}, u32[]{:S(2)}) collective-permute-start(f32[8,384]{1,0:T(8,128)S(1)} %get-tuple-element.38), channel_id=1, source_target_pairs={{0,1},{1,0},{2,3},{3,2},{4,5},{5,4},{6,7},{7,6},{8,9},{9,8},{10,11... | collective-permute-start | bytes 36872 | tf_op jit(solution)/shard_map/ppermute | solution.py:34
  133.5 76.2 %all-to-all-start = ((f32[16,192,256]{2,1,0:T(8,128)}), f32[16,192,256]{2,1,0:T(8,128)}, u32[]{:S(2)}, u32[]{:S(2)}) async-start(f32[16,192,256]{2,1,0:T(8,128)} %bitcast.114), calls=%async_computation | async-start | bytes 6291456 | tf_op jit(solution)/shard_map/cond/branch_0_fun/all_to_all | solution.py:59
  274.2 16.1 %all-to-all-start.3 = ((f32[32,8,256]{2,1,0:T(8,128)}), f32[32,8,256]{2,1,0:T(8,128)S(1)}, u32[]{:S(2)}, u32[]{:S(2)}) async-start(f32[32,8,256]{2,1,0:T(8,128)} %broadcast_in_dim.26), calls=%async_computation.3 | async-start | bytes 524288 | tf_op jit(solution)/shard_map/cond/branch_0_fun/all_to_all | solution.py:54
  307.5 24.2 %all-to-all-start.5 = ((f32[16,16,256]{2,1,0:T(8,128)}), f32[16,16,256]{2,1,0:T(8,128)S(1)}, u32[]{:S(2)}, u32[]{:S(2)}) async-start(f32[16,16,256]{2,1,0:T(8,128)} %broadcast_in_dim.27), calls=%async_computation.5 | async-start | bytes 524288 | tf_op jit(solution)/shard_map/cond/branch_0_fun/all_to_all | solution.py:54
  484.2 0.7 copy-start.3
  484.2 0.8 copy-start.4
